TPU v7x, 128 devices: a whole 4x4x4 slice. The times are simulated.
128 devices in a mesh: blk: 8 (over z_hi, x), grp: 16 (over z_lo, y, core).
Axes of the slice: x: 4, y: 4, z: 4 (z_hi: 2, z_lo: 2; z = z_hi * 2 + z_lo), core: 2. Of those that a mesh axis runs over, the one named last changes fastest.
Arguments:
- image_teacher: bfloat16 [16384, 1024], P('blk'), may hold values from -6 to 6
- text_teacher: bfloat16 [16384, 1024], P(('blk', 'grp')), may hold values from -6 to 6
- image_student: bfloat16 [16384, 512], P('blk'), may hold values from -6 to 6
- text_student: bfloat16 [16384, 512], P(('blk', 'grp')), may hold values from -6 to 6
Outputs:
- row_loss: float32 [16384], P('blk')
- grad_image: bfloat16 [16384, 512], P(('blk', 'grp'))
- grad_text: bfloat16 [16384, 512], P(('blk', 'grp'))
All inputs are finite; a program needn't handle non-finite values.
Results may differ from a plain program's by a relative error of at most 0.022.
Values may be sent and summed in bfloat16 or wider, within the bound.
No kernel may reach another device: no remote copies, remote signals or barrier semaphores. Data moves between devices by JAX's collectives and lax.ppermute only.
A program may use at most 128 MiB of HBM per device.

v0:
```python
import math

import jax
import jax.numpy as jnp
from jax import lax
from jax.sharding import PartitionSpec as P


def shards(image_teacher, text_teacher, image_student, text_student):
    width_t = image_teacher.shape[1]
    width_s = image_student.shape[1]
    teacher_scale = 3.0 / math.sqrt(width_t)
    student_scale = 3.0 / math.sqrt(width_s)
    joined = jnp.concatenate((text_teacher, text_student), axis=1)
    gathered = lax.all_gather(joined, "blk", axis=0, tiled=True)
    teacher_part = (
        jnp.einsum(
            "rd,cd->rc", image_teacher, gathered[:, :width_t], preferred_element_type=jnp.float32
        )
        * teacher_scale
    )
    student_part = (
        jnp.einsum(
            "rd,cd->rc", image_student, gathered[:, width_t:], preferred_element_type=jnp.float32
        )
        * student_scale
    )
    gap = teacher_part - student_part
    local_t = jnp.max(teacher_part, axis=1)
    local_s = jnp.max(student_part, axis=1)
    top_t, top_s = lax.pmax((local_t, local_s), "grp")
    exp_t = jnp.exp(teacher_part - top_t[:, None])
    exp_s = jnp.exp(student_part - top_s[:, None])
    sum_t, sum_s, weighted = lax.psum(
        (jnp.sum(exp_t, axis=1), jnp.sum(exp_s, axis=1), jnp.sum(exp_t * gap, axis=1)), "grp"
    )
    lse_t = top_t + jnp.log(sum_t)
    lse_s = top_s + jnp.log(sum_s)
    row_loss = weighted / sum_t - lse_t + lse_s
    prob_t = jnp.exp(teacher_part - lse_t[:, None])
    prob_s = jnp.exp(student_part - lse_s[:, None])
    delta = ((prob_s - prob_t) * student_scale).astype(jnp.bfloat16)
    image_term = jnp.dot(delta, gathered[:, width_t:], preferred_element_type=jnp.float32)
    grad_image = lax.psum_scatter(
        image_term.astype(jnp.bfloat16), "grp", scatter_dimension=0, tiled=True
    )
    grad_text = lax.psum_scatter(
        jnp.einsum("rc,rd->cd", delta, image_student, preferred_element_type=jnp.float32).astype(
            jnp.bfloat16
        ),
        "blk",
        scatter_dimension=0,
        tiled=True,
    )
    return (row_loss, grad_image, grad_text)


def solution(mesh):
    in_specs = (P("blk", None), P(("blk", "grp"), None), P("blk", None), P(("blk", "grp"), None))
    out_specs = (P("blk"), P(("blk", "grp"), None), P(("blk", "grp"), None))
    return jax.shard_map(shards, mesh=mesh, in_specs=in_specs, out_specs=out_specs, check_vma=False)
```

profile of v0, /device:TPU:0, one launch (start us, length us, event | category | flops | bytes accessed | tf_op | source)
XLA Modules:
  0.0 363.1 jit_solution(15251234702049372633)
XLA Ops:
  7.2 0.0 copy-start
  7.2 0.0 all-gather.2.cloned.1.call-start
  7.2 1.9 pad_maximum_fusion
  9.1 0.0 all-gather.2.cloned.1.call-update
  9.2 0.0 reduce-scatter.5.cloned.1.call-start
  9.2 66.7 %all-gather.2.cloned.1.call-done = bf16[1024,1536]{1,0:T(8,128)(2,1)} async-done(((bf16[128,1536]{1,0:T(8,128)(2,1)}), bf16[1024,1536]{1,0:T(8,128)(2,1)}) %all-gather.2.cloned.1.call-update) | async-done | bytes 3145744 | tf_op jit(solution)/shard_map/all_gather | solution.py:15
  75.9 10.6 %multiply_reduce_fusion.2 = (f32[2048]{0:T(1024)S(1)}, f32[1024,2048]{1,0:T(8,128)}) fusion(bf16[2048,1024]{1,0:T(8,128)(2,1)} %param.4, bf16[1024,1536]{1,0:T(8,128)(2,1)} %all-gather.2.cloned.1.call-done), kind=kOutput, calls=%fused_computation.6 | convolution fusion | flops 4299159552 | bytes 14688256 | tf_op jit(solution)/shard_map/rd,cd->rc/dot_general | solution.py:17
  86.5 29.5 %pmax.14 = f32[2048]{0:T(1024)S(1)} all-reduce(f32[2048]{0:T(1024)S(1)} %get-tuple-element.12), channel_id=1, replica_groups=mesh['blk'=8,'grp'=16] {'grp'}, use_global_device_ids=true, to_apply=%region_1.0 | all-reduce | flops 2048 | bytes 16384 | tf_op jit(solution)/shard_map/pmax | solution.py:31
  116.0 0.0 copy-done
  116.0 8.2 %multiply_reduce_fusion = (f32[2048]{0:T(1024)S(1)}, f32[2048]{0:T(1024)S(1)}, f32[2048]{0:T(1024)S(1)}, f32[1024,2048]{1,0:T(8,128)}) fusion(f32[1024,2048]{1,0:T(8,128)} %get-tuple-element.13, f32[2048]{0:T(1024)S(1)} %pmax.14, bf16[2048,512]{1,0:T(8,128)(2,1)S(1)} %copy-done, bf16[1024,1536]{1,0:T(8,128)(2,1)} %all-gather.2.cloned.1.call-done), kind=kOutput, calls=%fused_computation.2 | convolution fusion | flops 2164254720 | bytes 19955712 | tf_op jit(solution)/shard_map/rd,cd->rc/dot_general | solution.py:23
  124.2 27.6 %pmax.15 = f32[2048]{0:T(1024)S(1)} all-reduce(f32[2048]{0:T(1024)S(1)} %get-tuple-element.5), channel_id=1, replica_groups=mesh['blk'=8,'grp'=16] {'grp'}, use_global_device_ids=true, to_apply=%region_7.0 | all-reduce | flops 2048 | bytes 16384 | tf_op jit(solution)/shard_map/pmax | solution.py:31
  151.9 4.8 %exponential_reduce_fusion = f32[2048]{0:T(1024)S(1)} fusion(f32[1024,2048]{1,0:T(8,128)} %get-tuple-element.14, f32[2048]{0:T(1024)S(1)} %pmax.15), kind=kLoop, calls=%fused_computation.1 | loop fusion | flops 6289408 | bytes 8404992 | tf_op jit(solution)/shard_map/reduce_sum | solution.py:35
  156.6 52.9 %all-reduce = (f32[2048]{0:T(1024)S(1)}, f32[2048]{0:T(1024)S(1)}, f32[2048]{0:T(1024)S(1)}) all-reduce(f32[2048]{0:T(1024)S(1)} %exponential_reduce_fusion, f32[2048]{0:T(1024)S(1)} %get-tuple-element.4, f32[2048]{0:T(1024)S(1)} %get-tuple-element.3), channel_id=1, replica_groups=mesh['blk'=8,'grp'=16] {'grp'}, use_global_device_ids=true, to_apply=%region_9.0 | all-reduce | flops 6144 | bytes 49152 | tf_op jit(solution)/shard_map/psum | solution.py:34
  209.6 0.6 subtract_add_fusion
  210.2 7.3 %multiply_convert_fusion = bf16[1024,2048]{1,0:T(8,128)(2,1)S(1)} fusion(f32[1024,2048]{1,0:T(8,128)} %get-tuple-element.14, f32[1024,2048]{1,0:T(8,128)} %get-tuple-element.13, f32[2048]{0:T(1024)S(1)} %get-tuple-element.10, f32[2048]{0:T(1024)S(1)} %get-tuple-element.11), kind=kLoop, calls=%fused_computation | loop fusion | flops 14680064 | bytes 20987904 | tf_op jit(solution)/shard_map/convert_element_type | solution.py:42
  217.5 0.0 copy-start.1
  217.5 1.9 copy-done.1
  219.4 3.3 convolution_convert_fusion.1
  222.8 0.0 reduce-scatter.5.cloned.1.call-update
  222.8 0.0 reduce-scatter.3.cloned.1.call-start
  222.8 6.2 %convolution_convert_fusion = bf16[2048,512]{1,0:T(8,128)(2,1)} fusion(bf16[1024,2048]{1,0:T(8,128)(2,1)} %copy-done.1, bf16[1024,1536]{1,0:T(8,128)(2,1)} %all-gather.2.cloned.1.call-done), kind=kOutput, calls=%fused_computation.7 | convolution fusion | flops 2148532224 | bytes 7340032 | tf_op jit(solution)/shard_map/dot_general | solution.py:43
  229.0 0.0 reduce-scatter.3.cloned.1.call-update
  229.1 62.0 %reduce-scatter.5.cloned.1.call-done = bf16[128,512]{1,0:T(8,128)(2,1)} async-done(((bf16[1024,512]{1,0:T(8,128)(2,1)}), bf16[128,512]{1,0:T(8,128)(2,1)}) %reduce-scatter.5.cloned.1.call-update) | async-done | bytes 131088 | tf_op jit(solution)/shard_map/reduce_scatter | solution.py:47
  291.1 65.5 %reduce-scatter.3.cloned.1.call-done = bf16[128,512]{1,0:T(8,128)(2,1)} async-done(((bf16[2048,512]{1,0:T(8,128)(2,1)}), bf16[128,512]{1,0:T(8,128)(2,1)}) %reduce-scatter.3.cloned.1.call-update) | async-done | bytes 131088 | tf_op jit(solution)/shard_map/reduce_scatter | solution.py:44
Async XLA Ops:
  7.2 108.8 %copy-start = (bf16[2048,512]{1,0:T(8,128)(2,1)S(1)}, bf16[2048,512]{1,0:T(8,128)(2,1)}, u32[]{:S(2)}) copy-start(bf16[2048,512]{1,0:T(8,128)(2,1)} %param.6) | copy-start | bytes 6291460
  7.2 68.7 %all-gather.2.cloned.1.call-start = ((), (), s32[]{:S(2)}) async-start(), calls=%async_computation.2 | async-start | bytes 3538944 | tf_op jit(solution)/shard_map/all_gather | solution.py:15
  9.2 281.9 %reduce-scatter.5.cloned.1.call-start = ((), (), s32[]{:S(2)}) async-start(), calls=%async_computation.4 | async-start | bytes 1179648 | tf_op jit(solution)/shard_map/reduce_scatter | solution.py:47
  217.5 1.9 copy-start.1
  222.8 133.8 %reduce-scatter.3.cloned.1.call-start = ((), (), s32[]{:S(2)}) async-start(), calls=%async_computation.3 | async-start | bytes 2228224 | tf_op jit(solution)/shard_map/reduce_scatter | solution.py:44
Sparse Core Ops, SparseCore 0:
  10.3 65.5 all-gather.1
  222.9 68.1 reduce-scatter.4
  294.1 62.4 reduce-scatter.2
where the time goes:
time: 363 us
  waiting for transfers between devices  194 us (53%)
  blocking collectives  110 us (30%)
  matrix products  28.3 us (8%)
  other arithmetic  14.6 us (4%)
  between operations  13.8 us (4%)
    all_gather x1, waiting for transfers between devices, shards(): gathered = lax.all_gather(joined, 'blk', axis=0, tiled=True)  66.7 us
    reduce_scatter x1, waiting for transfers between devices, shards(): lax.psum_scatter(image_term.astype(jnp.bfloat16), 'grp', scatter_dimensio...  65.5 us
    reduce_scatter x1, waiting for transfers between devices, shards(): lax.psum_scatter(jnp.einsum('rc,rd->cd', delta, image_student, preferred_...  62 us
    pmax x2, blocking collectives, shards(): top_t, top_s = lax.pmax((local_t, local_s), 'grp')  57.1 us
    psum x1, blocking collectives, shards(): lax.psum((jnp.sum(exp_t, axis=1), jnp.sum(exp_s, axis=1), jnp.sum(exp_t *...  52.9 us
    dot_general x1, matrix products, shards(): jnp.einsum('rd,cd->rc', image_teacher, gathered[:, :width_t], preferred_e...  10.6 us
    dot_general x1, matrix products, shards(): jnp.einsum('rd,cd->rc', image_student, gathered[:, width_t:], preferred_e...  8.2 us
    convert_element_type x1, other arithmetic, shards(): delta = ((prob_s - prob_t) * student_scale).astype(jnp.bfloat16)  7.33 us
  transfers between devices with their start and end apart: 3, of which 3 were waited for; matrix products, arithmetic and copies ran while one was open for 2% of the time, Pallas kernels for 0%

commit v1 on v0

v1 whole, which is shorter than its diff:
```python
import functools
import math

import jax
import jax.numpy as jnp
from jax import lax
from jax.experimental import pallas as pl
from jax.experimental.pallas import tpu as pltpu
from jax.sharding import PartitionSpec as P

AXES = ("blk", "grp")
LOG2E = 1.0 / math.log(2.0)
LN2 = math.log(2.0)
VMEM_LIMIT = 32 * 1024 * 1024
F32 = jnp.float32
BF16 = jnp.bfloat16


def place(i):
    b, g = divmod(i, 16)
    zh, x = divmod(b, 4)
    zl, r = divmod(g, 8)
    y, c = divmod(r, 2)
    return zh, x, zl, y, c


def index(zh, x, zl, y, c):
    return (zh * 4 + x) * 16 + (zl * 4 + y) * 2 + c


def permute(v, move):
    return lax.ppermute(v, AXES, [(i, index(*move(*place(i)))) for i in range(128)])


def along_x(k):
    return lambda zh, x, zl, y, c: (zh, (x + k) % 4, zl, y, c)


def along_y(k, flip=0):
    return lambda zh, x, zl, y, c: (zh, x, zl ^ flip, (y + k) % 4, c)


def other_core(zh, x, zl, y, c):
    return (zh, x, zl, y, 1 - c)


def cross_z(zh, x, zl, y, c):
    return (1 - zh, x, 1 - zl, y, c)


NT = (((1,), (1,)), ((), ()))


def logits_kernel(n_text, first, last, scale_t, scale_s, *refs):
    texts = refs[:n_text]
    image_t, image_s = refs[n_text], refs[n_text + 1]
    k = n_text + 2
    before = None
    if not first:
        before = refs[k]
        k += 1
    out_t, out_s, stats = refs[k], refs[k + 1], refs[k + 2]
    width_t = image_t.shape[-1]
    rows_t = image_t[...].reshape(-1, width_t)
    rows_s = image_s[...].reshape(-1, image_s.shape[-1])
    row = 0
    for ref in texts:
        n = ref.shape[0]
        out_t[row : row + n, :] = (
            lax.dot_general(ref[:, :width_t], rows_t, NT, preferred_element_type=F32)
            * scale_t
        )
        out_s[row : row + n, :] = (
            lax.dot_general(ref[:, width_t:], rows_s, NT, preferred_element_type=F32)
            * scale_s
        )
        row += n
    t = out_t[...]
    s = out_s[...]
    top_t = jnp.max(t, axis=0, keepdims=True)
    top_s = jnp.max(s, axis=0, keepdims=True)
    if not first:
        old_t, old_s = before[0:1, :], before[2:3, :]
        top_t = jnp.maximum(top_t, old_t)
        top_s = jnp.maximum(top_s, old_s)
    exp_t = jnp.exp2(t - top_t)
    exp_s = jnp.exp2(s - top_s)
    sum_t = jnp.sum(exp_t, axis=0, keepdims=True)
    sum_s = jnp.sum(exp_s, axis=0, keepdims=True)
    gap = jnp.sum(exp_t * (t - s), axis=0, keepdims=True)
    if not first:
        shrink = jnp.exp2(old_t - top_t)
        sum_t += before[1:2, :] * shrink
        gap += before[4:5, :] * shrink
        sum_s += before[3:4, :] * jnp.exp2(old_s - top_s)
    if last:
        stats[0:1, :] = top_t + jnp.log2(sum_t)
        stats[1:2, :] = top_s + jnp.log2(sum_s)
        stats[2:3, :] = gap / sum_t
        stats[3:4, :] = jnp.zeros_like(gap)
    else:
        stats[0:1, :] = top_t
        stats[1:2, :] = sum_t
        stats[2:3, :] = top_s
        stats[3:4, :] = sum_s
        stats[4:5, :] = gap
        stats[5:8, :] = jnp.zeros((3, gap.shape[1]), F32)


def logits(texts, image_t, image_s, before, last, tile=4):
    blocks, cores, block = image_t.shape[:3]
    rows = blocks * cores * block
    width_t, width_s = image_t.shape[3], image_s.shape[3]
    n = sum(t.shape[0] for t in texts)
    first = before is None
    full = lambda c, j: (0, 0)
    image = lambda c, j: (j, c, 0, 0)
    column = lambda c, j: (0, c * (blocks // tile) + j)
    in_specs = [pl.BlockSpec(t.shape, full) for t in texts]
    in_specs += [
        pl.BlockSpec((tile, None, block, width_t), image),
        pl.BlockSpec((tile, None, block, width_s), image),
    ]
    args = list(texts) + [image_t, image_s]
    if not first:
        in_specs.append(pl.BlockSpec((8, tile * block), column))
        args.append(before)
    depth = 4 if last else 8
    return pl.pallas_call(
        functools.partial(
            logits_kernel,
            len(texts),
            first,
            last,
            3.0 / math.sqrt(width_t) * LOG2E,
            3.0 / math.sqrt(width_s) * LOG2E,
        ),
        grid=(cores, blocks // tile),
        in_specs=in_specs,
        out_specs=[
            pl.BlockSpec((n, tile * block), column),
            pl.BlockSpec((n, tile * block), column),
            pl.BlockSpec((depth, tile * block), column),
        ],
        out_shape=[
            jax.ShapeDtypeStruct((n, rows), F32),
            jax.ShapeDtypeStruct((n, rows), F32),
            jax.ShapeDtypeStruct((depth, rows), F32),
        ],
        compiler_params=pltpu.CompilerParams(vmem_limit_bytes=VMEM_LIMIT),
        cost_estimate=pl.CostEstimate(
            flops=2 * n * rows * (width_t + width_s),
            bytes_accessed=rows * (width_t + width_s) * 2 + 8 * n * rows,
            transcendentals=2 * n * rows,
        ),
    )(*args)


def merge(parts):
    def total(v):
        if len(v) == 4:
            return (v[0] + v[2]) + (v[1] + v[3])
        return v[0] + v[1]

    lse_t, lse_s, gap = ([p[k] for p in parts] for k in range(3))
    top_t, top_s = functools.reduce(jnp.maximum, lse_t), functools.reduce(jnp.maximum, lse_s)
    part_t = [jnp.exp2(v - top_t) for v in lse_t]
    sum_t = total(part_t)
    mean = total([p * g for p, g in zip(part_t, gap)]) / sum_t
    new_s = top_s + jnp.log2(total([jnp.exp2(v - top_s) for v in lse_s]))
    return jnp.stack([top_t + jnp.log2(sum_t), new_s, mean, jnp.zeros_like(mean)])


ORDER = ((0, 0), (1, 0), (1, 1), (2, 1), (1, 2), (2, 2), (2, 0), (3, 0))


def delta_kernel(n_group, n_text, scale, which, *refs):
    logit_t, logit_s = refs[:n_group], refs[n_group : 2 * n_group]
    texts = refs[2 * n_group : 2 * n_group + n_text]
    stats, grad, delta, turned = refs[2 * n_group + n_text :]
    n = texts[0].shape[0]

    @pl.when(pl.program_id(0) == 0)
    def _():
        for k, ref in enumerate(texts):
            turned[:, n * k : n * k + n] = ref[...].T

    lse_t, lse_s = stats[0:1, :], stats[1:2, :]
    for k, (group, at) in enumerate(ORDER):
        prob_t = jnp.exp2(logit_t[group][n * at : n * at + n, :] - lse_t)
        prob_s = jnp.exp2(logit_s[group][n * at : n * at + n, :] - lse_s)
        delta[n * k : n * k + n, :] = ((prob_s - prob_t) * scale).astype(BF16)
    out = jnp.dot(turned[...], delta[...], preferred_element_type=F32).astype(BF16)
    for k in range(grad.shape[0]):
        grad[k, :, :] = out[:, 128 * k : 128 * k + 128]


def delta_part(half, groups_t, groups_s, texts, stats, width_s, tile=256):
    rows = stats.shape[1]
    count = sum(t.shape[0] for t in texts)
    steps = rows // 2 // tile
    column = lambda i, w: (0, w[0] * steps + i)
    in_specs = [pl.BlockSpec((t.shape[0], tile), column) for t in groups_t + groups_s]
    in_specs += [pl.BlockSpec((t.shape[0], width_s), lambda i, w: (0, 2)) for t in texts]
    in_specs.append(pl.BlockSpec((4, tile), column))
    return pl.pallas_call(
        functools.partial(delta_kernel, len(groups_t), len(texts), 3.0 / math.sqrt(width_s)),
        grid_spec=pltpu.PrefetchScalarGridSpec(
            num_scalar_prefetch=1,
            grid=(steps,),
            in_specs=in_specs,
            out_specs=[
                pl.BlockSpec((tile // 128, width_s, 128), lambda i, w: (i, 0, 0)),
                pl.BlockSpec((count, tile), lambda i, w: (0, i)),
            ],
            scratch_shapes=[pltpu.VMEM((width_s, count), BF16)],
        ),
        out_shape=[
            jax.ShapeDtypeStruct((rows // 256, width_s, 128), BF16),
            jax.ShapeDtypeStruct((count, rows // 2), BF16),
        ],
        compiler_params=pltpu.CompilerParams(vmem_limit_bytes=VMEM_LIMIT),
        cost_estimate=pl.CostEstimate(
            flops=count * rows * width_s,
            bytes_accessed=6 * count * rows,
            transcendentals=count * rows,
        ),
    )(half, *groups_t, *groups_s, *texts, stats)


def text_kernel(half, mine, other, image_mine, image_other, out):
    rows, width = mine.shape[1], out.shape[1]
    out[...] = (
        jnp.dot(mine[...], image_mine[...].reshape(rows, width), preferred_element_type=F32)
        + jnp.dot(other[...], image_other[...].reshape(rows, width), preferred_element_type=F32)
    ).astype(BF16)


def text_part(half, mine, other, image_s, part):
    blocks, _, block, width = image_s.shape
    count, rows = mine.shape
    tile = count // 4
    image = (blocks, None, block, width)
    return pl.pallas_call(
        text_kernel,
        grid_spec=pltpu.PrefetchScalarGridSpec(
            num_scalar_prefetch=1,
            grid=(1,),
            in_specs=[
                pl.BlockSpec((tile, rows), lambda i, w: (part, 0)),
                pl.BlockSpec((tile, rows), lambda i, w: (part, 0)),
                pl.BlockSpec(image, lambda i, w: (0, w[0], 0, 0)),
                pl.BlockSpec(image, lambda i, w: (0, 1 - w[0], 0, 0)),
            ],
            out_specs=pl.BlockSpec((tile, width), lambda i, w: (0, 0)),
        ),
        out_shape=jax.ShapeDtypeStruct((tile, width), BF16),
        compiler_params=pltpu.CompilerParams(vmem_limit_bytes=VMEM_LIMIT),
        cost_estimate=pl.CostEstimate(
            flops=4 * tile * rows * width,
            bytes_accessed=4 * tile * rows + 4 * rows * width,
            transcendentals=0,
        ),
    )(half, mine, other, image_s, image_s)


def pair_kernel(order, mine, other, *outs):
    for k, out in enumerate(outs):
        total = mine[order[k]].astype(F32) + other[order[k]].astype(F32)
        out[...] = total.astype(out.dtype)


def pair_sum(order, mine, other):
    blocks, width, block = mine.shape
    whole = lambda i, w: (0, 0, 0)
    return pl.pallas_call(
        pair_kernel,
        grid_spec=pltpu.PrefetchScalarGridSpec(
            num_scalar_prefetch=1,
            grid=(1,),
            in_specs=[pl.BlockSpec(mine.shape, whole)] * 2,
            out_specs=[pl.BlockSpec((width, block), lambda i, w: (0, 0))] * blocks,
        ),
        out_shape=[
            jax.ShapeDtypeStruct((width, block), F32 if k == 0 else BF16) for k in range(blocks)
        ],
        compiler_params=pltpu.CompilerParams(vmem_limit_bytes=VMEM_LIMIT),
        cost_estimate=pl.CostEstimate(
            flops=blocks * width * block, bytes_accessed=6 * blocks * width * block, transcendentals=0
        ),
    )(order, mine, other)


def total(parts):
    return functools.reduce(jnp.add, [p.astype(F32) for p in parts])


def shards(image_t, text_t, image_s, text_s):
    width_s = image_s.shape[1]
    n = text_t.shape[0]
    image_t = image_t.reshape(8, 2, 128, image_t.shape[1])
    image_s = image_s.reshape(8, 2, 128, width_s)
    own = jnp.concatenate((text_t, text_s), axis=1)

    across = permute(own, cross_z)
    left = permute(own, along_x(1))
    right = permute(own, along_x(3))
    t0, s0, stats = logits([own], image_t, image_s, None, False)
    far = jnp.concatenate(
        (permute(left[: n // 2], along_x(1)), permute(right[n // 2 :], along_x(3))), axis=0
    )
    across_left = permute(across, along_x(1))
    across_right = permute(across, along_x(3))
    t1, s1, stats = logits([across, left, right], image_t, image_s, stats, False)
    across_far = permute(far, cross_z)
    t2, s2, stats = logits([far, across_left, across_right], image_t, image_s, stats, False)
    t3, s3, stats = logits([across_far], image_t, image_s, stats, True)

    stats = merge([stats, permute(stats, other_core)])
    stats = merge([stats, permute(stats, along_y(0, 1))])
    stats = merge([stats] + [permute(stats, along_y(k)) for k in (1, 2, 3)])
    row_loss = (stats[2] - stats[0] + stats[1]) * LN2
    row_loss = row_loss.reshape(2, 8, 128).transpose(1, 0, 2).reshape(-1)

    spot = lax.axis_index("grp")
    core, y, z_lo = lax.rem(spot, 2), lax.rem(spot // 2, 4), spot // 8
    mine = jnp.reshape(core, (1,)).astype(jnp.int32)
    moves = [(0, 0)] + [(2, 1), (2, 0), (1, 1), (3, 1), (1, 0), (3, 0), (0, 1)]
    order = jnp.stack(
        [jnp.bitwise_xor(z_lo, flip) * 4 + lax.rem(y + k, 4) for k, flip in moves]
    ).astype(jnp.int32)
    groups_t, groups_s = (t0, t1, t2, t3), (s0, s1, s2, s3)
    texts = [own, across, left, across_left, right, across_right, far, across_far]
    grad_other, delta_other = delta_part(1 - mine, groups_t, groups_s, texts, stats, width_s)
    received = permute(grad_other, other_core)
    grad_mine, delta_mine = delta_part(mine, groups_t, groups_s, texts, stats, width_s)
    image_terms = pair_sum(order, grad_mine, received)
    image_terms = list(image_terms[:1]) + [
        permute(v, along_y(k, flip)) for v, (k, flip) in zip(image_terms[1:], moves[1:])
    ]
    grad_image = total(image_terms).T.astype(BF16)

    part = lambda k: text_part(mine, delta_mine, delta_other, image_s, k)
    text_terms = [
        permute(part(3), along_x(2)),
        permute(part(1), along_x(3)),
        permute(part(2), along_x(1)),
        part(0),
    ]
    text_sum = total(text_terms)
    from_across = permute(text_sum[n:].astype(BF16), cross_z)
    grad_text = (text_sum[:n] + from_across.astype(F32)).astype(BF16)
    return row_loss, grad_image, grad_text


def solution(mesh):
    in_specs = (P("blk", None), P(AXES, None), P("blk", None), P(AXES, None))
    out_specs = (P("blk"), P(AXES, None), P(AXES, None))
    return jax.shard_map(shards, mesh=mesh, in_specs=in_specs, out_specs=out_specs, check_vma=False)
```

time: 363 us -> 145 us (0.40)
  waiting for transfers between devices: 194 us -> 29.1 us
  blocking collectives: 110 us -> 0 us
  Pallas kernels: 0 us -> 38 us
  starting transfers between devices: 0.12 us -> 37.5 us
  local copies, waits for them, and re-layouts: 1.93 us -> 33.1 us
  matrix products: 28.3 us -> 0 us
  between operations: 13.8 us -> 1.09 us
  other arithmetic: 14.6 us -> 4.36 us
    reduce_scatter x2 -> x0, waiting for transfers between devices: 128 us -> none  [the longest x1 65.5 us: shards(): lax.psum_scatter(image_term.astype(jnp.bfloat16), 'grp', scatter_dimensio...]
    all_gather x1 -> x0, waiting for transfers between devices: 66.7 us -> none  [shards(): gathered = lax.all_gather(joined, 'blk', axis=0, tiled=True)]
    pmax x2 -> x0, blocking collectives: 57.1 us -> none  [shards(): top_t, top_s = lax.pmax((local_t, local_s), 'grp')]
    psum x1 -> x0, blocking collectives: 52.9 us -> none  [shards(): lax.psum((jnp.sum(exp_t, axis=1), jnp.sum(exp_s, axis=1), jnp.sum(exp_t *...]
    pallas_call x0 -> x11, Pallas kernels: none -> 38 us  [the longest x4 24.5 us: logits(): pl.pallas_call(functools.partial(logits_kernel, len(texts), first, last,...]
    ppermute x0 -> x25, starting transfers between devices: none -> 37.5 us  [permute(): lax.ppermute(v, AXES, [(i, index(*move(*place(i)))) for i in range(128)])]
    ppermute x0 -> x25, waiting for transfers between devices: none -> 29.1 us  [permute(): lax.ppermute(v, AXES, [(i, index(*move(*place(i)))) for i in range(128)])]
    dot_general x4 -> x0, matrix products: 28.3 us -> none  [the longest x1 10.6 us: shards(): jnp.einsum('rd,cd->rc', image_teacher, gathered[:, :width_t], preferred_e...]
  transfers between devices with their start and end apart: 3 -> 25, of which waited for: 3 -> 13; matrix products, arithmetic and copies ran while one was open for 2% -> 2% of each run, Pallas kernels for 0% -> 15%
where the time goes in v1:
time: 145 us; the launch traced here: 143 us
  Pallas kernels  38 us (26%)
  starting transfers between devices  37.5 us (26%)
  local copies, waits for them, and re-layouts  33.1 us (23%)
  waiting for transfers between devices  29.1 us (20%)
  other arithmetic  4.36 us (3%)
    ppermute x25, starting transfers between devices, permute(): lax.ppermute(v, AXES, [(i, index(*move(*place(i)))) for i in range(128)])  37.5 us
    unnamed x89, local copies, waits for them, and re-layouts  29.6 us
    ppermute x25, waiting for transfers between devices, permute(): lax.ppermute(v, AXES, [(i, index(*move(*place(i)))) for i in range(128)])  29.1 us
    pallas_call x4, Pallas kernels, logits(): pl.pallas_call(functools.partial(logits_kernel, len(texts), first, last,...  24.5 us
    pallas_call x2, Pallas kernels, delta_part(): pl.pallas_call(functools.partial(delta_kernel, len(groups_t), len(texts),...  9.94 us
  transfers between devices with their start and end apart: 25, of which 13 were waited for; matrix products, arithmetic and copies ran while one was open for 2% of the time, Pallas kernels for 15%

profile of v1, /device:TPU:0, one launch (start us, length us, event | category | flops | bytes accessed | tf_op | source)
XLA Modules:
  0.0 143.2 jit_solution(6103300246904663667)
XLA Ops:
  2.5 1.6 %collective-permute-start = (bf16[128,1536]{1,0:T(8,128)(2,1)S(1)}, bf16[128,1536]{1,0:T(8,128)(2,1)S(1)}, u32[]{:S(2)}, u32[]{:S(2)}) collective-permute-start(bf16[128,1536]{1,0:T(8,128)(2,1)S(1)} %constant_dynamic-update-slice_fusion.refs_0_.refs_8_), channel_id=1, source_target_pairs={{0,16},{1,17},{2,18},{3,19},{4,20},{5,21},{6,22},{7,23},{8,24},{9,... | collective-permute-start | bytes 1179656 | tf_op jit(solution)/shard_map/ppermute | solution.py:32
  4.2 1.7 %collective-permute-start.2 = (bf16[128,1536]{1,0:T(8,128)(2,1)S(1)}, bf16[128,1536]{1,0:T(8,128)(2,1)S(1)}, u32[]{:S(2)}, u32[]{:S(2)}) collective-permute-start(bf16[128,1536]{1,0:T(8,128)(2,1)S(1)} %constant_dynamic-update-slice_fusion.refs_0_.refs_8_), channel_id=1, source_target_pairs={{0,48},{1,49},{2,50},{3,51},{4,52},{5,53},{6,54},{7,55},{8,56},{9,... | collective-permute-start | bytes 1179656 | tf_op jit(solution)/shard_map/ppermute | solution.py:32
  5.8 4.1 %collective-permute-start.5 = (bf16[128,1536]{1,0:T(8,128)(2,1)S(1)}, bf16[128,1536]{1,0:T(8,128)(2,1)S(1)}, u32[]{:S(2)}, u32[]{:S(2)}) collective-permute-start(bf16[128,1536]{1,0:T(8,128)(2,1)S(1)} %constant_dynamic-update-slice_fusion.refs_0_.refs_8_), channel_id=1, source_target_pairs={{0,72},{1,73},{2,74},{3,75},{4,76},{5,77},{6,78},{7,79},{8,64},{9,... | collective-permute-start | bytes 1179656 | tf_op jit(solution)/shard_map/ppermute | solution.py:32
  9.9 4.6 %collective-permute-done.refs_1_.refs_10_ = bf16[128,1536]{1,0:T(8,128)(2,1)S(1)} collective-permute-done((bf16[128,1536]{1,0:T(8,128)(2,1)S(1)}, bf16[128,1536]{1,0:T(8,128)(2,1)S(1)}, u32[]{:S(2)}, u32[]{:S(2)}) %collective-permute-start) | collective-permute-done | bytes 393248 | tf_op jit(solution)/shard_map/ppermute | solution.py:32
  15.1 1.6 %copy-done = bf16[2048,512]{1,0:T(8,128)(2,1)S(1)} copy-done((bf16[2048,512]{1,0:T(8,128)(2,1)S(1)}, bf16[2048,512]{1,0:T(8,128)(2,1)}, u32[]{:S(2)}) %copy-start) | copy-done | bytes 2097176
  16.7 2.2 %copy-done.2 = bf16[2048,1024]{1,0:T(8,128)(2,1)S(1)} copy-done((bf16[2048,1024]{1,0:T(8,128)(2,1)S(1)}, bf16[2048,1024]{1,0:T(8,128)(2,1)}, u32[]{:S(2)}) %copy-start.2) | copy-done | bytes 4194328
  18.9 3.5 %shard_map.67 = (f32[128,2048]{1,0:T(8,128)S(1)}, f32[128,2048]{1,0:T(8,128)S(1)}, f32[8,2048]{1,0:T(8,128)S(1)}) custom-call(bf16[128,1536]{1,0:T(8,128)(2,1)S(1)} %constant_dynamic-update-slice_fusion.refs_0_.refs_8_, bf16[8,2,128,1024]{3,2,1,0:T(8,128)(2,1)S(1)} %bitcast.47, bf16[8,2,128,512]{3,2,1,0:T(8,128)(2,1)S(1)} %bitcast.35), custom_call_target="tpu_custom_call" | custom-call | flops 805306368 | bytes 8388608 | tf_op jit(solution)/shard_map/pallas_call | solution.py:129
  22.4 2.8 %collective-permute-start.3 = (bf16[64,1536]{1,0:T(8,128)(2,1)S(1)}, bf16[64,1536]{1,0:T(8,128)(2,1)S(1)}, u32[]{:S(2)}, u32[]{:S(2)}) collective-permute-start(bf16[64,1536]{1,0:T(8,128)(2,1)S(1)} %slice.90), channel_id=1, source_target_pairs={{0,48},{1,49},{2,50},{3,51},{4,52},{5,53},{6,54},{7,55},{8,56},{9,... | collective-permute-start | bytes 589832 | tf_op jit(solution)/shard_map/ppermute | solution.py:32
  27.3 3.3 %collective-permute-done.3 = bf16[64,1536]{1,0:T(8,128)(2,1)S(1)} collective-permute-done((bf16[64,1536]{1,0:T(8,128)(2,1)S(1)}, bf16[64,1536]{1,0:T(8,128)(2,1)S(1)}, u32[]{:S(2)}, u32[]{:S(2)}) %collective-permute-start.3) | collective-permute-done | bytes 196640 | tf_op jit(solution)/shard_map/ppermute | solution.py:32
  30.7 4.3 %collective-permute-start.4 = (bf16[128,1536]{1,0:T(8,128)(2,1)S(1)}, bf16[128,1536]{1,0:T(8,128)(2,1)S(1)}, u32[]{:S(2)}, u32[]{:S(2)}) collective-permute-start(bf16[128,1536]{1,0:T(8,128)(2,1)S(1)} %constant_dynamic-update-slice_fusion.2.refs_0_.refs_14_), channel_id=1, source_target_pairs={{0,72},{1,73},{2,74},{3,75},{4,76},{5,77},{6,78},{7,79},{8,64},{9,... | collective-permute-start | bytes 1179656 | tf_op jit(solution)/shard_map/ppermute | solution.py:32
  35.0 8.7 %shard_map.68 = (f32[384,2048]{1,0:T(8,128)S(1)}, f32[384,2048]{1,0:T(8,128)S(1)}, f32[8,2048]{1,0:T(8,128)S(1)}) custom-call(bf16[128,1536]{1,0:T(8,128)(2,1)S(1)} %collective-permute-done.5.refs_0_.refs_9_, bf16[128,1536]{1,0:T(8,128)(2,1)S(1)} %collective-permute-done.refs_1_.refs_10_, bf16[128,1536]{1,0:T(8,128)(2,1)S(1)} %collective-permute-done.2.refs_2_.refs_12_, ...), custom_call_target="tpu_custom_call" | custom-call | flops 2415919104 | bytes 12582912 | tf_op jit(solution)/shard_map/pallas_call | solution.py:129
  43.7 1.7 %copy-done.3 = f32[384,2048]{1,0:T(8,128)} copy-done((f32[384,2048]{1,0:T(8,128)}, f32[384,2048]{1,0:T(8,128)S(1)}, u32[]{:S(2)}) %copy-start.3) | copy-done | bytes 3145752
  45.4 1.7 %copy-done.5 = f32[384,2048]{1,0:T(8,128)} copy-done((f32[384,2048]{1,0:T(8,128)}, f32[384,2048]{1,0:T(8,128)S(1)}, u32[]{:S(2)}) %copy-start.5) | copy-done | bytes 3145752
  47.2 8.7 %shard_map.69 = (f32[384,2048]{1,0:T(8,128)S(1)}, f32[384,2048]{1,0:T(8,128)S(1)}, f32[8,2048]{1,0:T(8,128)S(1)}) custom-call(bf16[128,1536]{1,0:T(8,128)(2,1)S(1)} %constant_dynamic-update-slice_fusion.2.refs_0_.refs_14_, bf16[128,1536]{1,0:T(8,128)(2,1)S(1)} %collective-permute-done.6.refs_1_.refs_11_, ...), custom_call_target="tpu_custom_call" | custom-call | flops 2415919104 | bytes 12582912 | tf_op jit(solution)/shard_map/pallas_call | solution.py:129
  56.0 1.8 %copy-done.7 = f32[384,2048]{1,0:T(8,128)} copy-done((f32[384,2048]{1,0:T(8,128)}, f32[384,2048]{1,0:T(8,128)S(1)}, u32[]{:S(2)}) %copy-start.7) | copy-done | bytes 3145752
  57.7 3.5 %shard_map.70 = (f32[128,2048]{1,0:T(8,128)S(1)}, f32[128,2048]{1,0:T(8,128)S(1)}, f32[4,2048]{1,0:T(4,128)S(1)}) custom-call(bf16[128,1536]{1,0:T(8,128)(2,1)S(1)} %collective-permute-done.4.refs_0_.refs_15_, bf16[8,2,128,1024]{3,2,1,0:T(8,128)(2,1)S(1)} %bitcast.50, bf16[8,2,128,512]{3,2,1,0:T(8,128)(2,1)S(1)} %bitcast.38, ...), custom_call_target="tpu_custom_call" | custom-call | flops 805306368 | bytes 8388608 | tf_op jit(solution)/shard_map/pallas_call | solution.py:129
  65.3 3.9 %collective-permute-done.9 = f32[4,2048]{1,0:T(4,128)S(1)} collective-permute-done((f32[4,2048]{1,0:T(4,128)S(1)}, f32[4,2048]{1,0:T(4,128)S(1)}, u32[]{:S(2)}, u32[]{:S(2)}) %collective-permute-start.9) | collective-permute-done | bytes 32800 | tf_op jit(solution)/shard_map/ppermute | solution.py:32
  71.1 3.0 %collective-permute-start.12 = (f32[4,2048]{1,0:T(4,128)}, f32[4,2048]{1,0:T(4,128)}, u32[]{:S(2)}, u32[]{:S(2)}) collective-permute-start(f32[4,2048]{1,0:T(4,128)} %maximum_maximum_fusion.1), channel_id=1, source_target_pairs={{0,6},{1,7},{2,0},{3,1},{4,2},{5,3},{6,4},{7,5},{8,14},{9,15},{10,... | collective-permute-start | bytes 98312 | tf_op jit(solution)/shard_map/ppermute | solution.py:32
  76.0 3.8 %collective-permute-done.11 = f32[4,2048]{1,0:T(4,128)} collective-permute-done((f32[4,2048]{1,0:T(4,128)}, f32[4,2048]{1,0:T(4,128)}, u32[]{:S(2)}, u32[]{:S(2)}) %collective-permute-start.11) | collective-permute-done | bytes 32800 | tf_op jit(solution)/shard_map/ppermute | solution.py:32
  81.4 1.9 %copy-done.4 = f32[384,2048]{1,0:T(8,128)S(1)} copy-done((f32[384,2048]{1,0:T(8,128)S(1)}, f32[384,2048]{1,0:T(8,128)}, u32[]{:S(2)}) %copy-start.4) | copy-done | bytes 3145752
  83.3 1.9 %copy-done.6 = f32[384,2048]{1,0:T(8,128)S(1)} copy-done((f32[384,2048]{1,0:T(8,128)S(1)}, f32[384,2048]{1,0:T(8,128)}, u32[]{:S(2)}) %copy-start.6) | copy-done | bytes 3145752
  85.2 1.9 %copy-done.8 = f32[384,2048]{1,0:T(8,128)S(1)} copy-done((f32[384,2048]{1,0:T(8,128)S(1)}, f32[384,2048]{1,0:T(8,128)}, u32[]{:S(2)}) %copy-start.8) | copy-done | bytes 3145752
  97.8 5.0 %shard_map.71 = (bf16[8,512,128]{2,1,0:T(8,128)(2,1)S(1)}, bf16[1024,1024]{1,0:T(8,128)(2,1)S(1)}) custom-call(s32[1]{0:T(128)} %bitcast.30.which.half, f32[128,2048]{1,0:T(8,128)S(1)} %get-tuple-element.31.refs_0_, f32[384,2048]{1,0:T(8,128)S(1)} %copy-done.4, f32[384,2048]{1,0:T(8,128)S(1)} %copy-done.8, f32[128,2048]{1,0:T(8,128)S(1)} %copy-done.14, ...), custom_call_target="tpu_custom_call" | custom-call | flops 1073741824 | bytes 12582912 | tf_op jit(solution)/shard_map/pallas_call | solution.py:206
  102.8 5.0 %shard_map.72 = (bf16[8,512,128]{2,1,0:T(8,128)(2,1)S(1)}, bf16[1024,1024]{1,0:T(8,128)(2,1)S(1)}) custom-call(s32[1]{0:T(128)S(6)} %sub.187.which, f32[128,2048]{1,0:T(8,128)S(1)} %get-tuple-element.31.refs_0_, f32[384,2048]{1,0:T(8,128)S(1)} %copy-done.4, f32[384,2048]{1,0:T(8,128)S(1)} %copy-done.8, f32[128,2048]{1,0:T(8,128)S(1)} %copy-done.14, ...), custom_call_target="tpu_custom_call" | custom-call | flops 1073741824 | bytes 12582912 | tf_op jit(solution)/shard_map/pallas_call | solution.py:206
  110.7 2.3 %collective-permute-start.21 = (bf16[256,512]{1,0:T(8,128)(2,1)S(1)}, bf16[256,512]{1,0:T(8,128)(2,1)S(1)}, u32[]{:S(2)}, u32[]{:S(2)}) collective-permute-start(bf16[256,512]{1,0:T(8,128)(2,1)S(1)} %shard_map.74), channel_id=1, source_target_pairs={{0,32},{1,33},{2,34},{3,35},{4,36},{5,37},{6,38},{7,39},{8,40},{9,... | collective-permute-start | bytes 786440 | tf_op jit(solution)/shard_map/ppermute | solution.py:32
  117.1 3.9 %collective-permute-done.21 = bf16[256,512]{1,0:T(8,128)(2,1)S(1)} collective-permute-done((bf16[256,512]{1,0:T(8,128)(2,1)S(1)}, bf16[256,512]{1,0:T(8,128)(2,1)S(1)}, u32[]{:S(2)}, u32[]{:S(2)}) %collective-permute-start.21) | collective-permute-done | bytes 262176 | tf_op jit(solution)/shard_map/ppermute | solution.py:32
  120.9 3.8 %collective-permute-done.22 = bf16[256,512]{1,0:T(8,128)(2,1)S(1)} collective-permute-done((bf16[256,512]{1,0:T(8,128)(2,1)S(1)}, bf16[256,512]{1,0:T(8,128)(2,1)S(1)}, u32[]{:S(2)}, u32[]{:S(2)}) %collective-permute-start.22) | collective-permute-done | bytes 262176 | tf_op jit(solution)/shard_map/ppermute | solution.py:32
  127.0 2.1 %collective-permute-start.15 = (bf16[512,128]{1,0:T(8,128)(2,1)S(1)}, bf16[512,128]{1,0:T(8,128)(2,1)S(1)}, u32[]{:S(2)}, u32[]{:S(2)}) collective-permute-start(bf16[512,128]{1,0:T(8,128)(2,1)S(1)} %get-tuple-element.43), channel_id=1, source_target_pairs={{0,4},{1,5},{2,6},{3,7},{4,0},{5,1},{6,2},{7,3},{8,12},{9,13},{10,... | collective-permute-start | bytes 393224 | tf_op jit(solution)/shard_map/ppermute | solution.py:32
  130.6 3.5 %collective-permute-start.17 = (bf16[512,128]{1,0:T(8,128)(2,1)S(1)}, bf16[512,128]{1,0:T(8,128)(2,1)S(1)}, u32[]{:S(2)}, u32[]{:S(2)}) collective-permute-start(bf16[512,128]{1,0:T(8,128)(2,1)S(1)} %get-tuple-element.45), channel_id=1, source_target_pairs={{0,14},{1,15},{2,8},{3,9},{4,10},{5,11},{6,12},{7,13},{8,6},{9,7},... | collective-permute-start | bytes 393224 | tf_op jit(solution)/shard_map/ppermute | solution.py:32
  135.6 1.7 %collective-permute-start.19 = (bf16[512,128]{1,0:T(8,128)(2,1)S(1)}, bf16[512,128]{1,0:T(8,128)(2,1)S(1)}, u32[]{:S(2)}, u32[]{:S(2)}) collective-permute-start(bf16[512,128]{1,0:T(8,128)(2,1)S(1)} %get-tuple-element.47), channel_id=1, source_target_pairs={{0,6},{1,7},{2,0},{3,1},{4,2},{5,3},{6,4},{7,5},{8,14},{9,15},{10,... | collective-permute-start | bytes 393224 | tf_op jit(solution)/shard_map/ppermute | solution.py:32
  137.3 1.8 %collective-permute-start.20 = (bf16[512,128]{1,0:T(8,128)(2,1)S(1)}, bf16[512,128]{1,0:T(8,128)(2,1)S(1)}, u32[]{:S(2)}, u32[]{:S(2)}) collective-permute-start(bf16[512,128]{1,0:T(8,128)(2,1)S(1)} %get-tuple-element.48), channel_id=1, source_target_pairs={{0,8},{1,9},{2,10},{3,11},{4,12},{5,13},{6,14},{7,15},{8,0},{9,1},... | collective-permute-start | bytes 393224 | tf_op jit(solution)/shard_map/ppermute | solution.py:32
  140.5 1.7 %collective-permute-done.20 = bf16[512,128]{1,0:T(8,128)(2,1)S(1)} collective-permute-done((bf16[512,128]{1,0:T(8,128)(2,1)S(1)}, bf16[512,128]{1,0:T(8,128)(2,1)S(1)}, u32[]{:S(2)}, u32[]{:S(2)}) %collective-permute-start.20) | collective-permute-done | bytes 131104 | tf_op jit(solution)/shard_map/ppermute | solution.py:32
  (138 shorter events, 39.0 us)
Async XLA Ops:
  2.5 12.0 %collective-permute-start = (bf16[128,1536]{1,0:T(8,128)(2,1)S(1)}, bf16[128,1536]{1,0:T(8,128)(2,1)S(1)}, u32[]{:S(2)}, u32[]{:S(2)}) collective-permute-start(bf16[128,1536]{1,0:T(8,128)(2,1)S(1)} %constant_dynamic-update-slice_fusion.refs_0_.refs_8_), channel_id=1, source_target_pairs={{0,16},{1,17},{2,18},{3,19},{4,20},{5,21},{6,22},{7,23},{8,24},{9,... | collective-permute-start | bytes 1179656 | tf_op jit(solution)/shard_map/ppermute | solution.py:32
  4.2 18.2 %collective-permute-start.2 = (bf16[128,1536]{1,0:T(8,128)(2,1)S(1)}, bf16[128,1536]{1,0:T(8,128)(2,1)S(1)}, u32[]{:S(2)}, u32[]{:S(2)}) collective-permute-start(bf16[128,1536]{1,0:T(8,128)(2,1)S(1)} %constant_dynamic-update-slice_fusion.refs_0_.refs_8_), channel_id=1, source_target_pairs={{0,48},{1,49},{2,50},{3,51},{4,52},{5,53},{6,54},{7,55},{8,56},{9,... | collective-permute-start | bytes 1179656 | tf_op jit(solution)/shard_map/ppermute | solution.py:32
  5.8 19.5 %collective-permute-start.5 = (bf16[128,1536]{1,0:T(8,128)(2,1)S(1)}, bf16[128,1536]{1,0:T(8,128)(2,1)S(1)}, u32[]{:S(2)}, u32[]{:S(2)}) collective-permute-start(bf16[128,1536]{1,0:T(8,128)(2,1)S(1)} %constant_dynamic-update-slice_fusion.refs_0_.refs_8_), channel_id=1, source_target_pairs={{0,72},{1,73},{2,74},{3,75},{4,76},{5,77},{6,78},{7,79},{8,64},{9,... | collective-permute-start | bytes 1179656 | tf_op jit(solution)/shard_map/ppermute | solution.py:32
  14.5 20.4 %copy-start.19 = (bf16[128,1536]{1,0:T(8,128)(2,1)}, bf16[128,1536]{1,0:T(8,128)(2,1)S(1)}, u32[]{:S(2)}) copy-start(bf16[128,1536]{1,0:T(8,128)(2,1)S(1)} %collective-permute-done.refs_1_.refs_10_) | copy-start | bytes 1179652
  14.6 12.8 %collective-permute-start.1 = (bf16[64,1536]{1,0:T(8,128)(2,1)S(1)}, bf16[64,1536]{1,0:T(8,128)(2,1)S(1)}, u32[]{:S(2)}, u32[]{:S(2)}) collective-permute-start(bf16[64,1536]{1,0:T(8,128)(2,1)S(1)} %slice.89), channel_id=1, source_target_pairs={{0,16},{1,17},{2,18},{3,19},{4,20},{5,21},{6,22},{7,23},{8,24},{9,... | collective-permute-start | bytes 589832 | tf_op jit(solution)/shard_map/ppermute | solution.py:32
  22.4 21.3 %copy-start.21 = (bf16[128,1536]{1,0:T(8,128)(2,1)}, bf16[128,1536]{1,0:T(8,128)(2,1)S(1)}, u32[]{:S(2)}) copy-start(bf16[128,1536]{1,0:T(8,128)(2,1)S(1)} %collective-permute-done.2.refs_2_.refs_12_) | copy-start | bytes 1179652
  22.4 8.2 %collective-permute-start.3 = (bf16[64,1536]{1,0:T(8,128)(2,1)S(1)}, bf16[64,1536]{1,0:T(8,128)(2,1)S(1)}, u32[]{:S(2)}, u32[]{:S(2)}) collective-permute-start(bf16[64,1536]{1,0:T(8,128)(2,1)S(1)} %slice.90), channel_id=1, source_target_pairs={{0,48},{1,49},{2,50},{3,51},{4,52},{5,53},{6,54},{7,55},{8,56},{9,... | collective-permute-start | bytes 589832 | tf_op jit(solution)/shard_map/ppermute | solution.py:32
  25.3 21.9 %collective-permute-start.7 = (bf16[128,1536]{1,0:T(8,128)(2,1)S(1)}, bf16[128,1536]{1,0:T(8,128)(2,1)S(1)}, u32[]{:S(2)}, u32[]{:S(2)}) collective-permute-start(bf16[128,1536]{1,0:T(8,128)(2,1)S(1)} %collective-permute-done.5.refs_0_.refs_9_), channel_id=1, source_target_pairs={{0,48},{1,49},{2,50},{3,51},{4,52},{5,53},{6,54},{7,55},{8,56},{9,... | collective-permute-start | bytes 1179656 | tf_op jit(solution)/shard_map/ppermute | solution.py:32
  25.8 21.3 %collective-permute-start.6 = (bf16[128,1536]{1,0:T(8,128)(2,1)S(1)}, bf16[128,1536]{1,0:T(8,128)(2,1)S(1)}, u32[]{:S(2)}, u32[]{:S(2)}) collective-permute-start(bf16[128,1536]{1,0:T(8,128)(2,1)S(1)} %collective-permute-done.5.refs_0_.refs_9_), channel_id=1, source_target_pairs={{0,16},{1,17},{2,18},{3,19},{4,20},{5,21},{6,22},{7,23},{8,24},{9,... | collective-permute-start | bytes 1179656 | tf_op jit(solution)/shard_map/ppermute | solution.py:32
  30.7 27.1 %collective-permute-start.4 = (bf16[128,1536]{1,0:T(8,128)(2,1)S(1)}, bf16[128,1536]{1,0:T(8,128)(2,1)S(1)}, u32[]{:S(2)}, u32[]{:S(2)}) collective-permute-start(bf16[128,1536]{1,0:T(8,128)(2,1)S(1)} %constant_dynamic-update-slice_fusion.2.refs_0_.refs_14_), channel_id=1, source_target_pairs={{0,72},{1,73},{2,74},{3,75},{4,76},{5,77},{6,78},{7,79},{8,64},{9,... | collective-permute-start | bytes 1179656 | tf_op jit(solution)/shard_map/ppermute | solution.py:32
  63.2 1.2 collective-permute-start.8
  65.2 4.0 %collective-permute-start.9 = (f32[4,2048]{1,0:T(4,128)S(1)}, f32[4,2048]{1,0:T(4,128)S(1)}, u32[]{:S(2)}, u32[]{:S(2)}) collective-permute-start(f32[4,2048]{1,0:T(4,128)S(1)} %maximum_maximum_fusion), channel_id=1, source_target_pairs={{0,8},{1,9},{2,10},{3,11},{4,12},{5,13},{6,14},{7,15},{8,0},{9,1},... | collective-permute-start | bytes 98312 | tf_op jit(solution)/shard_map/ppermute | solution.py:32
  71.1 4.9 %collective-permute-start.12 = (f32[4,2048]{1,0:T(4,128)}, f32[4,2048]{1,0:T(4,128)}, u32[]{:S(2)}, u32[]{:S(2)}) collective-permute-start(f32[4,2048]{1,0:T(4,128)} %maximum_maximum_fusion.1), channel_id=1, source_target_pairs={{0,6},{1,7},{2,0},{3,1},{4,2},{5,3},{6,4},{7,5},{8,14},{9,15},{10,... | collective-permute-start | bytes 98312 | tf_op jit(solution)/shard_map/ppermute | solution.py:32
  74.1 5.7 %collective-permute-start.11 = (f32[4,2048]{1,0:T(4,128)}, f32[4,2048]{1,0:T(4,128)}, u32[]{:S(2)}, u32[]{:S(2)}) collective-permute-start(f32[4,2048]{1,0:T(4,128)} %maximum_maximum_fusion.1), channel_id=1, source_target_pairs={{0,4},{1,5},{2,6},{3,7},{4,0},{5,1},{6,2},{7,3},{8,12},{9,13},{10,... | collective-permute-start | bytes 98312 | tf_op jit(solution)/shard_map/ppermute | solution.py:32
  74.8 5.4 %collective-permute-start.10 = (f32[4,2048]{1,0:T(4,128)}, f32[4,2048]{1,0:T(4,128)}, u32[]{:S(2)}, u32[]{:S(2)}) collective-permute-start(f32[4,2048]{1,0:T(4,128)} %maximum_maximum_fusion.1), channel_id=1, source_target_pairs={{0,2},{1,3},{2,4},{3,5},{4,6},{5,7},{6,0},{7,1},{8,10},{9,11},{10,... | collective-permute-start | bytes 98312 | tf_op jit(solution)/shard_map/ppermute | solution.py:32
  110.6 18.5 %copy-start.34 = (f32[1,2048]{1,0:T(1,128)S(1)}, f32[1,2048]{1,0:T(1,128)}, u32[]{:S(2)}) copy-start(f32[1,2048]{1,0:T(1,128)} %get-tuple-element.76) | copy-start | bytes 24580
  110.6 18.5 %copy-start.35 = (f32[1,2048]{1,0:T(1,128)S(1)}, f32[1,2048]{1,0:T(1,128)}, u32[]{:S(2)}) copy-start(f32[1,2048]{1,0:T(1,128)} %get-tuple-element.78) | copy-start | bytes 24580
  110.6 18.5 %copy-start.36 = (f32[1,2048]{1,0:T(1,128)S(1)}, f32[1,2048]{1,0:T(1,128)}, u32[]{:S(2)}) copy-start(f32[1,2048]{1,0:T(1,128)} %get-tuple-element.85) | copy-start | bytes 24580
  110.6 18.5 %copy-start.37 = (f32[1,2048]{1,0:T(1,128)S(1)}, f32[1,2048]{1,0:T(1,128)}, u32[]{:S(2)}) copy-start(f32[1,2048]{1,0:T(1,128)} %get-tuple-element.72) | copy-start | bytes 24580
  110.6 18.5 %copy-start.38 = (f32[1,2048]{1,0:T(1,128)S(1)}, f32[1,2048]{1,0:T(1,128)}, u32[]{:S(2)}) copy-start(f32[1,2048]{1,0:T(1,128)} %get-tuple-element.73) | copy-start | bytes 24580
  110.7 10.3 %collective-permute-start.21 = (bf16[256,512]{1,0:T(8,128)(2,1)S(1)}, bf16[256,512]{1,0:T(8,128)(2,1)S(1)}, u32[]{:S(2)}, u32[]{:S(2)}) collective-permute-start(bf16[256,512]{1,0:T(8,128)(2,1)S(1)} %shard_map.74), channel_id=1, source_target_pairs={{0,32},{1,33},{2,34},{3,35},{4,36},{5,37},{6,38},{7,39},{8,40},{9,... | collective-permute-start | bytes 786440 | tf_op jit(solution)/shard_map/ppermute | solution.py:32
  113.0 11.7 %collective-permute-start.22 = (bf16[256,512]{1,0:T(8,128)(2,1)S(1)}, bf16[256,512]{1,0:T(8,128)(2,1)S(1)}, u32[]{:S(2)}, u32[]{:S(2)}) collective-permute-start(bf16[256,512]{1,0:T(8,128)(2,1)S(1)} %shard_map.75), channel_id=1, source_target_pairs={{0,48},{1,49},{2,50},{3,51},{4,52},{5,53},{6,54},{7,55},{8,56},{9,... | collective-permute-start | bytes 786440 | tf_op jit(solution)/shard_map/ppermute | solution.py:32
  114.5 10.2 %collective-permute-start.23 = (bf16[256,512]{1,0:T(8,128)(2,1)S(1)}, bf16[256,512]{1,0:T(8,128)(2,1)S(1)}, u32[]{:S(2)}, u32[]{:S(2)}) collective-permute-start(bf16[256,512]{1,0:T(8,128)(2,1)S(1)} %shard_map.76), channel_id=1, source_target_pairs={{0,16},{1,17},{2,18},{3,19},{4,20},{5,21},{6,22},{7,23},{8,24},{9,... | collective-permute-start | bytes 786440 | tf_op jit(solution)/shard_map/ppermute | solution.py:32
  115.3 9.7 %collective-permute-start.13 = (bf16[8,512,128]{2,1,0:T(8,128)(2,1)S(1)}, bf16[8,512,128]{2,1,0:T(8,128)(2,1)S(1)}, u32[]{:S(2)}, u32[]{:S(2)}) collective-permute-start(bf16[8,512,128]{2,1,0:T(8,128)(2,1)S(1)} %get-tuple-element.40), channel_id=1, source_target_pairs={{0,1},{1,0},{2,3},{3,2},{4,5},{5,4},{6,7},{7,6},{8,9},{9,8},{10,11... | collective-permute-start | bytes 3145736 | tf_op jit(solution)/shard_map/ppermute | solution.py:32
  124.9 9.1 %collective-permute-start.24 = (bf16[128,512]{1,0:T(8,128)(2,1)S(1)}, bf16[128,512]{1,0:T(8,128)(2,1)S(1)}, u32[]{:S(2)}, u32[]{:S(2)}) collective-permute-start(bf16[128,512]{1,0:T(8,128)(2,1)S(1)} %slice.136), channel_id=1, source_target_pairs={{0,72},{1,73},{2,74},{3,75},{4,76},{5,77},{6,78},{7,79},{8,64},{9,... | collective-permute-start | bytes 393224 | tf_op jit(solution)/shard_map/ppermute | solution.py:32
  125.8 9.7 %collective-permute-start.14 = (bf16[512,128]{1,0:T(8,128)(2,1)S(1)}, bf16[512,128]{1,0:T(8,128)(2,1)S(1)}, u32[]{:S(2)}, u32[]{:S(2)}) collective-permute-start(bf16[512,128]{1,0:T(8,128)(2,1)S(1)} %get-tuple-element.42), channel_id=1, source_target_pairs={{0,12},{1,13},{2,14},{3,15},{4,8},{5,9},{6,10},{7,11},{8,4},{9,5},... | collective-permute-start | bytes 393224 | tf_op jit(solution)/shard_map/ppermute | solution.py:32
  127.0 10.3 %collective-permute-start.15 = (bf16[512,128]{1,0:T(8,128)(2,1)S(1)}, bf16[512,128]{1,0:T(8,128)(2,1)S(1)}, u32[]{:S(2)}, u32[]{:S(2)}) collective-permute-start(bf16[512,128]{1,0:T(8,128)(2,1)S(1)} %get-tuple-element.43), channel_id=1, source_target_pairs={{0,4},{1,5},{2,6},{3,7},{4,0},{5,1},{6,2},{7,3},{8,12},{9,13},{10,... | collective-permute-start | bytes 393224 | tf_op jit(solution)/shard_map/ppermute | solution.py:32
  129.9 9.8 %collective-permute-start.16 = (bf16[512,128]{1,0:T(8,128)(2,1)S(1)}, bf16[512,128]{1,0:T(8,128)(2,1)S(1)}, u32[]{:S(2)}, u32[]{:S(2)}) collective-permute-start(bf16[512,128]{1,0:T(8,128)(2,1)S(1)} %get-tuple-element.44), channel_id=1, source_target_pairs={{0,10},{1,11},{2,12},{3,13},{4,14},{5,15},{6,8},{7,9},{8,2},{9,3},... | collective-permute-start | bytes 393224 | tf_op jit(solution)/shard_map/ppermute | solution.py:32
  130.6 9.2 %collective-permute-start.17 = (bf16[512,128]{1,0:T(8,128)(2,1)S(1)}, bf16[512,128]{1,0:T(8,128)(2,1)S(1)}, u32[]{:S(2)}, u32[]{:S(2)}) collective-permute-start(bf16[512,128]{1,0:T(8,128)(2,1)S(1)} %get-tuple-element.45), channel_id=1, source_target_pairs={{0,14},{1,15},{2,8},{3,9},{4,10},{5,11},{6,12},{7,13},{8,6},{9,7},... | collective-permute-start | bytes 393224 | tf_op jit(solution)/shard_map/ppermute | solution.py:32
  134.0 6.2 %collective-permute-start.18 = (bf16[512,128]{1,0:T(8,128)(2,1)S(1)}, bf16[512,128]{1,0:T(8,128)(2,1)S(1)}, u32[]{:S(2)}, u32[]{:S(2)}) collective-permute-start(bf16[512,128]{1,0:T(8,128)(2,1)S(1)} %get-tuple-element.46), channel_id=1, source_target_pairs={{0,2},{1,3},{2,4},{3,5},{4,6},{5,7},{6,0},{7,1},{8,10},{9,11},{10,... | collective-permute-start | bytes 393224 | tf_op jit(solution)/shard_map/ppermute | solution.py:32
  135.6 5.0 %collective-permute-start.19 = (bf16[512,128]{1,0:T(8,128)(2,1)S(1)}, bf16[512,128]{1,0:T(8,128)(2,1)S(1)}, u32[]{:S(2)}, u32[]{:S(2)}) collective-permute-start(bf16[512,128]{1,0:T(8,128)(2,1)S(1)} %get-tuple-element.47), channel_id=1, source_target_pairs={{0,6},{1,7},{2,0},{3,1},{4,2},{5,3},{6,4},{7,5},{8,14},{9,15},{10,... | collective-permute-start | bytes 393224 | tf_op jit(solution)/shard_map/ppermute | solution.py:32
  137.3 5.0 %collective-permute-start.20 = (bf16[512,128]{1,0:T(8,128)(2,1)S(1)}, bf16[512,128]{1,0:T(8,128)(2,1)S(1)}, u32[]{:S(2)}, u32[]{:S(2)}) collective-permute-start(bf16[512,128]{1,0:T(8,128)(2,1)S(1)} %get-tuple-element.48), channel_id=1, source_target_pairs={{0,8},{1,9},{2,10},{3,11},{4,12},{5,13},{6,14},{7,15},{8,0},{9,1},... | collective-permute-start | bytes 393224 | tf_op jit(solution)/shard_map/ppermute | solution.py:32
  (36 other events, 201.4 us)

commit v2 on v0

v2 whole, which is shorter than its diff:
```python
import functools
import math

import jax
import jax.numpy as jnp
from jax import lax
from jax.experimental import pallas as pl
from jax.experimental.pallas import tpu as pltpu
from jax.sharding import PartitionSpec as P

AXES = ("blk", "grp")
LOG2E = 1.0 / math.log(2.0)
LN2 = math.log(2.0)
MIB = 1024 * 1024
F32 = jnp.float32
BF16 = jnp.bfloat16
VMEM = pltpu.VMEM
LANES = 128
WIDE = 256


def place(i):
    b, g = divmod(i, 16)
    zh, x = divmod(b, 4)
    zl, r = divmod(g, 8)
    y, c = divmod(r, 2)
    return zh, x, zl, y, c


def index(zh, x, zl, y, c):
    return (zh * 4 + x) * 16 + (zl * 4 + y) * 2 + c


def permute(v, move):
    return lax.ppermute(v, AXES, [(i, index(*move(*place(i)))) for i in range(128)])


def along_x(k):
    return lambda zh, x, zl, y, c: (zh, (x + k) % 4, zl, y, c)


def along_y(k, flip=0):
    return lambda zh, x, zl, y, c: (zh, x, zl ^ flip, (y + k) % 4, c)


def other_core(zh, x, zl, y, c):
    return (zh, x, zl, y, 1 - c)


def other_core_and_z(zh, x, zl, y, c):
    return (zh, x, 1 - zl, y, 1 - c)


def cross_z(zh, x, zl, y, c):
    return (1 - zh, x, 1 - zl, y, c)


def call(body, args, out_shape, limit, flops=0, size=0, exps=0, **more):
    specs = [pl.BlockSpec(memory_space=space) for space, _ in args]
    values = [
        v if space is pltpu.SMEM else pltpu.with_memory_space_constraint(v, space)
        for space, v in args
    ]
    return pl.pallas_call(
        body,
        in_specs=specs,
        out_specs=[pl.BlockSpec(memory_space=VMEM)] * len(out_shape),
        out_shape=[VMEM(*s) for s in out_shape],
        compiler_params=pltpu.CompilerParams(vmem_limit_bytes=limit * MIB),
        cost_estimate=pl.CostEstimate(flops=flops, bytes_accessed=size, transcendentals=exps),
        **more,
    )(*values)


def join_kernel(text_t, text_s, out, sems):
    width = text_t.shape[1]
    copies = [
        pltpu.make_async_copy(text_t, out.at[:, :width], sems.at[0]),
        pltpu.make_async_copy(text_s, out.at[:, width:], sems.at[1]),
    ]
    for copy in copies:
        copy.start()
    for copy in copies:
        copy.wait()


def join(text_t, text_s):
    n, width = text_t.shape[0], text_t.shape[1] + text_s.shape[1]
    return call(
        join_kernel,
        [(pltpu.HBM, text_t), (pltpu.HBM, text_s)],
        [((n, width), BF16)],
        4,
        scratch_shapes=[pltpu.SemaphoreType.DMA((2,))],
    )[0]


def scales(width_t, width_s):
    return 3.0 / math.sqrt(width_t) * LOG2E, 3.0 / math.sqrt(width_s) * LOG2E


def tile_logits(parts, image_t, image_s, logit_t, logit_s, before, cols):
    scale_t, scale_s = scales(image_t.shape[0], image_s.shape[0])
    tops_t, tops_s = [], []
    for at, text_t, text_s in parts:
        n = text_t.shape[0]
        t = jnp.dot(text_t, image_t[:, cols], preferred_element_type=F32) * scale_t
        s = jnp.dot(text_s, image_s[:, cols], preferred_element_type=F32) * scale_s
        logit_t[at : at + n, cols] = t
        logit_s[at : at + n, cols] = s
        tops_t.append(jnp.max(t, axis=0, keepdims=True))
        tops_s.append(jnp.max(s, axis=0, keepdims=True))
    if before is not None:
        old_t, sum_t, old_s, sum_s, gap = (before[k : k + 1, cols] for k in range(5))
        tops_t.append(old_t)
        tops_s.append(old_s)
    top_t = functools.reduce(jnp.maximum, tops_t)
    top_s = functools.reduce(jnp.maximum, tops_s)
    sums = []
    for at, text_t, _ in parts:
        n = text_t.shape[0]
        t = logit_t[at : at + n, cols]
        s = logit_s[at : at + n, cols]
        exp_t = jnp.exp2(t - top_t)
        sums.append(
            [
                jnp.sum(v, axis=0, keepdims=True)
                for v in (exp_t, jnp.exp2(s - top_s), exp_t * (t - s))
            ]
        )
    if before is not None:
        shrink = jnp.exp2(old_t - top_t)
        sums.append([sum_t * shrink, sum_s * jnp.exp2(old_s - top_s), gap * shrink])
    new_t, new_s, new_gap = (functools.reduce(jnp.add, v) for v in zip(*sums))
    return top_t, new_t, top_s, new_s, new_gap


def put_running(stats, cols, values):
    for k, v in enumerate(values):
        stats[k : k + 1, cols] = v
    stats[5:8, cols] = jnp.zeros((3, values[0].shape[1]), F32)


def first_kernel(
    own, far_t, far_s, image_t, image_s, logit_t, logit_s, turned, stats, held_t, held_s, sems
):
    blocks, cores, block, width_t = far_t.shape
    width_s = far_s.shape[3]
    half = blocks // 2
    wide = half * block
    copies = []
    for k in range(2 * cores):
        c, j = divmod(k, 2)
        pieces = [
            pltpu.make_async_copy(far_t.at[half * j : half * j + half, c], held_t.at[k], sems.at[k, 0]),
            pltpu.make_async_copy(far_s.at[half * j : half * j + half, c], held_s.at[k], sems.at[k, 1]),
        ]
        for piece in pieces:
            piece.start()
        copies.append(pieces)
    turned[:, : own.shape[0]] = own[:, width_t:].T
    for k, pieces in enumerate(copies):
        for piece in pieces:
            piece.wait()
        cols = slice(k * wide, k * wide + wide)
        image_t[:, cols] = held_t[k].reshape(wide, width_t).T
        image_s[:, cols] = held_s[k].reshape(wide, width_s).T
        parts = [(0, own[:, :width_t], own[:, width_t:])]
        for at in range(k * wide, k * wide + wide, WIDE):
            cols = slice(at, at + WIDE)
            put_running(
                stats, cols, tile_logits(parts, image_t, image_s, logit_t, logit_s, None, cols)
            )


def first_logits(own, image_t, image_s, texts):
    blocks, cores, block, width_t = image_t.shape
    width_s = image_s.shape[3]
    rows = blocks * cores * block
    out = [
        ((width_t, rows), BF16),
        ((width_s, rows), BF16),
        ((texts, rows), F32),
        ((texts, rows), F32),
        ((width_s, texts), BF16),
        ((8, rows), F32),
    ]
    n = own.shape[0]
    return call(
        first_kernel,
        [(VMEM, own), (pltpu.HBM, image_t), (pltpu.HBM, image_s)],
        out,
        12,
        flops=2 * n * rows * (width_t + width_s),
        size=2 * rows * (width_t + width_s),
        exps=2 * n * rows,
        scratch_shapes=[
            pltpu.VMEM((2 * cores, blocks // 2, block, width_t), BF16),
            pltpu.VMEM((2 * cores, blocks // 2, block, width_s), BF16),
            pltpu.SemaphoreType.DMA((2 * cores, 2)),
        ],
    )


def more_kernel(places, last, *refs):
    count = len(places)
    texts = refs[:count]
    image_t, image_s, _, _, _, before, logit_t, logit_s, turned, stats = refs[count:]
    width_t, rows = image_t.shape
    for at, ref in zip(places, texts):
        turned[:, at : at + ref.shape[0]] = ref[:, width_t:].T
    for begin in range(0, rows, WIDE):
        cols = slice(begin, begin + WIDE)
        parts = [(at, ref[:, :width_t], ref[:, width_t:]) for at, ref in zip(places, texts)]
        top_t, sum_t, top_s, sum_s, gap = values = tile_logits(
            parts, image_t, image_s, logit_t, logit_s, before, cols
        )
        if not last:
            put_running(stats, cols, values)
            continue
        found = (top_t + jnp.log2(sum_t), top_s + jnp.log2(sum_s), gap / sum_t)
        for q, v in enumerate(found):
            for j in range(WIDE // LANES):
                row = q * (rows // LANES) + begin // LANES + j
                stats[row : row + 1, :] = v[:, j * LANES : j * LANES + LANES]


def more_logits(chunks, state, last=False):
    places = tuple(at for at, _ in chunks)
    image_t, image_s, logit_t, logit_s, turned, stats = state
    width_t, rows = image_t.shape
    width_s = image_s.shape[0]
    n = sum(v.shape[0] for _, v in chunks)
    count = len(chunks)
    shape = ((3 * rows // LANES, LANES), F32) if last else (stats.shape, F32)
    logit_t, logit_s, turned, stats = call(
        functools.partial(more_kernel, places, last),
        [(VMEM, v) for _, v in chunks] + [(VMEM, v) for v in state],
        [(logit_t.shape, F32), (logit_s.shape, F32), (turned.shape, BF16), shape],
        4,
        flops=2 * n * rows * (width_t + width_s),
        size=2 * n * rows,
        exps=2 * n * rows,
        input_output_aliases={count + 2: 0, count + 3: 1, count + 4: 2},
    )
    return image_t, image_s, logit_t, logit_s, turned, stats


def merged(parts):
    def total(v):
        return (v[0] + v[1]) + (v[2] + v[3])

    rows = parts[0].shape[0] // 3
    lse_t, lse_s, gap = ([p[rows * k : rows * k + rows, :] for p in parts] for k in range(3))
    top_t = functools.reduce(jnp.maximum, lse_t)
    top_s = functools.reduce(jnp.maximum, lse_s)
    part_t = [jnp.exp2(v - top_t) for v in lse_t]
    sum_t = total(part_t)
    mean = total([p * g for p, g in zip(part_t, gap)]) / sum_t
    all_s = top_s + jnp.log2(total([jnp.exp2(v - top_s) for v in lse_s]))
    return top_t + jnp.log2(sum_t), all_s, mean


def merge_kernel(a, b, c, d, _, __, out, *held):
    rows = out.shape[0] // 3
    for k, v in enumerate(merged((a, b, c, d))):
        out[rows * k : rows * k + rows, :] = v


def merge(parts, held):
    out, *held = call(
        merge_kernel,
        [(VMEM, v) for v in (*parts, *held)],
        [(parts[0].shape, F32)] + [(v.shape, F32) for v in held],
        4,
        input_output_aliases={4: 1, 5: 2},
    )
    return out, held


def put_merged(parts, lse, loss):
    rows = lse.shape[0] // 2
    all_t, all_s, mean = merged(parts)
    lse[:rows, :] = all_t
    lse[rows:, :] = all_s
    value = (mean - all_t + all_s) * LN2
    for j in range(rows // 2):
        for c in range(2):
            at = c * (rows // 2) + j
            loss[2 * j + c : 2 * j + c + 1, :] = value[at : at + 1, :]


def delta_kernel(scale, logit_t, logit_s, turned, a, b, c, d, grad, delta, loss, lse):
    put_merged((a, b, c, d), lse, loss)
    away = 1 - lax.rem(lax.axis_index("grp"), 2)
    count, rows = logit_t.shape
    half = rows // 2
    pair = WIDE // LANES
    for begin in range(0, rows, WIDE):
        cols = slice(begin, begin + WIDE)
        spots = [begin // LANES + k for k in range(pair)]
        low_t = jnp.concatenate([lse[k : k + 1, :] for k in spots], axis=1)
        low_s = jnp.concatenate(
            [lse[k + rows // LANES : k + rows // LANES + 1, :] for k in spots], axis=1
        )
        prob_t = jnp.exp2(logit_t[:, cols] - low_t)
        prob_s = jnp.exp2(logit_s[:, cols] - low_s)
        delta[begin // half, :, begin % half : begin % half + WIDE] = (
            (prob_s - prob_t) * scale
        ).astype(BF16)
    for begin in range(0, half, WIDE):
        out = jnp.dot(
            turned[...], delta[away, :, begin : begin + WIDE], preferred_element_type=F32
        ).astype(BF16)
        for k in range(pair):
            grad[begin // LANES + k] = out[:, k * LANES : k * LANES + LANES]


def delta_part(logit_t, logit_s, turned, stats):
    count, rows = logit_t.shape
    width = turned.shape[0]
    return call(
        functools.partial(delta_kernel, 3.0 / math.sqrt(width)),
        [(VMEM, v) for v in (logit_t, logit_s, turned, *stats)],
        [
            ((rows // 2 // LANES, width, LANES), BF16),
            ((2, count, rows // 2), BF16),
            ((rows // LANES, LANES), F32),
        ],
        4,
        flops=count * rows * width,
        size=2 * count * rows,
        exps=2 * count * rows,
        scratch_shapes=[pltpu.VMEM((2 * rows // LANES, LANES), F32)],
    )


def text_kernel(delta, image_s, *outs):
    blocks, cores, block, width = image_s.shape
    for k, out in zip((3, 1, 2, 0), outs[1:4] + outs[:1]):
        n = out.shape[0]
        total = 0.0
        for c in range(cores):
            total += jnp.dot(
                delta[c, n * k : n * k + n, :],
                image_s[:, c].reshape(blocks * block, width),
                preferred_element_type=F32,
            )
        out[...] = total.astype(out.dtype)


def text_part(delta, image_s):
    _, count, rows = delta.shape
    width = image_s.shape[3]
    return call(
        text_kernel,
        [(VMEM, delta), (VMEM, image_s)],
        [((count // 4, width), F32 if k == 0 else BF16) for k in range(4)] + [(delta.shape, BF16)],
        6,
        flops=4 * count * rows * width,
        size=count * rows,
        input_output_aliases={0: 4},
    )


def image_kernel(turned, delta, other, *outs):
    spot = lax.axis_index("grp")
    core, y, z = lax.rem(spot, 2), lax.rem(lax.div(spot, 2), 4), lax.div(spot, 8)
    for k, out in zip((2, 1, 3, 0), outs[1:] + outs[:1]):
        for flip in range(2):
            at = (z + flip - 2 * z * flip) * 4 + lax.rem(y + k, 4)
            begin = pl.multiple_of(at * LANES, LANES)
            mine = jnp.dot(
                turned[...], delta[core, :, pl.ds(begin, LANES)], preferred_element_type=F32
            )
            out[flip] = (mine + other[at].astype(F32)).astype(out.dtype)


def image_part(turned, delta, other):
    _, count, rows = delta.shape
    blocks, width, block = other.shape
    return call(
        image_kernel,
        [(VMEM, turned), (VMEM, delta), (VMEM, other)],
        [((2, width, block), F32 if k == 0 else BF16) for k in range(blocks // 2)],
        4,
        flops=2 * count * rows * width,
        size=count * rows,
    )


def total(parts):
    return functools.reduce(jnp.add, [p.astype(F32) for p in parts])


def shards(image_t, text_t, image_s, text_s):
    width_t, width_s = image_t.shape[1], image_s.shape[1]
    n = text_t.shape[0]
    cut = n // 2
    image_t = image_t.reshape(8, 2, 128, width_t)
    image_s = image_s.reshape(8, 2, 128, width_s)

    own = join(text_t, text_s)
    across = permute(own, cross_z)
    left = permute(own, along_x(1))
    right = permute(own, along_x(3))
    state = first_logits(own, image_t, image_s, 8 * n)
    across, left, right, running = lax.optimization_barrier((across, left, right, state[5]))
    state = (*state[:5], running)
    far = jnp.concatenate(
        (permute(left[:cut], along_x(1)), permute(right[cut:], along_x(3))), axis=0
    )
    across_left = permute(across, along_x(1))
    across_right = permute(across, along_x(3))
    across_far = permute(far, cross_z)
    state = more_logits([(n, across), (2 * n, left), (4 * n, right), (6 * n, far)], state)
    state = more_logits([(3 * n, across_left), (5 * n, across_right)], state)
    state = more_logits([(7 * n, across_far)], state, last=True)
    _, _, logit_t, logit_s, turned, stats = state
    stats, (logit_t, logit_s) = merge(
        [stats] + [permute(stats, m) for m in (other_core, along_y(0, 1), other_core_and_z)],
        [logit_t, logit_s],
    )
    stats = [stats] + [permute(stats, along_y(k)) for k in (2, 1, 3)]
    grad_other, delta, row_loss = delta_part(logit_t, logit_s, turned, stats)
    from_core = permute(grad_other, other_core)
    kept_text, *away_text, delta = text_part(delta, image_s)
    kept_image, *away_image = image_part(turned, delta, from_core)
    *away_text, _ = lax.optimization_barrier((*away_text, away_image[0]))
    image_terms = [kept_image] + [permute(v, along_y(k)) for v, k in zip(away_image, (2, 1, 3))]
    text_terms = [kept_text] + [permute(v, along_x(k)) for v, k in zip(away_text, (2, 3, 1))]
    image_sum = total(image_terms)
    from_z = permute(image_sum[1].astype(BF16), along_y(0, 1))
    grad_image = (image_sum[0] + from_z.astype(F32)).T.astype(BF16)
    text_sum = total(text_terms)
    from_across = permute(text_sum[n:].astype(BF16), cross_z)
    grad_text = (text_sum[:n] + from_across.astype(F32)).astype(BF16)
    return row_loss.reshape(-1), grad_image, grad_text


def solution(mesh):
    in_specs = (P("blk", None), P(AXES, None), P("blk", None), P(AXES, None))
    out_specs = (P("blk"), P(AXES, None), P(AXES, None))
    return jax.shard_map(shards, mesh=mesh, in_specs=in_specs, out_specs=out_specs, check_vma=False)
```

time: 363 us -> 96.2 us (0.27)
  waiting for transfers between devices: 194 us -> 32.6 us
  blocking collectives: 110 us -> 0 us
  starting transfers between devices: 0.12 us -> 35.3 us
  matrix products: 28.3 us -> 0 us
  Pallas kernels: 0 us -> 24.7 us
  other arithmetic: 14.6 us -> 0.95 us
  between operations: 13.8 us -> 0.82 us
    reduce_scatter x2 -> x0, waiting for transfers between devices: 128 us -> none  [the longest x1 65.5 us: shards(): lax.psum_scatter(image_term.astype(jnp.bfloat16), 'grp', scatter_dimensio...]
    all_gather x1 -> x0, waiting for transfers between devices: 66.7 us -> none  [shards(): gathered = lax.all_gather(joined, 'blk', axis=0, tiled=True)]
    pmax x2 -> x0, blocking collectives: 57.1 us -> none  [shards(): top_t, top_s = lax.pmax((local_t, local_s), 'grp')]
    psum x1 -> x0, blocking collectives: 52.9 us -> none  [shards(): lax.psum((jnp.sum(exp_t, axis=1), jnp.sum(exp_s, axis=1), jnp.sum(exp_t *...]
    ppermute x0 -> x23, starting transfers between devices: none -> 35.3 us  [permute(): lax.ppermute(v, AXES, [(i, index(*move(*place(i)))) for i in range(128)])]
    ppermute x0 -> x23, waiting for transfers between devices: none -> 32.6 us  [permute(): lax.ppermute(v, AXES, [(i, index(*move(*place(i)))) for i in range(128)])]
    dot_general x4 -> x0, matrix products: 28.3 us -> none  [the longest x1 10.6 us: shards(): jnp.einsum('rd,cd->rc', image_teacher, gathered[:, :width_t], preferred_e...]
    pallas_call x0 -> x9, Pallas kernels: none -> 24.7 us  [call(): pl.pallas_call(body, in_specs=specs, out_specs=[pl.BlockSpec(memory_space...]
  transfers between devices with their start and end apart: 3 -> 23, of which waited for: 3 -> 14; matrix products, arithmetic and copies ran while one was open for 2% -> 2% of each run, Pallas kernels for 0% -> 17%
where the time goes in v2:
time: 96.2 us; the launch traced here: 95.9 us
  starting transfers between devices  35.3 us (37%)
  waiting for transfers between devices  32.6 us (34%)
  Pallas kernels  24.7 us (26%)
  local copies, waits for them, and re-layouts  1.46 us (2%)
    ppermute x23, starting transfers between devices, permute(): lax.ppermute(v, AXES, [(i, index(*move(*place(i)))) for i in range(128)])  35.3 us
    ppermute x23, waiting for transfers between devices, permute(): lax.ppermute(v, AXES, [(i, index(*move(*place(i)))) for i in range(128)])  32.6 us
    pallas_call x9, Pallas kernels, call(): pl.pallas_call(body, in_specs=specs, out_specs=[pl.BlockSpec(memory_space...  24.7 us
  transfers between devices with their start and end apart: 23, of which 14 were waited for; matrix products, arithmetic and copies ran while one was open for 2% of the time, Pallas kernels for 17%

profile of v2, /device:TPU:0, one launch (start us, length us, event | category | flops | bytes accessed | tf_op | source)
XLA Modules:
  0.0 95.9 jit_solution(3429936250510830410)
XLA Ops:
  0.6 1.0 %shard_map.67.own = bf16[128,1536]{1,0:T(8,128)(2,1)S(1)} custom-call(bf16[128,1024]{1,0:T(8,128)(2,1)} %text_t.1, bf16[128,512]{1,0:T(8,128)(2,1)} %text_s.1), custom_call_target="tpu_custom_call" | custom-call | tf_op jit(solution)/shard_map/pallas_call | solution.py:64
  1.6 2.9 %collective-permute-start.2 = (bf16[128,1536]{1,0:T(8,128)(2,1)S(1)}, bf16[128,1536]{1,0:T(8,128)(2,1)S(1)}, u32[]{:S(2)}, u32[]{:S(2)}) collective-permute-start(bf16[128,1536]{1,0:T(8,128)(2,1)S(1)} %shard_map.67.own), channel_id=1, source_target_pairs={{0,48},{1,49},{2,50},{3,51},{4,52},{5,53},{6,54},{7,55},{8,56},{9,... | collective-permute-start | bytes 1179656 | tf_op jit(solution)/shard_map/ppermute | solution.py:35
  4.6 4.0 %collective-permute-start = (bf16[128,1536]{1,0:T(8,128)(2,1)S(1)}, bf16[128,1536]{1,0:T(8,128)(2,1)S(1)}, u32[]{:S(2)}, u32[]{:S(2)}) collective-permute-start(bf16[128,1536]{1,0:T(8,128)(2,1)S(1)} %shard_map.67.own), channel_id=1, source_target_pairs={{0,72},{1,73},{2,74},{3,75},{4,76},{5,77},{6,78},{7,79},{8,64},{9,... | collective-permute-start | bytes 1179656 | tf_op jit(solution)/shard_map/ppermute | solution.py:35
  8.6 4.4 %shard_map.68 = (bf16[1024,2048]{1,0:T(8,128)(2,1)S(1)}, bf16[512,2048]{1,0:T(8,128)(2,1)S(1)}, f32[1024,2048]{1,0:T(8,128)S(1)}, f32[1024,2048]{1,0:T(8,128)S(1...) custom-call(bf16[128,1536]{1,0:T(8,128)(2,1)S(1)} %shard_map.67.own, bf16[8,2,128,1024]{3,2,1,0:T(8,128)(2,1)} %bitcast.18, ...), custom_call_target="tpu_custom_call" | custom-call | flops 805306368 | bytes 6291456 | tf_op jit(solution)/shard_map/pallas_call | solution.py:64
  13.0 3.4 %collective-permute-done.1.refs_1_ = bf16[128,1536]{1,0:T(8,128)(2,1)S(1)} collective-permute-done((bf16[128,1536]{1,0:T(8,128)(2,1)S(1)}, bf16[128,1536]{1,0:T(8,128)(2,1)S(1)}, u32[]{:S(2)}, u32[]{:S(2)}) %collective-permute-start.1) | collective-permute-done | bytes 393248 | tf_op jit(solution)/shard_map/ppermute | solution.py:35
  16.3 1.1 %collective-permute-done.refs_0_ = bf16[128,1536]{1,0:T(8,128)(2,1)S(1)} collective-permute-done((bf16[128,1536]{1,0:T(8,128)(2,1)S(1)}, bf16[128,1536]{1,0:T(8,128)(2,1)S(1)}, u32[]{:S(2)}, u32[]{:S(2)}) %collective-permute-start) | collective-permute-done | bytes 393248 | tf_op jit(solution)/shard_map/ppermute | solution.py:35
  18.0 2.8 %collective-permute-start.7 = (bf16[128,1536]{1,0:T(8,128)(2,1)S(1)}, bf16[128,1536]{1,0:T(8,128)(2,1)S(1)}, u32[]{:S(2)}, u32[]{:S(2)}) collective-permute-start(bf16[128,1536]{1,0:T(8,128)(2,1)S(1)} %collective-permute-done.refs_0_), channel_id=1, source_target_pairs={{0,48},{1,49},{2,50},{3,51},{4,52},{5,53},{6,54},{7,55},{8,56},{9,... | collective-permute-start | bytes 1179656 | tf_op jit(solution)/shard_map/ppermute | solution.py:35
  20.8 3.3 %collective-permute-start.4 = (bf16[64,1536]{1,0:T(8,128)(2,1)S(1)}, bf16[64,1536]{1,0:T(8,128)(2,1)S(1)}, u32[]{:S(2)}, u32[]{:S(2)}) collective-permute-start(bf16[64,1536]{1,0:T(8,128)(2,1)S(1)} %slice.21), channel_id=1, source_target_pairs={{0,48},{1,49},{2,50},{3,51},{4,52},{5,53},{6,54},{7,55},{8,56},{9,... | collective-permute-start | bytes 589832 | tf_op jit(solution)/shard_map/ppermute | solution.py:35
  24.1 2.0 %collective-permute-done.3 = bf16[64,1536]{1,0:T(8,128)(2,1)S(1)} collective-permute-done((bf16[64,1536]{1,0:T(8,128)(2,1)S(1)}, bf16[64,1536]{1,0:T(8,128)(2,1)S(1)}, u32[]{:S(2)}, u32[]{:S(2)}) %collective-permute-start.3) | collective-permute-done | bytes 196640 | tf_op jit(solution)/shard_map/ppermute | solution.py:35
  26.1 6.1 %collective-permute-done.4 = bf16[64,1536]{1,0:T(8,128)(2,1)S(1)} collective-permute-done((bf16[64,1536]{1,0:T(8,128)(2,1)S(1)}, bf16[64,1536]{1,0:T(8,128)(2,1)S(1)}, u32[]{:S(2)}, u32[]{:S(2)}) %collective-permute-start.4) | collective-permute-done | bytes 196640 | tf_op jit(solution)/shard_map/ppermute | solution.py:35
  32.2 2.9 %collective-permute-start.5 = (bf16[128,1536]{1,0:T(8,128)(2,1)S(1)}, bf16[128,1536]{1,0:T(8,128)(2,1)S(1)}, u32[]{:S(2)}, u32[]{:S(2)}) collective-permute-start(bf16[128,1536]{1,0:T(8,128)(2,1)S(1)} %constant_dynamic-update-slice_fusion.refs_3_), channel_id=1, source_target_pairs={{0,72},{1,73},{2,74},{3,75},{4,76},{5,77},{6,78},{7,79},{8,64},{9,... | collective-permute-start | bytes 1179656 | tf_op jit(solution)/shard_map/ppermute | solution.py:35
  35.1 6.4 %shard_map.69 = (f32[1024,2048]{1,0:T(8,128)S(1)}, f32[1024,2048]{1,0:T(8,128)S(1)}, bf16[512,1024]{1,0:T(8,128)(2,1)S(1)}, f32[8,2048]{1,0:T(8,128)S(1)}) custom-call(bf16[128,1536]{1,0:T(8,128)(2,1)S(1)} %collective-permute-done.refs_0_, ...), custom_call_target="tpu_custom_call", output_to_operand_aliasing={{0}: (6, {}), {1}: (7, {}), {2}: (8, {})} | custom-call | flops 3221225472 | bytes 2097152 | tf_op jit(solution)/shard_map/pallas_call | solution.py:64
  41.6 3.3 %shard_map.70 = (f32[1024,2048]{1,0:T(8,128)S(1)}, f32[1024,2048]{1,0:T(8,128)S(1)}, bf16[512,1024]{1,0:T(8,128)(2,1)S(1)}, f32[8,2048]{1,0:T(8,128)S(1)}) custom-call(bf16[128,1536]{1,0:T(8,128)(2,1)S(1)} %collective-permute-done.6.refs_0_, ...), custom_call_target="tpu_custom_call", output_to_operand_aliasing={{0}: (4, {}), {1}: (5, {}), {2}: (6, {})} | custom-call | flops 1610612736 | bytes 1048576 | tf_op jit(solution)/shard_map/pallas_call | solution.py:64
  44.9 1.6 %shard_map.71 = (f32[1024,2048]{1,0:T(8,128)S(1)}, f32[1024,2048]{1,0:T(8,128)S(1)}, bf16[512,1024]{1,0:T(8,128)(2,1)S(1)}, f32[48,128]{1,0:T(8,128)S(1)}) custom-call(bf16[128,1536]{1,0:T(8,128)(2,1)S(1)} %collective-permute-done.5.refs_0_, ...), custom_call_target="tpu_custom_call", output_to_operand_aliasing={{0}: (3, {}), {1}: (4, {}), {2}: (5, {})} | custom-call | flops 805306368 | bytes 524288 | tf_op jit(solution)/shard_map/pallas_call | solution.py:64
  46.7 1.8 %collective-permute-start.8 = (f32[48,128]{1,0:T(8,128)S(1)}, f32[48,128]{1,0:T(8,128)S(1)}, u32[]{:S(2)}, u32[]{:S(2)}) collective-permute-start(f32[48,128]{1,0:T(8,128)S(1)} %get-tuple-element.61.a), channel_id=1, source_target_pairs={{0,1},{1,0},{2,3},{3,2},{4,5},{5,4},{6,7},{7,6},{8,9},{9,8},{10,11... | collective-permute-start | bytes 73736 | tf_op jit(solution)/shard_map/ppermute | solution.py:35
  48.4 1.4 %collective-permute-done.10.d = f32[48,128]{1,0:T(8,128)S(1)} collective-permute-done((f32[48,128]{1,0:T(8,128)S(1)}, f32[48,128]{1,0:T(8,128)S(1)}, u32[]{:S(2)}, u32[]{:S(2)}) %collective-permute-start.10) | collective-permute-done | bytes 24608 | tf_op jit(solution)/shard_map/ppermute | solution.py:35
  50.5 3.1 %collective-permute-start.13 = (f32[48,128]{1,0:T(8,128)S(1)}, f32[48,128]{1,0:T(8,128)S(1)}, u32[]{:S(2)}, u32[]{:S(2)}) collective-permute-start(f32[48,128]{1,0:T(8,128)S(1)} %get-tuple-element.67.a), channel_id=1, source_target_pairs={{0,6},{1,7},{2,0},{3,1},{4,2},{5,3},{6,4},{7,5},{8,14},{9,15},{10,... | collective-permute-start | bytes 73736 | tf_op jit(solution)/shard_map/ppermute | solution.py:35
  53.6 2.2 %collective-permute-start.11 = (f32[48,128]{1,0:T(8,128)S(1)}, f32[48,128]{1,0:T(8,128)S(1)}, u32[]{:S(2)}, u32[]{:S(2)}) collective-permute-start(f32[48,128]{1,0:T(8,128)S(1)} %get-tuple-element.67.a), channel_id=1, source_target_pairs={{0,4},{1,5},{2,6},{3,7},{4,0},{5,1},{6,2},{7,3},{8,12},{9,13},{10,... | collective-permute-start | bytes 73736 | tf_op jit(solution)/shard_map/ppermute | solution.py:35
  55.8 2.8 %collective-permute-done.12.c = f32[48,128]{1,0:T(8,128)S(1)} collective-permute-done((f32[48,128]{1,0:T(8,128)S(1)}, f32[48,128]{1,0:T(8,128)S(1)}, u32[]{:S(2)}, u32[]{:S(2)}) %collective-permute-start.12) | collective-permute-done | bytes 24608 | tf_op jit(solution)/shard_map/ppermute | solution.py:35
  58.9 3.3 %shard_map.73 = (bf16[8,512,128]{2,1,0:T(8,128)(2,1)S(1)}, bf16[2,1024,1024]{2,1,0:T(8,128)(2,1)S(1)}, f32[16,128]{1,0:T(8,128)S(1)}) custom-call(f32[1024,2048]{1,0:T(8,128)S(1)} %get-tuple-element.64.logit_t, f32[1024,2048]{1,0:T(8,128)S(1)} %get-tuple-element.65.logit_s, bf16[512,1024]{1,0:T(8,128)(2,1)S(1)} %get-tuple-element.66.turned, ...), custom_call_target="tpu_custom_call" | custom-call | flops 1073741824 | bytes 4194304 | tf_op jit(solution)/shard_map/pallas_call | solution.py:64
  62.4 2.3 %shard_map.74 = (f32[256,512]{1,0:T(8,128)S(1)}, bf16[256,512]{1,0:T(8,128)(2,1)S(1)}, bf16[256,512]{1,0:T(8,128)(2,1)S(1)}, bf16[256,512]{1,0:T(8,128)(2,1)S(1)}, bf16[2,1024,1024]{2,1,0:T(8,128)(2,1)S(1)}) custom-call(bf16[2,1024,1024]{2,1,0:T(8,128)(2,1)S(1)} %get-tuple-element.69.delta, ...), custom_call_target="tpu_custom_call", output_to_operand_aliasing={{4}: (0, {})} | custom-call | flops 2147483648 | bytes 1048576 | tf_op jit(solution)/shard_map/pallas_call | solution.py:64
  65.0 2.4 %shard_map.75 = (f32[2,512,128]{2,1,0:T(8,128)S(1)}, bf16[2,512,128]{2,1,0:T(8,128)(2,1)S(1)}, bf16[2,512,128]{2,1,0:T(8,128)(2,1)S(1)}, bf16[2,512,128]{2,1,0:T(8,128)(2,1)S(1)}) custom-call(bf16[512,1024]{1,0:T(8,128)(2,1)S(1)} %get-tuple-element.66.turned, bf16[2,1024,1024]{2,1,0:T(8,128)(2,1)S(1)} %get-tuple-element.70.delta, ...), custom_call_target="tpu_custom_call" | custom-call | flops 1073741824 | bytes 1048576 | tf_op jit(solution)/shard_map/pallas_call | solution.py:64
  68.0 2.7 %collective-permute-start.17 = (bf16[2,512,128]{2,1,0:T(8,128)(2,1)S(1)}, bf16[2,512,128]{2,1,0:T(8,128)(2,1)S(1)}, u32[]{:S(2)}, u32[]{:S(2)}) collective-permute-start(bf16[2,512,128]{2,1,0:T(8,128)(2,1)S(1)} %get-tuple-element.75), channel_id=1, source_target_pairs={{0,6},{1,7},{2,0},{3,1},{4,2},{5,3},{6,4},{7,5},{8,14},{9,15},{10,... | collective-permute-start | bytes 786440 | tf_op jit(solution)/shard_map/ppermute | solution.py:35
  70.8 1.4 %collective-permute-start.15 = (bf16[2,512,128]{2,1,0:T(8,128)(2,1)S(1)}, bf16[2,512,128]{2,1,0:T(8,128)(2,1)S(1)}, u32[]{:S(2)}, u32[]{:S(2)}) collective-permute-start(bf16[2,512,128]{2,1,0:T(8,128)(2,1)S(1)} %get-tuple-element.73), channel_id=1, source_target_pairs={{0,4},{1,5},{2,6},{3,7},{4,0},{5,1},{6,2},{7,3},{8,12},{9,13},{10,... | collective-permute-start | bytes 786440 | tf_op jit(solution)/shard_map/ppermute | solution.py:35
  72.8 3.4 %collective-permute-start.19 = (bf16[256,512]{1,0:T(8,128)(2,1)S(1)}, bf16[256,512]{1,0:T(8,128)(2,1)S(1)}, u32[]{:S(2)}, u32[]{:S(2)}) collective-permute-start(bf16[256,512]{1,0:T(8,128)(2,1)S(1)} %get-tuple-element.80), channel_id=1, source_target_pairs={{0,32},{1,33},{2,34},{3,35},{4,36},{5,37},{6,38},{7,39},{8,40},{9,... | collective-permute-start | bytes 786440 | tf_op jit(solution)/shard_map/ppermute | solution.py:35
  76.1 0.9 collective-permute-start.20
  77.4 1.6 %collective-permute-start.21 = (bf16[256,512]{1,0:T(8,128)(2,1)S(1)}, bf16[256,512]{1,0:T(8,128)(2,1)S(1)}, u32[]{:S(2)}, u32[]{:S(2)}) collective-permute-start(bf16[256,512]{1,0:T(8,128)(2,1)S(1)} %get-tuple-element.82), channel_id=1, source_target_pairs={{0,16},{1,17},{2,18},{3,19},{4,20},{5,21},{6,22},{7,23},{8,24},{9,... | collective-permute-start | bytes 786440 | tf_op jit(solution)/shard_map/ppermute | solution.py:35
  78.9 3.4 %collective-permute-done.17 = bf16[2,512,128]{2,1,0:T(8,128)(2,1)S(1)} collective-permute-done((bf16[2,512,128]{2,1,0:T(8,128)(2,1)S(1)}, bf16[2,512,128]{2,1,0:T(8,128)(2,1)S(1)}, u32[]{:S(2)}, u32[]{:S(2)}) %collective-permute-start.17) | collective-permute-done | bytes 262176 | tf_op jit(solution)/shard_map/ppermute | solution.py:35
  82.3 1.8 %collective-permute-done.15 = bf16[2,512,128]{2,1,0:T(8,128)(2,1)S(1)} collective-permute-done((bf16[2,512,128]{2,1,0:T(8,128)(2,1)S(1)}, bf16[2,512,128]{2,1,0:T(8,128)(2,1)S(1)}, u32[]{:S(2)}, u32[]{:S(2)}) %collective-permute-start.15) | collective-permute-done | bytes 262176 | tf_op jit(solution)/shard_map/ppermute | solution.py:35
  84.6 4.2 %collective-permute-done.20 = bf16[256,512]{1,0:T(8,128)(2,1)S(1)} collective-permute-done((bf16[256,512]{1,0:T(8,128)(2,1)S(1)}, bf16[256,512]{1,0:T(8,128)(2,1)S(1)}, u32[]{:S(2)}, u32[]{:S(2)}) %collective-permute-start.20) | collective-permute-done | bytes 262176 | tf_op jit(solution)/shard_map/ppermute | solution.py:35
  89.7 0.8 copy.19
  90.5 4.8 %collective-permute-done.22 = bf16[128,512]{1,0:T(8,128)(2,1)S(1)} collective-permute-done((bf16[128,512]{1,0:T(8,128)(2,1)S(1)}, bf16[128,512]{1,0:T(8,128)(2,1)S(1)}, u32[]{:S(2)}, u32[]{:S(2)}) %collective-permute-start.22) | collective-permute-done | bytes 131104 | tf_op jit(solution)/shard_map/ppermute | solution.py:35
  (37 shorter events, 5.8 us)
Async XLA Ops:
  1.6 11.3 %collective-permute-start.2 = (bf16[128,1536]{1,0:T(8,128)(2,1)S(1)}, bf16[128,1536]{1,0:T(8,128)(2,1)S(1)}, u32[]{:S(2)}, u32[]{:S(2)}) collective-permute-start(bf16[128,1536]{1,0:T(8,128)(2,1)S(1)} %shard_map.67.own), channel_id=1, source_target_pairs={{0,48},{1,49},{2,50},{3,51},{4,52},{5,53},{6,54},{7,55},{8,56},{9,... | collective-permute-start | bytes 1179656 | tf_op jit(solution)/shard_map/ppermute | solution.py:35
  4.6 11.8 %collective-permute-start.1 = (bf16[128,1536]{1,0:T(8,128)(2,1)S(1)}, bf16[128,1536]{1,0:T(8,128)(2,1)S(1)}, u32[]{:S(2)}, u32[]{:S(2)}) collective-permute-start(bf16[128,1536]{1,0:T(8,128)(2,1)S(1)} %shard_map.67.own), channel_id=1, source_target_pairs={{0,16},{1,17},{2,18},{3,19},{4,20},{5,21},{6,22},{7,23},{8,24},{9,... | collective-permute-start | bytes 1179656 | tf_op jit(solution)/shard_map/ppermute | solution.py:35
  4.6 12.9 %collective-permute-start = (bf16[128,1536]{1,0:T(8,128)(2,1)S(1)}, bf16[128,1536]{1,0:T(8,128)(2,1)S(1)}, u32[]{:S(2)}, u32[]{:S(2)}) collective-permute-start(bf16[128,1536]{1,0:T(8,128)(2,1)S(1)} %shard_map.67.own), channel_id=1, source_target_pairs={{0,72},{1,73},{2,74},{3,75},{4,76},{5,77},{6,78},{7,79},{8,64},{9,... | collective-permute-start | bytes 1179656 | tf_op jit(solution)/shard_map/ppermute | solution.py:35
  17.4 8.6 %collective-permute-start.3 = (bf16[64,1536]{1,0:T(8,128)(2,1)S(1)}, bf16[64,1536]{1,0:T(8,128)(2,1)S(1)}, u32[]{:S(2)}, u32[]{:S(2)}) collective-permute-start(bf16[64,1536]{1,0:T(8,128)(2,1)S(1)} %slice.20), channel_id=1, source_target_pairs={{0,16},{1,17},{2,18},{3,19},{4,20},{5,21},{6,22},{7,23},{8,24},{9,... | collective-permute-start | bytes 589832 | tf_op jit(solution)/shard_map/ppermute | solution.py:35
  18.0 23.6 %collective-permute-start.7 = (bf16[128,1536]{1,0:T(8,128)(2,1)S(1)}, bf16[128,1536]{1,0:T(8,128)(2,1)S(1)}, u32[]{:S(2)}, u32[]{:S(2)}) collective-permute-start(bf16[128,1536]{1,0:T(8,128)(2,1)S(1)} %collective-permute-done.refs_0_), channel_id=1, source_target_pairs={{0,48},{1,49},{2,50},{3,51},{4,52},{5,53},{6,54},{7,55},{8,56},{9,... | collective-permute-start | bytes 1179656 | tf_op jit(solution)/shard_map/ppermute | solution.py:35
  20.7 20.8 %collective-permute-start.6 = (bf16[128,1536]{1,0:T(8,128)(2,1)S(1)}, bf16[128,1536]{1,0:T(8,128)(2,1)S(1)}, u32[]{:S(2)}, u32[]{:S(2)}) collective-permute-start(bf16[128,1536]{1,0:T(8,128)(2,1)S(1)} %collective-permute-done.refs_0_), channel_id=1, source_target_pairs={{0,16},{1,17},{2,18},{3,19},{4,20},{5,21},{6,22},{7,23},{8,24},{9,... | collective-permute-start | bytes 1179656 | tf_op jit(solution)/shard_map/ppermute | solution.py:35
  20.8 11.4 %collective-permute-start.4 = (bf16[64,1536]{1,0:T(8,128)(2,1)S(1)}, bf16[64,1536]{1,0:T(8,128)(2,1)S(1)}, u32[]{:S(2)}, u32[]{:S(2)}) collective-permute-start(bf16[64,1536]{1,0:T(8,128)(2,1)S(1)} %slice.21), channel_id=1, source_target_pairs={{0,48},{1,49},{2,50},{3,51},{4,52},{5,53},{6,54},{7,55},{8,56},{9,... | collective-permute-start | bytes 589832 | tf_op jit(solution)/shard_map/ppermute | solution.py:35
  32.2 12.7 %collective-permute-start.5 = (bf16[128,1536]{1,0:T(8,128)(2,1)S(1)}, bf16[128,1536]{1,0:T(8,128)(2,1)S(1)}, u32[]{:S(2)}, u32[]{:S(2)}) collective-permute-start(bf16[128,1536]{1,0:T(8,128)(2,1)S(1)} %constant_dynamic-update-slice_fusion.refs_3_), channel_id=1, source_target_pairs={{0,72},{1,73},{2,74},{3,75},{4,76},{5,77},{6,78},{7,79},{8,64},{9,... | collective-permute-start | bytes 1179656 | tf_op jit(solution)/shard_map/ppermute | solution.py:35
  46.5 3.3 %collective-permute-start.10 = (f32[48,128]{1,0:T(8,128)S(1)}, f32[48,128]{1,0:T(8,128)S(1)}, u32[]{:S(2)}, u32[]{:S(2)}) collective-permute-start(f32[48,128]{1,0:T(8,128)S(1)} %get-tuple-element.61.a), channel_id=1, source_target_pairs={{0,9},{1,8},{2,11},{3,10},{4,13},{5,12},{6,15},{7,14},{8,1},{9,0},... | collective-permute-start | bytes 73736 | tf_op jit(solution)/shard_map/ppermute | solution.py:35
  46.6 3.9 %collective-permute-start.9 = (f32[48,128]{1,0:T(8,128)S(1)}, f32[48,128]{1,0:T(8,128)S(1)}, u32[]{:S(2)}, u32[]{:S(2)}) collective-permute-start(f32[48,128]{1,0:T(8,128)S(1)} %get-tuple-element.61.a), channel_id=1, source_target_pairs={{0,8},{1,9},{2,10},{3,11},{4,12},{5,13},{6,14},{7,15},{8,0},{9,1},... | collective-permute-start | bytes 73736 | tf_op jit(solution)/shard_map/ppermute | solution.py:35
  46.7 3.8 %collective-permute-start.8 = (f32[48,128]{1,0:T(8,128)S(1)}, f32[48,128]{1,0:T(8,128)S(1)}, u32[]{:S(2)}, u32[]{:S(2)}) collective-permute-start(f32[48,128]{1,0:T(8,128)S(1)} %get-tuple-element.61.a), channel_id=1, source_target_pairs={{0,1},{1,0},{2,3},{3,2},{4,5},{5,4},{6,7},{7,6},{8,9},{9,8},{10,11... | collective-permute-start | bytes 73736 | tf_op jit(solution)/shard_map/ppermute | solution.py:35
  50.5 5.3 %collective-permute-start.13 = (f32[48,128]{1,0:T(8,128)S(1)}, f32[48,128]{1,0:T(8,128)S(1)}, u32[]{:S(2)}, u32[]{:S(2)}) collective-permute-start(f32[48,128]{1,0:T(8,128)S(1)} %get-tuple-element.67.a), channel_id=1, source_target_pairs={{0,6},{1,7},{2,0},{3,1},{4,2},{5,3},{6,4},{7,5},{8,14},{9,15},{10,... | collective-permute-start | bytes 73736 | tf_op jit(solution)/shard_map/ppermute | solution.py:35
  53.6 5.0 %collective-permute-start.12 = (f32[48,128]{1,0:T(8,128)S(1)}, f32[48,128]{1,0:T(8,128)S(1)}, u32[]{:S(2)}, u32[]{:S(2)}) collective-permute-start(f32[48,128]{1,0:T(8,128)S(1)} %get-tuple-element.67.a), channel_id=1, source_target_pairs={{0,2},{1,3},{2,4},{3,5},{4,6},{5,7},{6,0},{7,1},{8,10},{9,11},{10,... | collective-permute-start | bytes 73736 | tf_op jit(solution)/shard_map/ppermute | solution.py:35
  53.6 5.3 %collective-permute-start.11 = (f32[48,128]{1,0:T(8,128)S(1)}, f32[48,128]{1,0:T(8,128)S(1)}, u32[]{:S(2)}, u32[]{:S(2)}) collective-permute-start(f32[48,128]{1,0:T(8,128)S(1)} %get-tuple-element.67.a), channel_id=1, source_target_pairs={{0,4},{1,5},{2,6},{3,7},{4,0},{5,1},{6,2},{7,3},{8,12},{9,13},{10,... | collective-permute-start | bytes 73736 | tf_op jit(solution)/shard_map/ppermute | solution.py:35
  58.9 3.4 %copy-start = (bf16[2048,512]{1,0:T(8,128)(2,1)S(1)}, bf16[2048,512]{1,0:T(8,128)(2,1)}, u32[]{:S(2)}) copy-start(bf16[2048,512]{1,0:T(8,128)(2,1)} %param.6) | copy-start | bytes 6291460
  62.3 2.7 %collective-permute-start.14 = (bf16[8,512,128]{2,1,0:T(8,128)(2,1)S(1)}, bf16[8,512,128]{2,1,0:T(8,128)(2,1)S(1)}, u32[]{:S(2)}, u32[]{:S(2)}) collective-permute-start(bf16[8,512,128]{2,1,0:T(8,128)(2,1)S(1)} %get-tuple-element.71), channel_id=1, source_target_pairs={{0,1},{1,0},{2,3},{3,2},{4,5},{5,4},{6,7},{7,6},{8,9},{9,8},{10,11... | collective-permute-start | bytes 3145736 | tf_op jit(solution)/shard_map/ppermute | solution.py:35
  67.4 10.0 %collective-permute-start.16 = (bf16[2,512,128]{2,1,0:T(8,128)(2,1)S(1)}, bf16[2,512,128]{2,1,0:T(8,128)(2,1)S(1)}, u32[]{:S(2)}, u32[]{:S(2)}) collective-permute-start(bf16[2,512,128]{2,1,0:T(8,128)(2,1)S(1)} %get-tuple-element.74), channel_id=1, source_target_pairs={{0,2},{1,3},{2,4},{3,5},{4,6},{5,7},{6,0},{7,1},{8,10},{9,11},{10,... | collective-permute-start | bytes 786440 | tf_op jit(solution)/shard_map/ppermute | solution.py:35
  68.0 14.3 %collective-permute-start.17 = (bf16[2,512,128]{2,1,0:T(8,128)(2,1)S(1)}, bf16[2,512,128]{2,1,0:T(8,128)(2,1)S(1)}, u32[]{:S(2)}, u32[]{:S(2)}) collective-permute-start(bf16[2,512,128]{2,1,0:T(8,128)(2,1)S(1)} %get-tuple-element.75), channel_id=1, source_target_pairs={{0,6},{1,7},{2,0},{3,1},{4,2},{5,3},{6,4},{7,5},{8,14},{9,15},{10,... | collective-permute-start | bytes 786440 | tf_op jit(solution)/shard_map/ppermute | solution.py:35
  70.8 13.4 %collective-permute-start.15 = (bf16[2,512,128]{2,1,0:T(8,128)(2,1)S(1)}, bf16[2,512,128]{2,1,0:T(8,128)(2,1)S(1)}, u32[]{:S(2)}, u32[]{:S(2)}) collective-permute-start(bf16[2,512,128]{2,1,0:T(8,128)(2,1)S(1)} %get-tuple-element.73), channel_id=1, source_target_pairs={{0,4},{1,5},{2,6},{3,7},{4,0},{5,1},{6,2},{7,3},{8,12},{9,13},{10,... | collective-permute-start | bytes 786440 | tf_op jit(solution)/shard_map/ppermute | solution.py:35
  72.8 11.8 %collective-permute-start.19 = (bf16[256,512]{1,0:T(8,128)(2,1)S(1)}, bf16[256,512]{1,0:T(8,128)(2,1)S(1)}, u32[]{:S(2)}, u32[]{:S(2)}) collective-permute-start(bf16[256,512]{1,0:T(8,128)(2,1)S(1)} %get-tuple-element.80), channel_id=1, source_target_pairs={{0,32},{1,33},{2,34},{3,35},{4,36},{5,37},{6,38},{7,39},{8,40},{9,... | collective-permute-start | bytes 786440 | tf_op jit(solution)/shard_map/ppermute | solution.py:35
  76.1 12.7 %collective-permute-start.20 = (bf16[256,512]{1,0:T(8,128)(2,1)S(1)}, bf16[256,512]{1,0:T(8,128)(2,1)S(1)}, u32[]{:S(2)}, u32[]{:S(2)}) collective-permute-start(bf16[256,512]{1,0:T(8,128)(2,1)S(1)} %get-tuple-element.81), channel_id=1, source_target_pairs={{0,48},{1,49},{2,50},{3,51},{4,52},{5,53},{6,54},{7,55},{8,56},{9,... | collective-permute-start | bytes 786440 | tf_op jit(solution)/shard_map/ppermute | solution.py:35
  77.4 11.4 %collective-permute-start.21 = (bf16[256,512]{1,0:T(8,128)(2,1)S(1)}, bf16[256,512]{1,0:T(8,128)(2,1)S(1)}, u32[]{:S(2)}, u32[]{:S(2)}) collective-permute-start(bf16[256,512]{1,0:T(8,128)(2,1)S(1)} %get-tuple-element.82), channel_id=1, source_target_pairs={{0,16},{1,17},{2,18},{3,19},{4,20},{5,21},{6,22},{7,23},{8,24},{9,... | collective-permute-start | bytes 786440 | tf_op jit(solution)/shard_map/ppermute | solution.py:35
  84.3 5.4 %collective-permute-start.18 = (bf16[512,128]{1,0:T(8,128)(2,1)S(1)}, bf16[512,128]{1,0:T(8,128)(2,1)S(1)}, u32[]{:S(2)}, u32[]{:S(2)}) collective-permute-start(bf16[512,128]{1,0:T(8,128)(2,1)S(1)} %fusion.4), channel_id=1, source_target_pairs={{0,8},{1,9},{2,10},{3,11},{4,12},{5,13},{6,14},{7,15},{8,0},{9,1},... | collective-permute-start | bytes 393224 | tf_op jit(solution)/shard_map/ppermute | solution.py:35
  88.9 6.3 %collective-permute-start.22 = (bf16[128,512]{1,0:T(8,128)(2,1)S(1)}, bf16[128,512]{1,0:T(8,128)(2,1)S(1)}, u32[]{:S(2)}, u32[]{:S(2)}) collective-permute-start(bf16[128,512]{1,0:T(8,128)(2,1)S(1)} %slice.44), channel_id=1, source_target_pairs={{0,72},{1,73},{2,74},{3,75},{4,76},{5,77},{6,78},{7,79},{8,64},{9,... | collective-permute-start | bytes 393224 | tf_op jit(solution)/shard_map/ppermute | solution.py:35

commit v3 on v2

--- a/solution.py
+++ b/solution.py
@@ -16,7 +16,7 @@
 BF16 = jnp.bfloat16
 VMEM = pltpu.VMEM
 LANES = 128
-WIDE = 256
+WIDE = 512
 
 
 def place(i):
@@ -99,26 +99,24 @@
     return 3.0 / math.sqrt(width_t) * LOG2E, 3.0 / math.sqrt(width_s) * LOG2E
 
 
-def tile_logits(parts, image_t, image_s, logit_t, logit_s, before, cols):
-    scale_t, scale_s = scales(image_t.shape[0], image_s.shape[0])
-    tops_t, tops_s = [], []
-    for at, text_t, text_s in parts:
-        n = text_t.shape[0]
-        t = jnp.dot(text_t, image_t[:, cols], preferred_element_type=F32) * scale_t
-        s = jnp.dot(text_s, image_s[:, cols], preferred_element_type=F32) * scale_s
-        logit_t[at : at + n, cols] = t
-        logit_s[at : at + n, cols] = s
-        tops_t.append(jnp.max(t, axis=0, keepdims=True))
-        tops_s.append(jnp.max(s, axis=0, keepdims=True))
+def tile_logits(text, spans, image_t, image_s, logit_t, logit_s, before, cols):
+    width_t = image_t.shape[0]
+    scale_t, scale_s = scales(width_t, image_s.shape[0])
+    t = jnp.dot(text[:, :width_t], image_t[:, cols], preferred_element_type=F32) * scale_t
+    s = jnp.dot(text[:, width_t:], image_s[:, cols], preferred_element_type=F32) * scale_s
+    row = 0
+    for at, n in spans:
+        logit_t[at : at + n, cols] = t[row : row + n]
+        logit_s[at : at + n, cols] = s[row : row + n]
+        row += n
+    top_t = jnp.max(t, axis=0, keepdims=True)
+    top_s = jnp.max(s, axis=0, keepdims=True)
     if before is not None:
         old_t, sum_t, old_s, sum_s, gap = (before[k : k + 1, cols] for k in range(5))
-        tops_t.append(old_t)
-        tops_s.append(old_s)
-    top_t = functools.reduce(jnp.maximum, tops_t)
-    top_s = functools.reduce(jnp.maximum, tops_s)
+        top_t = jnp.maximum(top_t, old_t)
+        top_s = jnp.maximum(top_s, old_s)
     sums = []
-    for at, text_t, _ in parts:
-        n = text_t.shape[0]
+    for at, n in spans:
         t = logit_t[at : at + n, cols]
         s = logit_s[at : at + n, cols]
         exp_t = jnp.exp2(t - top_t)
@@ -165,12 +163,10 @@
         cols = slice(k * wide, k * wide + wide)
         image_t[:, cols] = held_t[k].reshape(wide, width_t).T
         image_s[:, cols] = held_s[k].reshape(wide, width_s).T
-        parts = [(0, own[:, :width_t], own[:, width_t:])]
-        for at in range(k * wide, k * wide + wide, WIDE):
-            cols = slice(at, at + WIDE)
-            put_running(
-                stats, cols, tile_logits(parts, image_t, image_s, logit_t, logit_s, None, cols)
-            )
+        spans = [(0, own.shape[0])]
+        put_running(
+            stats, cols, tile_logits(own, spans, image_t, image_s, logit_t, logit_s, None, cols)
+        )
 
 
 def first_logits(own, image_t, image_s, texts):
@@ -205,15 +201,20 @@
 def more_kernel(places, last, *refs):
     count = len(places)
     texts = refs[:count]
-    image_t, image_s, _, _, _, before, logit_t, logit_s, turned, stats = refs[count:]
+    image_t, image_s, _, _, _, before, logit_t, logit_s, turned, stats, joined = refs[count:]
     width_t, rows = image_t.shape
+    spans = []
+    row = 0
     for at, ref in zip(places, texts):
-        turned[:, at : at + ref.shape[0]] = ref[:, width_t:].T
+        n = ref.shape[0]
+        spans.append((at, n))
+        joined[row : row + n, :] = ref[...]
+        turned[:, at : at + n] = ref[:, width_t:].T
+        row += n
     for begin in range(0, rows, WIDE):
         cols = slice(begin, begin + WIDE)
-        parts = [(at, ref[:, :width_t], ref[:, width_t:]) for at, ref in zip(places, texts)]
         top_t, sum_t, top_s, sum_s, gap = values = tile_logits(
-            parts, image_t, image_s, logit_t, logit_s, before, cols
+            joined, spans, image_t, image_s, logit_t, logit_s, before, cols
         )
         if not last:
             put_running(stats, cols, values)
@@ -237,11 +238,12 @@
         functools.partial(more_kernel, places, last),
         [(VMEM, v) for _, v in chunks] + [(VMEM, v) for v in state],
         [(logit_t.shape, F32), (logit_s.shape, F32), (turned.shape, BF16), shape],
-        4,
+        6,
         flops=2 * n * rows * (width_t + width_s),
         size=2 * n * rows,
         exps=2 * n * rows,
         input_output_aliases={count + 2: 0, count + 3: 1, count + 4: 2},
+        scratch_shapes=[pltpu.VMEM((n, width_t + width_s), BF16)],
     )
     return image_t, image_s, logit_t, logit_s, turned, stats
 
@@ -290,76 +292,60 @@
             loss[2 * j + c : 2 * j + c + 1, :] = value[at : at + 1, :]
 
 
-def delta_kernel(scale, logit_t, logit_s, turned, a, b, c, d, grad, delta, loss, lse):
+def delta_kernel(
+    scale, logit_t, logit_s, turned, image_s, a, b, c, d, other, own, far, left, right, delta, loss, lse
+):
     put_merged((a, b, c, d), lse, loss)
     away = 1 - lax.rem(lax.axis_index("grp"), 2)
-    count, rows = logit_t.shape
+    rows = logit_t.shape[1]
     half = rows // 2
-    pair = WIDE // LANES
-    for begin in range(0, rows, WIDE):
-        cols = slice(begin, begin + WIDE)
-        spots = [begin // LANES + k for k in range(pair)]
-        low_t = jnp.concatenate([lse[k : k + 1, :] for k in spots], axis=1)
-        low_s = jnp.concatenate(
-            [lse[k + rows // LANES : k + rows // LANES + 1, :] for k in spots], axis=1
-        )
-        prob_t = jnp.exp2(logit_t[:, cols] - low_t)
-        prob_s = jnp.exp2(logit_s[:, cols] - low_s)
-        delta[begin // half, :, begin % half : begin % half + WIDE] = (
-            (prob_s - prob_t) * scale
-        ).astype(BF16)
+    blocks, cores, block, width = image_s.shape
+    pieces = WIDE // LANES
+    for k, out in ((3, far), (1, left), (2, right), (0, own)):
+        n = out.shape[0]
+        span = slice(n * k, n * k + n)
+        for begin in range(0, rows, WIDE):
+            cols = slice(begin, begin + WIDE)
+            spots = [begin // LANES + j for j in range(pieces)]
+            low_t = jnp.concatenate([lse[j : j + 1, :] for j in spots], axis=1)
+            low_s = jnp.concatenate(
+                [lse[j + rows // LANES : j + rows // LANES + 1, :] for j in spots], axis=1
+            )
+            prob_t = jnp.exp2(logit_t[span, cols] - low_t)
+            prob_s = jnp.exp2(logit_s[span, cols] - low_s)
+            delta[begin // half, span, begin % half : begin % half + WIDE] = (
+                (prob_s - prob_t) * scale
+            ).astype(BF16)
+        total = 0.0
+        for core in range(cores):
+            total += jnp.dot(
+                delta[core, span, :],
+                image_s[:, core].reshape(blocks * block, width),
+                preferred_element_type=F32,
+            )
+        out[...] = total.astype(out.dtype)
     for begin in range(0, half, WIDE):
         out = jnp.dot(
             turned[...], delta[away, :, begin : begin + WIDE], preferred_element_type=F32
         ).astype(BF16)
-        for k in range(pair):
-            grad[begin // LANES + k] = out[:, k * LANES : k * LANES + LANES]
-
-
-def delta_part(logit_t, logit_s, turned, stats):
+        for j in range(pieces):
+            other[begin // LANES + j] = out[:, j * LANES : j * LANES + LANES]
+
+
+def delta_part(logit_t, logit_s, turned, image_s, stats):
     count, rows = logit_t.shape
     width = turned.shape[0]
     return call(
         functools.partial(delta_kernel, 3.0 / math.sqrt(width)),
-        [(VMEM, v) for v in (logit_t, logit_s, turned, *stats)],
-        [
-            ((rows // 2 // LANES, width, LANES), BF16),
-            ((2, count, rows // 2), BF16),
-            ((rows // LANES, LANES), F32),
-        ],
-        4,
-        flops=count * rows * width,
-        size=2 * count * rows,
+        [(VMEM, v) for v in (logit_t, logit_s, turned, image_s, *stats)],
+        [((rows // 2 // LANES, width, LANES), BF16)]
+        + [((count // 4, width), F32 if k == 0 else BF16) for k in range(4)]
+        + [((2, count, rows // 2), BF16), ((rows // LANES, LANES), F32)],
+        6,
+        flops=3 * count * rows * width,
+        size=4 * count * rows,
         exps=2 * count * rows,
         scratch_shapes=[pltpu.VMEM((2 * rows // LANES, LANES), F32)],
-    )
-
-
-def text_kernel(delta, image_s, *outs):
-    blocks, cores, block, width = image_s.shape
-    for k, out in zip((3, 1, 2, 0), outs[1:4] + outs[:1]):
-        n = out.shape[0]
-        total = 0.0
-        for c in range(cores):
-            total += jnp.dot(
-                delta[c, n * k : n * k + n, :],
-                image_s[:, c].reshape(blocks * block, width),
-                preferred_element_type=F32,
-            )
-        out[...] = total.astype(out.dtype)
-
-
-def text_part(delta, image_s):
-    _, count, rows = delta.shape
-    width = image_s.shape[3]
-    return call(
-        text_kernel,
-        [(VMEM, delta), (VMEM, image_s)],
-        [((count // 4, width), F32 if k == 0 else BF16) for k in range(4)] + [(delta.shape, BF16)],
-        6,
-        flops=4 * count * rows * width,
-        size=count * rows,
-        input_output_aliases={0: 4},
     )
 
 
@@ -367,13 +353,16 @@
     spot = lax.axis_index("grp")
     core, y, z = lax.rem(spot, 2), lax.rem(lax.div(spot, 2), 4), lax.div(spot, 8)
     for k, out in zip((2, 1, 3, 0), outs[1:] + outs[:1]):
-        for flip in range(2):
-            at = (z + flip - 2 * z * flip) * 4 + lax.rem(y + k, 4)
-            begin = pl.multiple_of(at * LANES, LANES)
-            mine = jnp.dot(
-                turned[...], delta[core, :, pl.ds(begin, LANES)], preferred_element_type=F32
-            )
-            out[flip] = (mine + other[at].astype(F32)).astype(out.dtype)
+        places = [(z + flip - 2 * z * flip) * 4 + lax.rem(y + k, 4) for flip in range(2)]
+        both = jnp.concatenate(
+            [delta[core, :, pl.ds(pl.multiple_of(at * LANES, LANES), LANES)] for at in places],
+            axis=1,
+        )
+        mine = jnp.dot(turned[...], both, preferred_element_type=F32)
+        for flip, at in enumerate(places):
+            out[flip] = (
+                mine[:, flip * LANES : flip * LANES + LANES] + other[at].astype(F32)
+            ).astype(out.dtype)
 
 
 def image_part(turned, delta, other):
@@ -396,40 +385,40 @@
 def shards(image_t, text_t, image_s, text_s):
     width_t, width_s = image_t.shape[1], image_s.shape[1]
     n = text_t.shape[0]
-    cut = n // 2
     image_t = image_t.reshape(8, 2, 128, width_t)
     image_s = image_s.reshape(8, 2, 128, width_s)
 
     own = join(text_t, text_s)
-    across = permute(own, cross_z)
     left = permute(own, along_x(1))
     right = permute(own, along_x(3))
+    far = permute(own, along_x(2))
+    across = permute(own, cross_z)
     state = first_logits(own, image_t, image_s, 8 * n)
-    across, left, right, running = lax.optimization_barrier((across, left, right, state[5]))
+    across, far, running = lax.optimization_barrier((across, far, state[5]))
     state = (*state[:5], running)
-    far = jnp.concatenate(
-        (permute(left[:cut], along_x(1)), permute(right[cut:], along_x(3))), axis=0
-    )
     across_left = permute(across, along_x(1))
     across_right = permute(across, along_x(3))
     across_far = permute(far, cross_z)
-    state = more_logits([(n, across), (2 * n, left), (4 * n, right), (6 * n, far)], state)
-    state = more_logits([(3 * n, across_left), (5 * n, across_right)], state)
-    state = more_logits([(7 * n, across_far)], state, last=True)
+    state = more_logits([(n, across), (6 * n, far), (2 * n, left), (4 * n, right)], state)
+    state = more_logits([(7 * n, across_far)], state)
+    state = more_logits([(3 * n, across_left), (5 * n, across_right)], state, last=True)
     _, _, logit_t, logit_s, turned, stats = state
     stats, (logit_t, logit_s) = merge(
         [stats] + [permute(stats, m) for m in (other_core, along_y(0, 1), other_core_and_z)],
         [logit_t, logit_s],
     )
     stats = [stats] + [permute(stats, along_y(k)) for k in (2, 1, 3)]
-    grad_other, delta, row_loss = delta_part(logit_t, logit_s, turned, stats)
+    grad_other, kept_text, away_far, away_left, away_right, delta, row_loss = delta_part(
+        logit_t, logit_s, turned, image_s, stats
+    )
     from_core = permute(grad_other, other_core)
-    kept_text, *away_text, delta = text_part(delta, image_s)
+    from_far = permute(away_far, along_x(2))
     kept_image, *away_image = image_part(turned, delta, from_core)
-    *away_text, _ = lax.optimization_barrier((*away_text, away_image[0]))
-    image_terms = [kept_image] + [permute(v, along_y(k)) for v, k in zip(away_image, (2, 1, 3))]
-    text_terms = [kept_text] + [permute(v, along_x(k)) for v, k in zip(away_text, (2, 3, 1))]
-    image_sum = total(image_terms)
+    away_left, away_right, _ = lax.optimization_barrier((away_left, away_right, away_image[0]))
+    image_terms = [permute(v, along_y(k)) for v, k in zip(away_image, (2, 1, 3))]
+    *image_terms, from_far = lax.optimization_barrier((*image_terms, from_far))
+    image_sum = total([kept_image] + image_terms)
+    text_terms = [kept_text, from_far, permute(away_left, along_x(3)), permute(away_right, along_x(1))]
     from_z = permute(image_sum[1].astype(BF16), along_y(0, 1))
     grad_image = (image_sum[0] + from_z.astype(F32)).T.astype(BF16)
     text_sum = total(text_terms)

time: 96.2 us -> 80.6 us (0.84)
  waiting for transfers between devices: 32.6 us -> 22.1 us
  Pallas kernels: 24.7 us -> 19.1 us
    ppermute x23 -> x22, waiting for transfers between devices: 32.6 us -> 22.1 us  [permute(): lax.ppermute(v, AXES, [(i, index(*move(*place(i)))) for i in range(128)])]
    pallas_call x9 -> x8, Pallas kernels: 24.7 us -> 19.1 us  [call(): pl.pallas_call(body, in_specs=specs, out_specs=[pl.BlockSpec(memory_space...]
    ppermute x23 -> x22, starting transfers between devices: 35.3 us -> 36.1 us  [permute(): lax.ppermute(v, AXES, [(i, index(*move(*place(i)))) for i in range(128)])]
  transfers between devices with their start and end apart: 23 -> 22, of which waited for: 14 -> 14; matrix products, arithmetic and copies ran while one was open for 2% -> 2% of each run, Pallas kernels for 17% -> 15%
where the time goes in v3:
time: 80.6 us; the launch traced here: 80.5 us
  starting transfers between devices  36.1 us (45%)
  waiting for transfers between devices  22.1 us (27%)
  Pallas kernels  19.1 us (24%)
  local copies, waits for them, and re-layouts  1.41 us (2%)
  other arithmetic  0.97 us (1%)
    ppermute x22, starting transfers between devices, permute(): lax.ppermute(v, AXES, [(i, index(*move(*place(i)))) for i in range(128)])  36.1 us
    ppermute x22, waiting for transfers between devices, permute(): lax.ppermute(v, AXES, [(i, index(*move(*place(i)))) for i in range(128)])  22.1 us
    pallas_call x8, Pallas kernels, call(): pl.pallas_call(body, in_specs=specs, out_specs=[pl.BlockSpec(memory_space...  19.1 us
  transfers between devices with their start and end apart: 22, of which 14 were waited for; matrix products, arithmetic and copies ran while one was open for 2% of the time, Pallas kernels for 15%

profile of v3, /device:TPU:0, one launch (start us, length us, event | category | flops | bytes accessed | tf_op | source)
XLA Modules:
  0.0 80.5 jit_solution(11272729936562199908)
XLA Ops:
  0.6 1.0 %shard_map.67.own = bf16[128,1536]{1,0:T(8,128)(2,1)S(1)} custom-call(bf16[128,1024]{1,0:T(8,128)(2,1)} %text_t.1, bf16[128,512]{1,0:T(8,128)(2,1)} %text_s.1), custom_call_target="tpu_custom_call" | custom-call | tf_op jit(solution)/shard_map/pallas_call | solution.py:64
  1.6 3.2 %collective-permute-start.1 = (bf16[128,1536]{1,0:T(8,128)(2,1)S(1)}, bf16[128,1536]{1,0:T(8,128)(2,1)S(1)}, u32[]{:S(2)}, u32[]{:S(2)}) collective-permute-start(bf16[128,1536]{1,0:T(8,128)(2,1)S(1)} %shard_map.67.own), channel_id=1, source_target_pairs={{0,32},{1,33},{2,34},{3,35},{4,36},{5,37},{6,38},{7,39},{8,40},{9,... | collective-permute-start | bytes 1179656 | tf_op jit(solution)/shard_map/ppermute | solution.py:35
  4.8 4.0 %collective-permute-start = (bf16[128,1536]{1,0:T(8,128)(2,1)S(1)}, bf16[128,1536]{1,0:T(8,128)(2,1)S(1)}, u32[]{:S(2)}, u32[]{:S(2)}) collective-permute-start(bf16[128,1536]{1,0:T(8,128)(2,1)S(1)} %shard_map.67.own), channel_id=1, source_target_pairs={{0,72},{1,73},{2,74},{3,75},{4,76},{5,77},{6,78},{7,79},{8,64},{9,... | collective-permute-start | bytes 1179656 | tf_op jit(solution)/shard_map/ppermute | solution.py:35
  8.9 1.1 %collective-permute-start.6 = (bf16[128,1536]{1,0:T(8,128)(2,1)S(1)}, bf16[128,1536]{1,0:T(8,128)(2,1)S(1)}, u32[]{:S(2)}, u32[]{:S(2)}) collective-permute-start(bf16[128,1536]{1,0:T(8,128)(2,1)S(1)} %shard_map.67.own), channel_id=1, source_target_pairs={{0,48},{1,49},{2,50},{3,51},{4,52},{5,53},{6,54},{7,55},{8,56},{9,... | collective-permute-start | bytes 1179656 | tf_op jit(solution)/shard_map/ppermute | solution.py:35
  10.0 0.9 %collective-permute-start.5 = (bf16[128,1536]{1,0:T(8,128)(2,1)S(1)}, bf16[128,1536]{1,0:T(8,128)(2,1)S(1)}, u32[]{:S(2)}, u32[]{:S(2)}) collective-permute-start(bf16[128,1536]{1,0:T(8,128)(2,1)S(1)} %shard_map.67.own), channel_id=1, source_target_pairs={{0,16},{1,17},{2,18},{3,19},{4,20},{5,21},{6,22},{7,23},{8,24},{9,... | collective-permute-start | bytes 1179656 | tf_op jit(solution)/shard_map/ppermute | solution.py:35
  10.9 4.4 %shard_map.68 = (bf16[1024,2048]{1,0:T(8,128)(2,1)S(1)}, bf16[512,2048]{1,0:T(8,128)(2,1)S(1)}, f32[1024,2048]{1,0:T(8,128)S(1)}, f32[1024,2048]{1,0:T(8,128)S(1...) custom-call(bf16[128,1536]{1,0:T(8,128)(2,1)S(1)} %shard_map.67.own, bf16[8,2,128,1024]{3,2,1,0:T(8,128)(2,1)} %bitcast.18, ...), custom_call_target="tpu_custom_call" | custom-call | flops 805306368 | bytes 6291456 | tf_op jit(solution)/shard_map/pallas_call | solution.py:64
  15.3 2.4 %collective-permute-done.refs_0_ = bf16[128,1536]{1,0:T(8,128)(2,1)S(1)} collective-permute-done((bf16[128,1536]{1,0:T(8,128)(2,1)S(1)}, bf16[128,1536]{1,0:T(8,128)(2,1)S(1)}, u32[]{:S(2)}, u32[]{:S(2)}) %collective-permute-start) | collective-permute-done | bytes 393248 | tf_op jit(solution)/shard_map/ppermute | solution.py:35
  17.7 3.0 %collective-permute-start.4 = (bf16[128,1536]{1,0:T(8,128)(2,1)S(1)}, bf16[128,1536]{1,0:T(8,128)(2,1)S(1)}, u32[]{:S(2)}, u32[]{:S(2)}) collective-permute-start(bf16[128,1536]{1,0:T(8,128)(2,1)S(1)} %collective-permute-done.1.refs_1_), channel_id=1, source_target_pairs={{0,72},{1,73},{2,74},{3,75},{4,76},{5,77},{6,78},{7,79},{8,64},{9,... | collective-permute-start | bytes 1179656 | tf_op jit(solution)/shard_map/ppermute | solution.py:35
  20.6 1.5 %collective-permute-start.3 = (bf16[128,1536]{1,0:T(8,128)(2,1)S(1)}, bf16[128,1536]{1,0:T(8,128)(2,1)S(1)}, u32[]{:S(2)}, u32[]{:S(2)}) collective-permute-start(bf16[128,1536]{1,0:T(8,128)(2,1)S(1)} %collective-permute-done.refs_0_), channel_id=1, source_target_pairs={{0,48},{1,49},{2,50},{3,51},{4,52},{5,53},{6,54},{7,55},{8,56},{9,... | collective-permute-start | bytes 1179656 | tf_op jit(solution)/shard_map/ppermute | solution.py:35
  22.7 1.1 %collective-permute-done.6.refs_3_ = bf16[128,1536]{1,0:T(8,128)(2,1)S(1)} collective-permute-done((bf16[128,1536]{1,0:T(8,128)(2,1)S(1)}, bf16[128,1536]{1,0:T(8,128)(2,1)S(1)}, u32[]{:S(2)}, u32[]{:S(2)}) %collective-permute-start.6) | collective-permute-done | bytes 393248 | tf_op jit(solution)/shard_map/ppermute | solution.py:35
  23.8 5.0 %shard_map.69 = (f32[1024,2048]{1,0:T(8,128)S(1)}, f32[1024,2048]{1,0:T(8,128)S(1)}, bf16[512,1024]{1,0:T(8,128)(2,1)S(1)}, f32[8,2048]{1,0:T(8,128)S(1)}) custom-call(bf16[128,1536]{1,0:T(8,128)(2,1)S(1)} %collective-permute-done.refs_0_, ...), custom_call_target="tpu_custom_call", output_to_operand_aliasing={{0}: (6, {}), {1}: (7, {}), {2}: (8, {})} | custom-call | flops 3221225472 | bytes 2097152 | tf_op jit(solution)/shard_map/pallas_call | solution.py:64
  28.9 1.4 %shard_map.70 = (f32[1024,2048]{1,0:T(8,128)S(1)}, f32[1024,2048]{1,0:T(8,128)S(1)}, bf16[512,1024]{1,0:T(8,128)(2,1)S(1)}, f32[8,2048]{1,0:T(8,128)S(1)}) custom-call(bf16[128,1536]{1,0:T(8,128)(2,1)S(1)} %collective-permute-done.4.refs_0_, ...), custom_call_target="tpu_custom_call", output_to_operand_aliasing={{0}: (3, {}), {1}: (4, {}), {2}: (5, {})} | custom-call | flops 805306368 | bytes 524288 | tf_op jit(solution)/shard_map/pallas_call | solution.py:64
  30.3 0.9 %collective-permute-done.3.refs_1_ = bf16[128,1536]{1,0:T(8,128)(2,1)S(1)} collective-permute-done((bf16[128,1536]{1,0:T(8,128)(2,1)S(1)}, bf16[128,1536]{1,0:T(8,128)(2,1)S(1)}, u32[]{:S(2)}, u32[]{:S(2)}) %collective-permute-start.3) | collective-permute-done | bytes 393248 | tf_op jit(solution)/shard_map/ppermute | solution.py:35
  31.1 1.0 %collective-permute-done.2.refs_0_ = bf16[128,1536]{1,0:T(8,128)(2,1)S(1)} collective-permute-done((bf16[128,1536]{1,0:T(8,128)(2,1)S(1)}, bf16[128,1536]{1,0:T(8,128)(2,1)S(1)}, u32[]{:S(2)}, u32[]{:S(2)}) %collective-permute-start.2) | collective-permute-done | bytes 393248 | tf_op jit(solution)/shard_map/ppermute | solution.py:35
  32.1 2.5 %shard_map.71 = (f32[1024,2048]{1,0:T(8,128)S(1)}, f32[1024,2048]{1,0:T(8,128)S(1)}, bf16[512,1024]{1,0:T(8,128)(2,1)S(1)}, f32[48,128]{1,0:T(8,128)S(1)}) custom-call(bf16[128,1536]{1,0:T(8,128)(2,1)S(1)} %collective-permute-done.2.refs_0_, ...), custom_call_target="tpu_custom_call", output_to_operand_aliasing={{0}: (4, {}), {1}: (5, {}), {2}: (6, {})} | custom-call | flops 1610612736 | bytes 1048576 | tf_op jit(solution)/shard_map/pallas_call | solution.py:64
  34.7 1.0 %collective-permute-start.8 = (f32[48,128]{1,0:T(8,128)S(1)}, f32[48,128]{1,0:T(8,128)S(1)}, u32[]{:S(2)}, u32[]{:S(2)}) collective-permute-start(f32[48,128]{1,0:T(8,128)S(1)} %get-tuple-element.61.a), channel_id=1, source_target_pairs={{0,8},{1,9},{2,10},{3,11},{4,12},{5,13},{6,14},{7,15},{8,0},{9,1},... | collective-permute-start | bytes 73736 | tf_op jit(solution)/shard_map/ppermute | solution.py:35
  36.5 1.4 %collective-permute-done.9.d = f32[48,128]{1,0:T(8,128)S(1)} collective-permute-done((f32[48,128]{1,0:T(8,128)S(1)}, f32[48,128]{1,0:T(8,128)S(1)}, u32[]{:S(2)}, u32[]{:S(2)}) %collective-permute-start.9) | collective-permute-done | bytes 24608 | tf_op jit(solution)/shard_map/ppermute | solution.py:35
  37.9 0.9 %collective-permute-done.8.c = f32[48,128]{1,0:T(8,128)S(1)} collective-permute-done((f32[48,128]{1,0:T(8,128)S(1)}, f32[48,128]{1,0:T(8,128)S(1)}, u32[]{:S(2)}, u32[]{:S(2)}) %collective-permute-start.8) | collective-permute-done | bytes 24608 | tf_op jit(solution)/shard_map/ppermute | solution.py:35
  38.9 3.1 %collective-permute-start.12 = (f32[48,128]{1,0:T(8,128)S(1)}, f32[48,128]{1,0:T(8,128)S(1)}, u32[]{:S(2)}, u32[]{:S(2)}) collective-permute-start(f32[48,128]{1,0:T(8,128)S(1)} %get-tuple-element.67.a), channel_id=1, source_target_pairs={{0,6},{1,7},{2,0},{3,1},{4,2},{5,3},{6,4},{7,5},{8,14},{9,15},{10,... | collective-permute-start | bytes 73736 | tf_op jit(solution)/shard_map/ppermute | solution.py:35
  41.9 2.2 %collective-permute-start.10 = (f32[48,128]{1,0:T(8,128)S(1)}, f32[48,128]{1,0:T(8,128)S(1)}, u32[]{:S(2)}, u32[]{:S(2)}) collective-permute-start(f32[48,128]{1,0:T(8,128)S(1)} %get-tuple-element.67.a), channel_id=1, source_target_pairs={{0,4},{1,5},{2,6},{3,7},{4,0},{5,1},{6,2},{7,3},{8,12},{9,13},{10,... | collective-permute-start | bytes 73736 | tf_op jit(solution)/shard_map/ppermute | solution.py:35
  44.1 2.8 %collective-permute-done.11.c = f32[48,128]{1,0:T(8,128)S(1)} collective-permute-done((f32[48,128]{1,0:T(8,128)S(1)}, f32[48,128]{1,0:T(8,128)S(1)}, u32[]{:S(2)}, u32[]{:S(2)}) %collective-permute-start.11) | collective-permute-done | bytes 24608 | tf_op jit(solution)/shard_map/ppermute | solution.py:35
  47.3 3.6 %shard_map.73 = (bf16[8,512,128]{2,1,0:T(8,128)(2,1)S(1)}, f32[256,512]{1,0:T(8,128)S(1)}, bf16[256,512]{1,0:T(8,128)(2,1)S(1)}, bf16[256,512]{1,0:T(8,128)(2,1)...) custom-call(f32[1024,2048]{1,0:T(8,128)S(1)} %get-tuple-element.64.logit_t, ...), custom_call_target="tpu_custom_call" | custom-call | flops 3221225472 | bytes 8388608 | tf_op jit(solution)/shard_map/pallas_call | solution.py:64
  50.9 3.2 %collective-permute-start.17 = (bf16[256,512]{1,0:T(8,128)(2,1)S(1)}, bf16[256,512]{1,0:T(8,128)(2,1)S(1)}, u32[]{:S(2)}, u32[]{:S(2)}) collective-permute-start(bf16[256,512]{1,0:T(8,128)(2,1)S(1)} %get-tuple-element.75), channel_id=1, source_target_pairs={{0,32},{1,33},{2,34},{3,35},{4,36},{5,37},{6,38},{7,39},{8,40},{9,... | collective-permute-start | bytes 786440 | tf_op jit(solution)/shard_map/ppermute | solution.py:35
  54.2 1.4 %shard_map.74 = (f32[2,512,128]{2,1,0:T(8,128)S(1)}, bf16[2,512,128]{2,1,0:T(8,128)(2,1)S(1)}, bf16[2,512,128]{2,1,0:T(8,128)(2,1)S(1)}, bf16[2,512,128]{2,1,0:T(8,128)(2,1)S(1)}) custom-call(bf16[512,1024]{1,0:T(8,128)(2,1)S(1)} %get-tuple-element.66.turned, bf16[2,1024,1024]{2,1,0:T(8,128)(2,1)S(1)} %get-tuple-element.69.delta, ...), custom_call_target="tpu_custom_call" | custom-call | flops 1073741824 | bytes 1048576 | tf_op jit(solution)/shard_map/pallas_call | solution.py:64
  56.2 2.7 %collective-permute-start.16 = (bf16[2,512,128]{2,1,0:T(8,128)(2,1)S(1)}, bf16[2,512,128]{2,1,0:T(8,128)(2,1)S(1)}, u32[]{:S(2)}, u32[]{:S(2)}) collective-permute-start(bf16[2,512,128]{2,1,0:T(8,128)(2,1)S(1)} %get-tuple-element.74), channel_id=1, source_target_pairs={{0,6},{1,7},{2,0},{3,1},{4,2},{5,3},{6,4},{7,5},{8,14},{9,15},{10,... | collective-permute-start | bytes 786440 | tf_op jit(solution)/shard_map/ppermute | solution.py:35
  58.9 1.4 %collective-permute-start.14 = (bf16[2,512,128]{2,1,0:T(8,128)(2,1)S(1)}, bf16[2,512,128]{2,1,0:T(8,128)(2,1)S(1)}, u32[]{:S(2)}, u32[]{:S(2)}) collective-permute-start(bf16[2,512,128]{2,1,0:T(8,128)(2,1)S(1)} %get-tuple-element.72), channel_id=1, source_target_pairs={{0,4},{1,5},{2,6},{3,7},{4,0},{5,1},{6,2},{7,3},{8,12},{9,13},{10,... | collective-permute-start | bytes 786440 | tf_op jit(solution)/shard_map/ppermute | solution.py:35
  60.9 2.3 %collective-permute-start.19 = (bf16[256,512]{1,0:T(8,128)(2,1)S(1)}, bf16[256,512]{1,0:T(8,128)(2,1)S(1)}, u32[]{:S(2)}, u32[]{:S(2)}) collective-permute-start(bf16[256,512]{1,0:T(8,128)(2,1)S(1)} %get-tuple-element.83), channel_id=1, source_target_pairs={{0,48},{1,49},{2,50},{3,51},{4,52},{5,53},{6,54},{7,55},{8,56},{9,... | collective-permute-start | bytes 786440 | tf_op jit(solution)/shard_map/ppermute | solution.py:35
  63.2 2.3 %collective-permute-done.15 = bf16[2,512,128]{2,1,0:T(8,128)(2,1)S(1)} collective-permute-done((bf16[2,512,128]{2,1,0:T(8,128)(2,1)S(1)}, bf16[2,512,128]{2,1,0:T(8,128)(2,1)S(1)}, u32[]{:S(2)}, u32[]{:S(2)}) %collective-permute-start.15) | collective-permute-done | bytes 262176 | tf_op jit(solution)/shard_map/ppermute | solution.py:35
  65.5 5.0 %collective-permute-done.16 = bf16[2,512,128]{2,1,0:T(8,128)(2,1)S(1)} collective-permute-done((bf16[2,512,128]{2,1,0:T(8,128)(2,1)S(1)}, bf16[2,512,128]{2,1,0:T(8,128)(2,1)S(1)}, u32[]{:S(2)}, u32[]{:S(2)}) %collective-permute-start.16) | collective-permute-done | bytes 262176 | tf_op jit(solution)/shard_map/ppermute | solution.py:35
  70.4 1.8 %collective-permute-done.14 = bf16[2,512,128]{2,1,0:T(8,128)(2,1)S(1)} collective-permute-done((bf16[2,512,128]{2,1,0:T(8,128)(2,1)S(1)}, bf16[2,512,128]{2,1,0:T(8,128)(2,1)S(1)}, u32[]{:S(2)}, u32[]{:S(2)}) %collective-permute-start.14) | collective-permute-done | bytes 262176 | tf_op jit(solution)/shard_map/ppermute | solution.py:35
  73.2 3.6 %collective-permute-start.21 = (bf16[128,512]{1,0:T(8,128)(2,1)S(1)}, bf16[128,512]{1,0:T(8,128)(2,1)S(1)}, u32[]{:S(2)}, u32[]{:S(2)}) collective-permute-start(bf16[128,512]{1,0:T(8,128)(2,1)S(1)} %slice.36), channel_id=1, source_target_pairs={{0,72},{1,73},{2,74},{3,75},{4,76},{5,77},{6,78},{7,79},{8,64},{9,... | collective-permute-start | bytes 393224 | tf_op jit(solution)/shard_map/ppermute | solution.py:35
  78.3 1.6 %collective-permute-done.21 = bf16[128,512]{1,0:T(8,128)(2,1)S(1)} collective-permute-done((bf16[128,512]{1,0:T(8,128)(2,1)S(1)}, bf16[128,512]{1,0:T(8,128)(2,1)S(1)}, u32[]{:S(2)}, u32[]{:S(2)}) %collective-permute-start.21) | collective-permute-done | bytes 131104 | tf_op jit(solution)/shard_map/ppermute | solution.py:35
  (30 shorter events, 6.3 us)
Async XLA Ops:
  1.6 13.6 %collective-permute-start.1 = (bf16[128,1536]{1,0:T(8,128)(2,1)S(1)}, bf16[128,1536]{1,0:T(8,128)(2,1)S(1)}, u32[]{:S(2)}, u32[]{:S(2)}) collective-permute-start(bf16[128,1536]{1,0:T(8,128)(2,1)S(1)} %shard_map.67.own), channel_id=1, source_target_pairs={{0,32},{1,33},{2,34},{3,35},{4,36},{5,37},{6,38},{7,39},{8,40},{9,... | collective-permute-start | bytes 1179656 | tf_op jit(solution)/shard_map/ppermute | solution.py:35
  4.8 12.9 %collective-permute-start = (bf16[128,1536]{1,0:T(8,128)(2,1)S(1)}, bf16[128,1536]{1,0:T(8,128)(2,1)S(1)}, u32[]{:S(2)}, u32[]{:S(2)}) collective-permute-start(bf16[128,1536]{1,0:T(8,128)(2,1)S(1)} %shard_map.67.own), channel_id=1, source_target_pairs={{0,72},{1,73},{2,74},{3,75},{4,76},{5,77},{6,78},{7,79},{8,64},{9,... | collective-permute-start | bytes 1179656 | tf_op jit(solution)/shard_map/ppermute | solution.py:35
  8.9 14.9 %collective-permute-start.6 = (bf16[128,1536]{1,0:T(8,128)(2,1)S(1)}, bf16[128,1536]{1,0:T(8,128)(2,1)S(1)}, u32[]{:S(2)}, u32[]{:S(2)}) collective-permute-start(bf16[128,1536]{1,0:T(8,128)(2,1)S(1)} %shard_map.67.own), channel_id=1, source_target_pairs={{0,48},{1,49},{2,50},{3,51},{4,52},{5,53},{6,54},{7,55},{8,56},{9,... | collective-permute-start | bytes 1179656 | tf_op jit(solution)/shard_map/ppermute | solution.py:35
  10.0 13.8 %collective-permute-start.5 = (bf16[128,1536]{1,0:T(8,128)(2,1)S(1)}, bf16[128,1536]{1,0:T(8,128)(2,1)S(1)}, u32[]{:S(2)}, u32[]{:S(2)}) collective-permute-start(bf16[128,1536]{1,0:T(8,128)(2,1)S(1)} %shard_map.67.own), channel_id=1, source_target_pairs={{0,16},{1,17},{2,18},{3,19},{4,20},{5,21},{6,22},{7,23},{8,24},{9,... | collective-permute-start | bytes 1179656 | tf_op jit(solution)/shard_map/ppermute | solution.py:35
  17.7 11.2 %collective-permute-start.4 = (bf16[128,1536]{1,0:T(8,128)(2,1)S(1)}, bf16[128,1536]{1,0:T(8,128)(2,1)S(1)}, u32[]{:S(2)}, u32[]{:S(2)}) collective-permute-start(bf16[128,1536]{1,0:T(8,128)(2,1)S(1)} %collective-permute-done.1.refs_1_), channel_id=1, source_target_pairs={{0,72},{1,73},{2,74},{3,75},{4,76},{5,77},{6,78},{7,79},{8,64},{9,... | collective-permute-start | bytes 1179656 | tf_op jit(solution)/shard_map/ppermute | solution.py:35
  20.6 10.5 %collective-permute-start.3 = (bf16[128,1536]{1,0:T(8,128)(2,1)S(1)}, bf16[128,1536]{1,0:T(8,128)(2,1)S(1)}, u32[]{:S(2)}, u32[]{:S(2)}) collective-permute-start(bf16[128,1536]{1,0:T(8,128)(2,1)S(1)} %collective-permute-done.refs_0_), channel_id=1, source_target_pairs={{0,48},{1,49},{2,50},{3,51},{4,52},{5,53},{6,54},{7,55},{8,56},{9,... | collective-permute-start | bytes 1179656 | tf_op jit(solution)/shard_map/ppermute | solution.py:35
  22.2 10.0 %collective-permute-start.2 = (bf16[128,1536]{1,0:T(8,128)(2,1)S(1)}, bf16[128,1536]{1,0:T(8,128)(2,1)S(1)}, u32[]{:S(2)}, u32[]{:S(2)}) collective-permute-start(bf16[128,1536]{1,0:T(8,128)(2,1)S(1)} %collective-permute-done.refs_0_), channel_id=1, source_target_pairs={{0,16},{1,17},{2,18},{3,19},{4,20},{5,21},{6,22},{7,23},{8,24},{9,... | collective-permute-start | bytes 1179656 | tf_op jit(solution)/shard_map/ppermute | solution.py:35
  34.6 3.3 %collective-permute-start.9 = (f32[48,128]{1,0:T(8,128)S(1)}, f32[48,128]{1,0:T(8,128)S(1)}, u32[]{:S(2)}, u32[]{:S(2)}) collective-permute-start(f32[48,128]{1,0:T(8,128)S(1)} %get-tuple-element.61.a), channel_id=1, source_target_pairs={{0,9},{1,8},{2,11},{3,10},{4,13},{5,12},{6,15},{7,14},{8,1},{9,0},... | collective-permute-start | bytes 73736 | tf_op jit(solution)/shard_map/ppermute | solution.py:35
  34.7 4.2 %collective-permute-start.8 = (f32[48,128]{1,0:T(8,128)S(1)}, f32[48,128]{1,0:T(8,128)S(1)}, u32[]{:S(2)}, u32[]{:S(2)}) collective-permute-start(f32[48,128]{1,0:T(8,128)S(1)} %get-tuple-element.61.a), channel_id=1, source_target_pairs={{0,8},{1,9},{2,10},{3,11},{4,12},{5,13},{6,14},{7,15},{8,0},{9,1},... | collective-permute-start | bytes 73736 | tf_op jit(solution)/shard_map/ppermute | solution.py:35
  35.7 3.1 %collective-permute-start.7 = (f32[48,128]{1,0:T(8,128)S(1)}, f32[48,128]{1,0:T(8,128)S(1)}, u32[]{:S(2)}, u32[]{:S(2)}) collective-permute-start(f32[48,128]{1,0:T(8,128)S(1)} %get-tuple-element.61.a), channel_id=1, source_target_pairs={{0,1},{1,0},{2,3},{3,2},{4,5},{5,4},{6,7},{7,6},{8,9},{9,8},{10,11... | collective-permute-start | bytes 73736 | tf_op jit(solution)/shard_map/ppermute | solution.py:35
  38.8 8.4 %copy-start = (bf16[2048,512]{1,0:T(8,128)(2,1)S(1)}, bf16[2048,512]{1,0:T(8,128)(2,1)}, u32[]{:S(2)}) copy-start(bf16[2048,512]{1,0:T(8,128)(2,1)} %param.6) | copy-start | bytes 6291460
  38.9 5.3 %collective-permute-start.12 = (f32[48,128]{1,0:T(8,128)S(1)}, f32[48,128]{1,0:T(8,128)S(1)}, u32[]{:S(2)}, u32[]{:S(2)}) collective-permute-start(f32[48,128]{1,0:T(8,128)S(1)} %get-tuple-element.67.a), channel_id=1, source_target_pairs={{0,6},{1,7},{2,0},{3,1},{4,2},{5,3},{6,4},{7,5},{8,14},{9,15},{10,... | collective-permute-start | bytes 73736 | tf_op jit(solution)/shard_map/ppermute | solution.py:35
  41.9 5.0 %collective-permute-start.11 = (f32[48,128]{1,0:T(8,128)S(1)}, f32[48,128]{1,0:T(8,128)S(1)}, u32[]{:S(2)}, u32[]{:S(2)}) collective-permute-start(f32[48,128]{1,0:T(8,128)S(1)} %get-tuple-element.67.a), channel_id=1, source_target_pairs={{0,2},{1,3},{2,4},{3,5},{4,6},{5,7},{6,0},{7,1},{8,10},{9,11},{10,... | collective-permute-start | bytes 73736 | tf_op jit(solution)/shard_map/ppermute | solution.py:35
  41.9 5.3 %collective-permute-start.10 = (f32[48,128]{1,0:T(8,128)S(1)}, f32[48,128]{1,0:T(8,128)S(1)}, u32[]{:S(2)}, u32[]{:S(2)}) collective-permute-start(f32[48,128]{1,0:T(8,128)S(1)} %get-tuple-element.67.a), channel_id=1, source_target_pairs={{0,4},{1,5},{2,6},{3,7},{4,0},{5,1},{6,2},{7,3},{8,12},{9,13},{10,... | collective-permute-start | bytes 73736 | tf_op jit(solution)/shard_map/ppermute | solution.py:35
  50.8 3.3 %collective-permute-start.13 = (bf16[8,512,128]{2,1,0:T(8,128)(2,1)S(1)}, bf16[8,512,128]{2,1,0:T(8,128)(2,1)S(1)}, u32[]{:S(2)}, u32[]{:S(2)}) collective-permute-start(bf16[8,512,128]{2,1,0:T(8,128)(2,1)S(1)} %get-tuple-element.70), channel_id=1, source_target_pairs={{0,1},{1,0},{2,3},{3,2},{4,5},{5,4},{6,7},{7,6},{8,9},{9,8},{10,11... | collective-permute-start | bytes 3145736 | tf_op jit(solution)/shard_map/ppermute | solution.py:35
  50.9 12.3 %collective-permute-start.17 = (bf16[256,512]{1,0:T(8,128)(2,1)S(1)}, bf16[256,512]{1,0:T(8,128)(2,1)S(1)}, u32[]{:S(2)}, u32[]{:S(2)}) collective-permute-start(bf16[256,512]{1,0:T(8,128)(2,1)S(1)} %get-tuple-element.75), channel_id=1, source_target_pairs={{0,32},{1,33},{2,34},{3,35},{4,36},{5,37},{6,38},{7,39},{8,40},{9,... | collective-permute-start | bytes 786440 | tf_op jit(solution)/shard_map/ppermute | solution.py:35
  55.5 9.9 %collective-permute-start.15 = (bf16[2,512,128]{2,1,0:T(8,128)(2,1)S(1)}, bf16[2,512,128]{2,1,0:T(8,128)(2,1)S(1)}, u32[]{:S(2)}, u32[]{:S(2)}) collective-permute-start(bf16[2,512,128]{2,1,0:T(8,128)(2,1)S(1)} %get-tuple-element.73), channel_id=1, source_target_pairs={{0,2},{1,3},{2,4},{3,5},{4,6},{5,7},{6,0},{7,1},{8,10},{9,11},{10,... | collective-permute-start | bytes 786440 | tf_op jit(solution)/shard_map/ppermute | solution.py:35
  56.2 14.2 %collective-permute-start.16 = (bf16[2,512,128]{2,1,0:T(8,128)(2,1)S(1)}, bf16[2,512,128]{2,1,0:T(8,128)(2,1)S(1)}, u32[]{:S(2)}, u32[]{:S(2)}) collective-permute-start(bf16[2,512,128]{2,1,0:T(8,128)(2,1)S(1)} %get-tuple-element.74), channel_id=1, source_target_pairs={{0,6},{1,7},{2,0},{3,1},{4,2},{5,3},{6,4},{7,5},{8,14},{9,15},{10,... | collective-permute-start | bytes 786440 | tf_op jit(solution)/shard_map/ppermute | solution.py:35
  58.9 13.3 %collective-permute-start.14 = (bf16[2,512,128]{2,1,0:T(8,128)(2,1)S(1)}, bf16[2,512,128]{2,1,0:T(8,128)(2,1)S(1)}, u32[]{:S(2)}, u32[]{:S(2)}) collective-permute-start(bf16[2,512,128]{2,1,0:T(8,128)(2,1)S(1)} %get-tuple-element.72), channel_id=1, source_target_pairs={{0,4},{1,5},{2,6},{3,7},{4,0},{5,1},{6,2},{7,3},{8,12},{9,13},{10,... | collective-permute-start | bytes 786440 | tf_op jit(solution)/shard_map/ppermute | solution.py:35
  60.9 12.2 %collective-permute-start.19 = (bf16[256,512]{1,0:T(8,128)(2,1)S(1)}, bf16[256,512]{1,0:T(8,128)(2,1)S(1)}, u32[]{:S(2)}, u32[]{:S(2)}) collective-permute-start(bf16[256,512]{1,0:T(8,128)(2,1)S(1)} %get-tuple-element.83), channel_id=1, source_target_pairs={{0,48},{1,49},{2,50},{3,51},{4,52},{5,53},{6,54},{7,55},{8,56},{9,... | collective-permute-start | bytes 786440 | tf_op jit(solution)/shard_map/ppermute | solution.py:35
  63.2 9.9 %collective-permute-start.20 = (bf16[256,512]{1,0:T(8,128)(2,1)S(1)}, bf16[256,512]{1,0:T(8,128)(2,1)S(1)}, u32[]{:S(2)}, u32[]{:S(2)}) collective-permute-start(bf16[256,512]{1,0:T(8,128)(2,1)S(1)} %get-tuple-element.84), channel_id=1, source_target_pairs={{0,16},{1,17},{2,18},{3,19},{4,20},{5,21},{6,22},{7,23},{8,24},{9,... | collective-permute-start | bytes 786440 | tf_op jit(solution)/shard_map/ppermute | solution.py:35
  72.4 5.0 %collective-permute-start.18 = (bf16[512,128]{1,0:T(8,128)(2,1)S(1)}, bf16[512,128]{1,0:T(8,128)(2,1)S(1)}, u32[]{:S(2)}, u32[]{:S(2)}) collective-permute-start(bf16[512,128]{1,0:T(8,128)(2,1)S(1)} %fusion.4), channel_id=1, source_target_pairs={{0,8},{1,9},{2,10},{3,11},{4,12},{5,13},{6,14},{7,15},{8,0},{9,1},... | collective-permute-start | bytes 393224 | tf_op jit(solution)/shard_map/ppermute | solution.py:35
  73.2 6.6 %collective-permute-start.21 = (bf16[128,512]{1,0:T(8,128)(2,1)S(1)}, bf16[128,512]{1,0:T(8,128)(2,1)S(1)}, u32[]{:S(2)}, u32[]{:S(2)}) collective-permute-start(bf16[128,512]{1,0:T(8,128)(2,1)S(1)} %slice.36), channel_id=1, source_target_pairs={{0,72},{1,73},{2,74},{3,75},{4,76},{5,77},{6,78},{7,79},{8,64},{9,... | collective-permute-start | bytes 393224 | tf_op jit(solution)/shard_map/ppermute | solution.py:35

commit v4 on v3

--- a/solution.py
+++ b/solution.py
@@ -45,10 +45,6 @@
 
 def other_core(zh, x, zl, y, c):
     return (zh, x, zl, y, 1 - c)
-
-
-def other_core_and_z(zh, x, zl, y, c):
-    return (zh, x, 1 - zl, y, 1 - c)
 
 
 def cross_z(zh, x, zl, y, c):
@@ -249,40 +245,38 @@
 
 
 def merged(parts):
-    def total(v):
-        return (v[0] + v[1]) + (v[2] + v[3])
-
     rows = parts[0].shape[0] // 3
     lse_t, lse_s, gap = ([p[rows * k : rows * k + rows, :] for p in parts] for k in range(3))
     top_t = functools.reduce(jnp.maximum, lse_t)
     top_s = functools.reduce(jnp.maximum, lse_s)
     part_t = [jnp.exp2(v - top_t) for v in lse_t]
-    sum_t = total(part_t)
-    mean = total([p * g for p, g in zip(part_t, gap)]) / sum_t
-    all_s = top_s + jnp.log2(total([jnp.exp2(v - top_s) for v in lse_s]))
-    return top_t + jnp.log2(sum_t), all_s, mean
-
-
-def merge_kernel(a, b, c, d, _, __, out, *held):
-    rows = out.shape[0] // 3
-    for k, v in enumerate(merged((a, b, c, d))):
-        out[rows * k : rows * k + rows, :] = v
-
-
-def merge(parts, held):
+    sum_t = functools.reduce(jnp.add, part_t)
+    mean = functools.reduce(jnp.add, [p * g for p, g in zip(part_t, gap)]) / sum_t
+    sum_s = functools.reduce(jnp.add, [jnp.exp2(v - top_s) for v in lse_s])
+    return top_t + jnp.log2(sum_t), top_s + jnp.log2(sum_s), mean
+
+
+def merge_kernel(mine, other, _, __, out, *held):
+    rows = out.shape[1] // 3
+    for k, v in enumerate(merged((mine, other))):
+        for peer in range(out.shape[0]):
+            out[peer, rows * k : rows * k + rows, :] = v
+
+
+def merge(mine, other, held, copies):
     out, *held = call(
         merge_kernel,
-        [(VMEM, v) for v in (*parts, *held)],
-        [(parts[0].shape, F32)] + [(v.shape, F32) for v in held],
+        [(VMEM, v) for v in (mine, other, *held)],
+        [((copies, *mine.shape), F32)] + [(v.shape, F32) for v in held],
         4,
-        input_output_aliases={4: 1, 5: 2},
+        input_output_aliases={2: 1, 3: 2},
     )
     return out, held
 
 
-def put_merged(parts, lse, loss):
+def put_merged(received, lse, loss):
     rows = lse.shape[0] // 2
-    all_t, all_s, mean = merged(parts)
+    all_t, all_s, mean = merged([received.at[p] for p in range(received.shape[0])])
     lse[:rows, :] = all_t
     lse[rows:, :] = all_s
     value = (mean - all_t + all_s) * LN2
@@ -292,89 +286,136 @@
             loss[2 * j + c : 2 * j + c + 1, :] = value[at : at + 1, :]
 
 
-def delta_kernel(
-    scale, logit_t, logit_s, turned, image_s, a, b, c, d, other, own, far, left, right, delta, loss, lse
-):
-    put_merged((a, b, c, d), lse, loss)
+def tile_delta(logit_t, logit_s, lse, scale, begins):
+    count, rows = logit_t.shape
+    lows, parts = [], []
+    for values, first in ((logit_t, 0), (logit_s, rows // LANES)):
+        lows.append(
+            jnp.concatenate([lse[pl.ds(first + at, 1), :] for at in begins], axis=1)
+        )
+        parts.append(
+            jnp.concatenate(
+                [values[:, pl.ds(pl.multiple_of(at * LANES, LANES), LANES)] for at in begins], axis=1
+            )
+        )
+    prob_t, prob_s = (jnp.exp2(part - low) for part, low in zip(parts, lows))
+    return ((prob_s - prob_t) * scale).astype(BF16)
+
+
+PAIR = 2
+
+
+def away_kernel(scale, logit_t, logit_s, turned, received, out, delta, lse, loss, *held):
+    put_merged(received, lse, loss)
     away = 1 - lax.rem(lax.axis_index("grp"), 2)
-    rows = logit_t.shape[1]
-    half = rows // 2
-    blocks, cores, block, width = image_s.shape
-    pieces = WIDE // LANES
-    for k, out in ((3, far), (1, left), (2, right), (0, own)):
-        n = out.shape[0]
-        span = slice(n * k, n * k + n)
-        for begin in range(0, rows, WIDE):
-            cols = slice(begin, begin + WIDE)
-            spots = [begin // LANES + j for j in range(pieces)]
-            low_t = jnp.concatenate([lse[j : j + 1, :] for j in spots], axis=1)
-            low_s = jnp.concatenate(
-                [lse[j + rows // LANES : j + rows // LANES + 1, :] for j in spots], axis=1
-            )
-            prob_t = jnp.exp2(logit_t[span, cols] - low_t)
-            prob_s = jnp.exp2(logit_s[span, cols] - low_s)
-            delta[begin // half, span, begin % half : begin % half + WIDE] = (
-                (prob_s - prob_t) * scale
-            ).astype(BF16)
-        total = 0.0
-        for core in range(cores):
-            total += jnp.dot(
-                delta[core, span, :],
-                image_s[:, core].reshape(blocks * block, width),
-                preferred_element_type=F32,
-            )
-        out[...] = total.astype(out.dtype)
-    for begin in range(0, half, WIDE):
-        out = jnp.dot(
-            turned[...], delta[away, :, begin : begin + WIDE], preferred_element_type=F32
-        ).astype(BF16)
-        for j in range(pieces):
-            other[begin // LANES + j] = out[:, j * LANES : j * LANES + LANES]
-
-
-def delta_part(logit_t, logit_s, turned, image_s, stats):
+    blocks = out.shape[0]
+    for j in range(0, blocks, PAIR):
+        cols = slice(j * LANES, (j + PAIR) * LANES)
+        delta[:, cols] = tile_delta(
+            logit_t, logit_s, lse, scale, [away * blocks + j + k for k in range(PAIR)]
+        )
+        grad = jnp.dot(turned[...], delta[:, cols], preferred_element_type=F32).astype(BF16)
+        for k in range(PAIR):
+            out[j + k] = grad[:, k * LANES : k * LANES + LANES]
+
+
+def away_part(logit_t, logit_s, turned, received):
     count, rows = logit_t.shape
     width = turned.shape[0]
     return call(
-        functools.partial(delta_kernel, 3.0 / math.sqrt(width)),
-        [(VMEM, v) for v in (logit_t, logit_s, turned, image_s, *stats)],
-        [((rows // 2 // LANES, width, LANES), BF16)]
-        + [((count // 4, width), F32 if k == 0 else BF16) for k in range(4)]
-        + [((2, count, rows // 2), BF16), ((rows // LANES, LANES), F32)],
+        functools.partial(away_kernel, 3.0 / math.sqrt(width)),
+        [(VMEM, v) for v in (logit_t, logit_s, turned, received)],
+        [
+            ((rows // 2 // LANES, width, LANES), BF16),
+            ((count, rows // 2), BF16),
+            ((2 * rows // LANES, LANES), F32),
+            ((rows // LANES, LANES), F32),
+            (logit_t.shape, F32),
+            (logit_s.shape, F32),
+        ],
         6,
-        flops=3 * count * rows * width,
+        flops=count * rows * width,
         size=4 * count * rows,
-        exps=2 * count * rows,
-        scratch_shapes=[pltpu.VMEM((2 * rows // LANES, LANES), F32)],
-    )
-
-
-def image_kernel(turned, delta, other, *outs):
+        exps=count * rows,
+        input_output_aliases={0: 4, 1: 5},
+    )
+
+
+def near_kernel(scale, logit_t, logit_s, lse, away, image_s, near, *texts):
+    core = lax.rem(lax.axis_index("grp"), 2)
+    blocks, _, block, width = image_s.shape
+    rows = blocks * block
+    for j in range(0, blocks, PAIR):
+        near[:, j * LANES : (j + PAIR) * LANES] = tile_delta(
+            logit_t, logit_s, lse, scale, [core * blocks + j + k for k in range(PAIR)]
+        )
+    image_near = image_s[:, pl.ds(core, 1)].reshape(rows, width)
+    image_away = image_s[:, pl.ds(1 - core, 1)].reshape(rows, width)
+    row = 0
+    for out in texts:
+        span = slice(row, row + out.shape[0])
+        row += out.shape[0]
+        out[...] = (
+            jnp.dot(away[span, :], image_away, preferred_element_type=F32)
+            + jnp.dot(near[span, :], image_near, preferred_element_type=F32)
+        ).astype(out.dtype)
+
+
+def near_part(logit_t, logit_s, lse, away, image_s):
+    count, rows = logit_t.shape
+    width = image_s.shape[3]
+    return call(
+        functools.partial(near_kernel, 3.0 / math.sqrt(width)),
+        [(VMEM, v) for v in (logit_t, logit_s, lse, away, image_s)],
+        [(away.shape, BF16)]
+        + [
+            ((count // part, width), kind)
+            for part, kind in ((4, F32), (4, BF16), (4, BF16), (8, F32), (8, BF16))
+        ],
+        10,
+        flops=2 * count * rows * width,
+        size=4 * count * rows,
+        exps=count * rows,
+    )
+
+
+def image_kernel(turned, near, other, kept, up, down, far, far_flip):
     spot = lax.axis_index("grp")
-    core, y, z = lax.rem(spot, 2), lax.rem(lax.div(spot, 2), 4), lax.div(spot, 8)
-    for k, out in zip((2, 1, 3, 0), outs[1:] + outs[:1]):
+    y, z = lax.rem(lax.div(spot, 2), 4), lax.div(spot, 8)
+    outs = (
+        (1, (up.at[0], up.at[1])),
+        (3, (down.at[0], down.at[1])),
+        (2, (far, far_flip)),
+        (0, (kept.at[0], kept.at[1])),
+    )
+    for k, pair in outs:
         places = [(z + flip - 2 * z * flip) * 4 + lax.rem(y + k, 4) for flip in range(2)]
         both = jnp.concatenate(
-            [delta[core, :, pl.ds(pl.multiple_of(at * LANES, LANES), LANES)] for at in places],
-            axis=1,
+            [near[:, pl.ds(pl.multiple_of(at * LANES, LANES), LANES)] for at in places], axis=1
         )
         mine = jnp.dot(turned[...], both, preferred_element_type=F32)
-        for flip, at in enumerate(places):
-            out[flip] = (
+        for flip, (at, out) in enumerate(zip(places, pair)):
+            out[...] = (
                 mine[:, flip * LANES : flip * LANES + LANES] + other[at].astype(F32)
             ).astype(out.dtype)
 
 
-def image_part(turned, delta, other):
-    _, count, rows = delta.shape
-    blocks, width, block = other.shape
+def image_part(turned, near, other):
+    count, rows = near.shape
+    width = turned.shape[0]
     return call(
         image_kernel,
-        [(VMEM, turned), (VMEM, delta), (VMEM, other)],
-        [((2, width, block), F32 if k == 0 else BF16) for k in range(blocks // 2)],
+        [(VMEM, turned), (VMEM, near), (VMEM, other)],
+        [
+            ((2, width, LANES), F32),
+            ((2, width, LANES), BF16),
+            ((2, width, LANES), BF16),
+            ((width, LANES), F32),
+            ((width, LANES), BF16),
+        ],
         4,
         flops=2 * count * rows * width,
-        size=count * rows,
+        size=2 * count * rows,
     )
 
 
@@ -403,27 +444,31 @@
     state = more_logits([(7 * n, across_far)], state)
     state = more_logits([(3 * n, across_left), (5 * n, across_right)], state, last=True)
     _, _, logit_t, logit_s, turned, stats = state
-    stats, (logit_t, logit_s) = merge(
-        [stats] + [permute(stats, m) for m in (other_core, along_y(0, 1), other_core_and_z)],
-        [logit_t, logit_s],
-    )
-    stats = [stats] + [permute(stats, along_y(k)) for k in (2, 1, 3)]
-    grad_other, kept_text, away_far, away_left, away_right, delta, row_loss = delta_part(
-        logit_t, logit_s, turned, image_s, stats
+    stats, (logit_t, logit_s) = merge(stats, permute(stats, other_core), [logit_t, logit_s], 8)
+    peers = [[2 * j + c for j in range(8)] for c in range(2)]
+    received = lax.all_to_all(stats, "grp", 0, 0, tiled=True, axis_index_groups=peers)
+    grad_other, away, lse, row_loss, logit_t, logit_s = away_part(
+        logit_t, logit_s, turned, received
     )
     from_core = permute(grad_other, other_core)
-    from_far = permute(away_far, along_x(2))
-    kept_image, *away_image = image_part(turned, delta, from_core)
-    away_left, away_right, _ = lax.optimization_barrier((away_left, away_right, away_image[0]))
-    image_terms = [permute(v, along_y(k)) for v, k in zip(away_image, (2, 1, 3))]
-    *image_terms, from_far = lax.optimization_barrier((*image_terms, from_far))
-    image_sum = total([kept_image] + image_terms)
-    text_terms = [kept_text, from_far, permute(away_left, along_x(3)), permute(away_right, along_x(1))]
+    near, *texts = near_part(logit_t, logit_s, lse, away, image_s)
+    image_kept, image_up, image_down, image_far, far_flip = image_part(turned, near, from_core)
+    from_flip = permute(far_flip, along_y(0, 1))
+    from_down, from_up = permute(image_up, along_y(1)), permute(image_down, along_y(3))
+    text_kept, text_left, text_right, text_far, far_cross = texts
+    far_cross, image_kept = lax.optimization_barrier((far_cross, image_kept))
+    from_cross = permute(far_cross, cross_z)
+    from_right, from_left = permute(text_left, along_x(3)), permute(text_right, along_x(1))
+    image_far = permute((image_far + from_flip.astype(F32)).astype(BF16), along_y(2))
+    text_far = permute((text_far + from_cross.astype(F32)).astype(BF16), along_x(2))
+    row_loss, from_down = lax.optimization_barrier((row_loss, from_down))
+    image_sum = total([image_kept, from_down, from_up])
+    text_sum = total([text_kept, from_left, from_right])
+    image_sum, text_sum = lax.optimization_barrier((image_sum, text_sum))
     from_z = permute(image_sum[1].astype(BF16), along_y(0, 1))
-    grad_image = (image_sum[0] + from_z.astype(F32)).T.astype(BF16)
-    text_sum = total(text_terms)
     from_across = permute(text_sum[n:].astype(BF16), cross_z)
-    grad_text = (text_sum[:n] + from_across.astype(F32)).astype(BF16)
+    grad_image = total([image_sum[0], image_far, from_z]).T.astype(BF16)
+    grad_text = total([text_sum[:n], text_far, from_across]).astype(BF16)
     return row_loss.reshape(-1), grad_image, grad_text
 
 

time: 80.6 us -> 79.7 us (0.989)
  blocking collectives: 0 us -> 11.6 us
  waiting for transfers between devices: 22.1 us -> 10.7 us
  starting transfers between devices: 36.1 us -> 33.7 us
    all_to_all x0 -> x1, blocking collectives: none -> 11.6 us  [shards(): lax.all_to_all(stats, 'grp', 0, 0, tiled=True, axis_index_groups=peers)]
    ppermute x22 -> x19, waiting for transfers between devices: 22.1 us -> 10.7 us  [permute(): lax.ppermute(v, AXES, [(i, index(*move(*place(i)))) for i in range(128)])]
    ppermute x22 -> x19, starting transfers between devices: 36.1 us -> 33.7 us  [permute(): lax.ppermute(v, AXES, [(i, index(*move(*place(i)))) for i in range(128)])]
    pallas_call x8 -> x9, Pallas kernels: 19.1 us -> 19.8 us  [call(): pl.pallas_call(body, in_specs=specs, out_specs=[pl.BlockSpec(memory_space...]
  transfers between devices with their start and end apart: 22 -> 19, of which waited for: 14 -> 9; matrix products, arithmetic and copies ran while one was open for 2% -> 2% of each run, Pallas kernels for 15% -> 19%
where the time goes in v4:
time: 79.7 us; the launch traced here: 79 us
  starting transfers between devices  33.7 us (42%)
  Pallas kernels  19.8 us (25%)
  blocking collectives  11.6 us (15%)
  waiting for transfers between devices  10.7 us (13%)
  local copies, waits for them, and re-layouts  1.41 us (2%)
  other arithmetic  0.97 us (1%)
    ppermute x19, starting transfers between devices, permute(): lax.ppermute(v, AXES, [(i, index(*move(*place(i)))) for i in range(128)])  33.7 us
    pallas_call x9, Pallas kernels, call(): pl.pallas_call(body, in_specs=specs, out_specs=[pl.BlockSpec(memory_space...  19.8 us
    all_to_all x1, blocking collectives, shards(): lax.all_to_all(stats, 'grp', 0, 0, tiled=True, axis_index_groups=peers)  11.6 us
    ppermute x19, waiting for transfers between devices, permute(): lax.ppermute(v, AXES, [(i, index(*move(*place(i)))) for i in range(128)])  10.7 us
  transfers between devices with their start and end apart: 19, of which 9 were waited for; matrix products, arithmetic and copies ran while one was open for 2% of the time, Pallas kernels for 19%

profile of v4, /device:TPU:0, one launch (start us, length us, event | category | flops | bytes accessed | tf_op | source)
XLA Modules:
  0.0 79.0 jit_solution(12207156199943552500)
XLA Ops:
  0.6 1.0 %shard_map.67.own = bf16[128,1536]{1,0:T(8,128)(2,1)S(1)} custom-call(bf16[128,1024]{1,0:T(8,128)(2,1)} %text_t.1, bf16[128,512]{1,0:T(8,128)(2,1)} %text_s.1), custom_call_target="tpu_custom_call" | custom-call | tf_op jit(solution)/shard_map/pallas_call | solution.py:60
  1.6 3.2 %collective-permute-start.1 = (bf16[128,1536]{1,0:T(8,128)(2,1)S(1)}, bf16[128,1536]{1,0:T(8,128)(2,1)S(1)}, u32[]{:S(2)}, u32[]{:S(2)}) collective-permute-start(bf16[128,1536]{1,0:T(8,128)(2,1)S(1)} %shard_map.67.own), channel_id=1, source_target_pairs={{0,32},{1,33},{2,34},{3,35},{4,36},{5,37},{6,38},{7,39},{8,40},{9,... | collective-permute-start | bytes 1179656 | tf_op jit(solution)/shard_map/ppermute | solution.py:35
  4.8 4.0 %collective-permute-start = (bf16[128,1536]{1,0:T(8,128)(2,1)S(1)}, bf16[128,1536]{1,0:T(8,128)(2,1)S(1)}, u32[]{:S(2)}, u32[]{:S(2)}) collective-permute-start(bf16[128,1536]{1,0:T(8,128)(2,1)S(1)} %shard_map.67.own), channel_id=1, source_target_pairs={{0,72},{1,73},{2,74},{3,75},{4,76},{5,77},{6,78},{7,79},{8,64},{9,... | collective-permute-start | bytes 1179656 | tf_op jit(solution)/shard_map/ppermute | solution.py:35
  8.9 1.1 %collective-permute-start.6 = (bf16[128,1536]{1,0:T(8,128)(2,1)S(1)}, bf16[128,1536]{1,0:T(8,128)(2,1)S(1)}, u32[]{:S(2)}, u32[]{:S(2)}) collective-permute-start(bf16[128,1536]{1,0:T(8,128)(2,1)S(1)} %shard_map.67.own), channel_id=1, source_target_pairs={{0,48},{1,49},{2,50},{3,51},{4,52},{5,53},{6,54},{7,55},{8,56},{9,... | collective-permute-start | bytes 1179656 | tf_op jit(solution)/shard_map/ppermute | solution.py:35
  10.0 0.9 %collective-permute-start.5 = (bf16[128,1536]{1,0:T(8,128)(2,1)S(1)}, bf16[128,1536]{1,0:T(8,128)(2,1)S(1)}, u32[]{:S(2)}, u32[]{:S(2)}) collective-permute-start(bf16[128,1536]{1,0:T(8,128)(2,1)S(1)} %shard_map.67.own), channel_id=1, source_target_pairs={{0,16},{1,17},{2,18},{3,19},{4,20},{5,21},{6,22},{7,23},{8,24},{9,... | collective-permute-start | bytes 1179656 | tf_op jit(solution)/shard_map/ppermute | solution.py:35
  10.9 4.4 %shard_map.68 = (bf16[1024,2048]{1,0:T(8,128)(2,1)S(1)}, bf16[512,2048]{1,0:T(8,128)(2,1)S(1)}, f32[1024,2048]{1,0:T(8,128)S(1)}, f32[1024,2048]{1,0:T(8,128)S(1...) custom-call(bf16[128,1536]{1,0:T(8,128)(2,1)S(1)} %shard_map.67.own, bf16[8,2,128,1024]{3,2,1,0:T(8,128)(2,1)} %bitcast.18, ...), custom_call_target="tpu_custom_call" | custom-call | flops 805306368 | bytes 6291456 | tf_op jit(solution)/shard_map/pallas_call | solution.py:60
  15.3 2.4 %collective-permute-done.refs_0_ = bf16[128,1536]{1,0:T(8,128)(2,1)S(1)} collective-permute-done((bf16[128,1536]{1,0:T(8,128)(2,1)S(1)}, bf16[128,1536]{1,0:T(8,128)(2,1)S(1)}, u32[]{:S(2)}, u32[]{:S(2)}) %collective-permute-start) | collective-permute-done | bytes 393248 | tf_op jit(solution)/shard_map/ppermute | solution.py:35
  17.7 3.0 %collective-permute-start.4 = (bf16[128,1536]{1,0:T(8,128)(2,1)S(1)}, bf16[128,1536]{1,0:T(8,128)(2,1)S(1)}, u32[]{:S(2)}, u32[]{:S(2)}) collective-permute-start(bf16[128,1536]{1,0:T(8,128)(2,1)S(1)} %collective-permute-done.1.refs_1_), channel_id=1, source_target_pairs={{0,72},{1,73},{2,74},{3,75},{4,76},{5,77},{6,78},{7,79},{8,64},{9,... | collective-permute-start | bytes 1179656 | tf_op jit(solution)/shard_map/ppermute | solution.py:35
  20.6 1.5 %collective-permute-start.3 = (bf16[128,1536]{1,0:T(8,128)(2,1)S(1)}, bf16[128,1536]{1,0:T(8,128)(2,1)S(1)}, u32[]{:S(2)}, u32[]{:S(2)}) collective-permute-start(bf16[128,1536]{1,0:T(8,128)(2,1)S(1)} %collective-permute-done.refs_0_), channel_id=1, source_target_pairs={{0,48},{1,49},{2,50},{3,51},{4,52},{5,53},{6,54},{7,55},{8,56},{9,... | collective-permute-start | bytes 1179656 | tf_op jit(solution)/shard_map/ppermute | solution.py:35
  22.7 1.1 %collective-permute-done.6.refs_3_ = bf16[128,1536]{1,0:T(8,128)(2,1)S(1)} collective-permute-done((bf16[128,1536]{1,0:T(8,128)(2,1)S(1)}, bf16[128,1536]{1,0:T(8,128)(2,1)S(1)}, u32[]{:S(2)}, u32[]{:S(2)}) %collective-permute-start.6) | collective-permute-done | bytes 393248 | tf_op jit(solution)/shard_map/ppermute | solution.py:35
  23.8 5.0 %shard_map.69 = (f32[1024,2048]{1,0:T(8,128)S(1)}, f32[1024,2048]{1,0:T(8,128)S(1)}, bf16[512,1024]{1,0:T(8,128)(2,1)S(1)}, f32[8,2048]{1,0:T(8,128)S(1)}) custom-call(bf16[128,1536]{1,0:T(8,128)(2,1)S(1)} %collective-permute-done.refs_0_, ...), custom_call_target="tpu_custom_call", output_to_operand_aliasing={{0}: (6, {}), {1}: (7, {}), {2}: (8, {})} | custom-call | flops 3221225472 | bytes 2097152 | tf_op jit(solution)/shard_map/pallas_call | solution.py:60
  28.9 1.4 %shard_map.70 = (f32[1024,2048]{1,0:T(8,128)S(1)}, f32[1024,2048]{1,0:T(8,128)S(1)}, bf16[512,1024]{1,0:T(8,128)(2,1)S(1)}, f32[8,2048]{1,0:T(8,128)S(1)}) custom-call(bf16[128,1536]{1,0:T(8,128)(2,1)S(1)} %collective-permute-done.4.refs_0_, ...), custom_call_target="tpu_custom_call", output_to_operand_aliasing={{0}: (3, {}), {1}: (4, {}), {2}: (5, {})} | custom-call | flops 805306368 | bytes 524288 | tf_op jit(solution)/shard_map/pallas_call | solution.py:60
  30.3 0.9 %collective-permute-done.3.refs_1_ = bf16[128,1536]{1,0:T(8,128)(2,1)S(1)} collective-permute-done((bf16[128,1536]{1,0:T(8,128)(2,1)S(1)}, bf16[128,1536]{1,0:T(8,128)(2,1)S(1)}, u32[]{:S(2)}, u32[]{:S(2)}) %collective-permute-start.3) | collective-permute-done | bytes 393248 | tf_op jit(solution)/shard_map/ppermute | solution.py:35
  31.1 1.0 %collective-permute-done.2.refs_0_ = bf16[128,1536]{1,0:T(8,128)(2,1)S(1)} collective-permute-done((bf16[128,1536]{1,0:T(8,128)(2,1)S(1)}, bf16[128,1536]{1,0:T(8,128)(2,1)S(1)}, u32[]{:S(2)}, u32[]{:S(2)}) %collective-permute-start.2) | collective-permute-done | bytes 393248 | tf_op jit(solution)/shard_map/ppermute | solution.py:35
  32.1 2.5 %shard_map.71 = (f32[1024,2048]{1,0:T(8,128)S(1)}, f32[1024,2048]{1,0:T(8,128)S(1)}, bf16[512,1024]{1,0:T(8,128)(2,1)S(1)}, f32[48,128]{1,0:T(8,128)S(1)}) custom-call(bf16[128,1536]{1,0:T(8,128)(2,1)S(1)} %collective-permute-done.2.refs_0_, ...), custom_call_target="tpu_custom_call", output_to_operand_aliasing={{0}: (4, {}), {1}: (5, {}), {2}: (6, {})} | custom-call | flops 1610612736 | bytes 1048576 | tf_op jit(solution)/shard_map/pallas_call | solution.py:60
  34.7 1.2 %collective-permute-done.7.other = f32[48,128]{1,0:T(8,128)S(1)} collective-permute-done((f32[48,128]{1,0:T(8,128)S(1)}, f32[48,128]{1,0:T(8,128)S(1)}, u32[]{:S(2)}, u32[]{:S(2)}) %collective-permute-start.7) | collective-permute-done | bytes 24608 | tf_op jit(solution)/shard_map/ppermute | solution.py:35
  35.9 11.6 %all_to_all.5.received = f32[8,48,128]{2,1,0:T(8,128)S(1)} all-to-all(f32[8,48,128]{2,1,0:T(8,128)S(1)} %get-tuple-element.73), channel_id=1, replica_groups={{0,2,4,6,8,10,12,14},{1,3,5,7,9,11,13,15},{16,18,20,22,24,26,28,30},{17..., dimensions={0} | all-to-all | bytes 393216 | tf_op jit(solution)/shard_map/all_to_all | solution.py:449
  47.5 1.6 %shard_map.73 = (bf16[8,512,128]{2,1,0:T(8,128)(2,1)S(1)}, bf16[1024,1024]{1,0:T(8,128)(2,1)S(1)}, f32[32,128]{1,0:T(8,128)S(1)}, f32[16,128]{1,0:T(8,128)S(1)},...) custom-call(f32[1024,2048]{1,0:T(8,128)S(1)} %get-tuple-element.70.logit_t, ...), custom_call_target="tpu_custom_call", output_to_operand_aliasing={{4}: (0, {}), {5}: (1, {})} | custom-call | flops 1073741824 | bytes 8388608 | tf_op jit(solution)/shard_map/pallas_call | solution.py:60
  49.4 2.6 %shard_map.74 = (bf16[1024,1024]{1,0:T(8,128)(2,1)S(1)}, f32[256,512]{1,0:T(8,128)S(1)}, bf16[256,512]{1,0:T(8,128)(2,1)S(1)}, bf16[256,512]{1,0:T(8,128)(2,1)S(...) custom-call(f32[1024,2048]{1,0:T(8,128)S(1)} %get-tuple-element.75.logit_t, ...), custom_call_target="tpu_custom_call" | custom-call | flops 2147483648 | bytes 8388608 | tf_op jit(solution)/shard_map/pallas_call | solution.py:60
  52.0 1.5 %collective-permute-start.11 = (bf16[256,512]{1,0:T(8,128)(2,1)S(1)}, bf16[256,512]{1,0:T(8,128)(2,1)S(1)}, u32[]{:S(2)}, u32[]{:S(2)}) collective-permute-start(bf16[256,512]{1,0:T(8,128)(2,1)S(1)} %get-tuple-element.89), channel_id=1, source_target_pairs={{0,16},{1,17},{2,18},{3,19},{4,20},{5,21},{6,22},{7,23},{8,24},{9,... | collective-permute-start | bytes 786440 | tf_op jit(solution)/shard_map/ppermute | solution.py:35
  53.5 1.8 %collective-permute-start.12 = (bf16[256,512]{1,0:T(8,128)(2,1)S(1)}, bf16[256,512]{1,0:T(8,128)(2,1)S(1)}, u32[]{:S(2)}, u32[]{:S(2)}) collective-permute-start(bf16[256,512]{1,0:T(8,128)(2,1)S(1)} %get-tuple-element.90), channel_id=1, source_target_pairs={{0,48},{1,49},{2,50},{3,51},{4,52},{5,53},{6,54},{7,55},{8,56},{9,... | collective-permute-start | bytes 786440 | tf_op jit(solution)/shard_map/ppermute | solution.py:35
  55.4 1.4 %shard_map.75 = (f32[2,512,128]{2,1,0:T(8,128)S(1)}, bf16[2,512,128]{2,1,0:T(8,128)(2,1)S(1)}, bf16[2,512,128]{2,1,0:T(8,128)(2,1)S(1)}, f32[512,128]{1,0:T(8,128)S(1)}, bf16[512,128]{1,0:T(8,128)(2,1)S(1)}) custom-call(bf16[512,1024]{1,0:T(8,128)(2,1)S(1)} %get-tuple-element.72.turned, bf16[1024,1024]{1,0:T(8,128)(2,1)S(1)} %get-tuple-element.79.near, ...), custom_call_target="tpu_custom_call" | custom-call | flops 1073741824 | bytes 2097152 | tf_op jit(solution)/shard_map/pallas_call | solution.py:60
  57.3 0.9 %collective-permute-start.9 = (bf16[2,512,128]{2,1,0:T(8,128)(2,1)S(1)}, bf16[2,512,128]{2,1,0:T(8,128)(2,1)S(1)}, u32[]{:S(2)}, u32[]{:S(2)}) collective-permute-start(bf16[2,512,128]{2,1,0:T(8,128)(2,1)S(1)} %get-tuple-element.81), channel_id=1, source_target_pairs={{0,2},{1,3},{2,4},{3,5},{4,6},{5,7},{6,0},{7,1},{8,10},{9,11},{10,... | collective-permute-start | bytes 786440 | tf_op jit(solution)/shard_map/ppermute | solution.py:35
  58.2 2.4 %collective-permute-start.10 = (bf16[2,512,128]{2,1,0:T(8,128)(2,1)S(1)}, bf16[2,512,128]{2,1,0:T(8,128)(2,1)S(1)}, u32[]{:S(2)}, u32[]{:S(2)}) collective-permute-start(bf16[2,512,128]{2,1,0:T(8,128)(2,1)S(1)} %get-tuple-element.87), channel_id=1, source_target_pairs={{0,6},{1,7},{2,0},{3,1},{4,2},{5,3},{6,4},{7,5},{8,14},{9,15},{10,... | collective-permute-start | bytes 786440 | tf_op jit(solution)/shard_map/ppermute | solution.py:35
  60.6 1.4 %collective-permute-done.11 = bf16[256,512]{1,0:T(8,128)(2,1)S(1)} collective-permute-done((bf16[256,512]{1,0:T(8,128)(2,1)S(1)}, bf16[256,512]{1,0:T(8,128)(2,1)S(1)}, u32[]{:S(2)}, u32[]{:S(2)}) %collective-permute-start.11) | collective-permute-done | bytes 262176 | tf_op jit(solution)/shard_map/ppermute | solution.py:35
  62.1 2.8 %collective-permute-start.16 = (bf16[128,512]{1,0:T(8,128)(2,1)S(1)}, bf16[128,512]{1,0:T(8,128)(2,1)S(1)}, u32[]{:S(2)}, u32[]{:S(2)}) collective-permute-start(bf16[128,512]{1,0:T(8,128)(2,1)S(1)} %get-tuple-element.96), channel_id=1, source_target_pairs={{0,72},{1,73},{2,74},{3,75},{4,76},{5,77},{6,78},{7,79},{8,64},{9,... | collective-permute-start | bytes 393224 | tf_op jit(solution)/shard_map/ppermute | solution.py:35
  64.9 1.0 %collective-permute-start.14 = (bf16[512,128]{1,0:T(8,128)(2,1)S(1)}, bf16[512,128]{1,0:T(8,128)(2,1)S(1)}, u32[]{:S(2)}, u32[]{:S(2)}) collective-permute-start(bf16[512,128]{1,0:T(8,128)(2,1)S(1)} %add_convert_fusion.2), channel_id=1, source_target_pairs={{0,4},{1,5},{2,6},{3,7},{4,0},{5,1},{6,2},{7,3},{8,12},{9,13},{10,... | collective-permute-start | bytes 393224 | tf_op jit(solution)/shard_map/ppermute | solution.py:35
  66.5 2.3 %collective-permute-start.15 = (bf16[512,128]{1,0:T(8,128)(2,1)S(1)}, bf16[512,128]{1,0:T(8,128)(2,1)S(1)}, u32[]{:S(2)}, u32[]{:S(2)}) collective-permute-start(bf16[512,128]{1,0:T(8,128)(2,1)S(1)} %fusion.3), channel_id=1, source_target_pairs={{0,8},{1,9},{2,10},{3,11},{4,12},{5,13},{6,14},{7,15},{8,0},{9,1},... | collective-permute-start | bytes 393224 | tf_op jit(solution)/shard_map/ppermute | solution.py:35
  68.8 2.3 %collective-permute-start.17 = (bf16[128,512]{1,0:T(8,128)(2,1)S(1)}, bf16[128,512]{1,0:T(8,128)(2,1)S(1)}, u32[]{:S(2)}, u32[]{:S(2)}) collective-permute-start(bf16[128,512]{1,0:T(8,128)(2,1)S(1)} %add_convert_fusion.1), channel_id=1, source_target_pairs={{0,32},{1,33},{2,34},{3,35},{4,36},{5,37},{6,38},{7,39},{8,40},{9,... | collective-permute-start | bytes 393224 | tf_op jit(solution)/shard_map/ppermute | solution.py:35
  71.7 3.6 %collective-permute-start.18 = (bf16[128,512]{1,0:T(8,128)(2,1)S(1)}, bf16[128,512]{1,0:T(8,128)(2,1)S(1)}, u32[]{:S(2)}, u32[]{:S(2)}) collective-permute-start(bf16[128,512]{1,0:T(8,128)(2,1)S(1)} %slice.28), channel_id=1, source_target_pairs={{0,72},{1,73},{2,74},{3,75},{4,76},{5,77},{6,78},{7,79},{8,64},{9,... | collective-permute-start | bytes 393224 | tf_op jit(solution)/shard_map/ppermute | solution.py:35
  75.4 0.8 copy.20
  76.2 2.1 %collective-permute-done.18 = bf16[128,512]{1,0:T(8,128)(2,1)S(1)} collective-permute-done((bf16[128,512]{1,0:T(8,128)(2,1)S(1)}, bf16[128,512]{1,0:T(8,128)(2,1)S(1)}, u32[]{:S(2)}, u32[]{:S(2)}) %collective-permute-start.18) | collective-permute-done | bytes 131104 | tf_op jit(solution)/shard_map/ppermute | solution.py:35
  (28 shorter events, 3.9 us)
Async XLA Ops:
  1.6 13.6 %collective-permute-start.1 = (bf16[128,1536]{1,0:T(8,128)(2,1)S(1)}, bf16[128,1536]{1,0:T(8,128)(2,1)S(1)}, u32[]{:S(2)}, u32[]{:S(2)}) collective-permute-start(bf16[128,1536]{1,0:T(8,128)(2,1)S(1)} %shard_map.67.own), channel_id=1, source_target_pairs={{0,32},{1,33},{2,34},{3,35},{4,36},{5,37},{6,38},{7,39},{8,40},{9,... | collective-permute-start | bytes 1179656 | tf_op jit(solution)/shard_map/ppermute | solution.py:35
  4.8 12.9 %collective-permute-start = (bf16[128,1536]{1,0:T(8,128)(2,1)S(1)}, bf16[128,1536]{1,0:T(8,128)(2,1)S(1)}, u32[]{:S(2)}, u32[]{:S(2)}) collective-permute-start(bf16[128,1536]{1,0:T(8,128)(2,1)S(1)} %shard_map.67.own), channel_id=1, source_target_pairs={{0,72},{1,73},{2,74},{3,75},{4,76},{5,77},{6,78},{7,79},{8,64},{9,... | collective-permute-start | bytes 1179656 | tf_op jit(solution)/shard_map/ppermute | solution.py:35
  8.9 14.9 %collective-permute-start.6 = (bf16[128,1536]{1,0:T(8,128)(2,1)S(1)}, bf16[128,1536]{1,0:T(8,128)(2,1)S(1)}, u32[]{:S(2)}, u32[]{:S(2)}) collective-permute-start(bf16[128,1536]{1,0:T(8,128)(2,1)S(1)} %shard_map.67.own), channel_id=1, source_target_pairs={{0,48},{1,49},{2,50},{3,51},{4,52},{5,53},{6,54},{7,55},{8,56},{9,... | collective-permute-start | bytes 1179656 | tf_op jit(solution)/shard_map/ppermute | solution.py:35
  10.0 13.8 %collective-permute-start.5 = (bf16[128,1536]{1,0:T(8,128)(2,1)S(1)}, bf16[128,1536]{1,0:T(8,128)(2,1)S(1)}, u32[]{:S(2)}, u32[]{:S(2)}) collective-permute-start(bf16[128,1536]{1,0:T(8,128)(2,1)S(1)} %shard_map.67.own), channel_id=1, source_target_pairs={{0,16},{1,17},{2,18},{3,19},{4,20},{5,21},{6,22},{7,23},{8,24},{9,... | collective-permute-start | bytes 1179656 | tf_op jit(solution)/shard_map/ppermute | solution.py:35
  17.7 11.2 %collective-permute-start.4 = (bf16[128,1536]{1,0:T(8,128)(2,1)S(1)}, bf16[128,1536]{1,0:T(8,128)(2,1)S(1)}, u32[]{:S(2)}, u32[]{:S(2)}) collective-permute-start(bf16[128,1536]{1,0:T(8,128)(2,1)S(1)} %collective-permute-done.1.refs_1_), channel_id=1, source_target_pairs={{0,72},{1,73},{2,74},{3,75},{4,76},{5,77},{6,78},{7,79},{8,64},{9,... | collective-permute-start | bytes 1179656 | tf_op jit(solution)/shard_map/ppermute | solution.py:35
  20.6 10.5 %collective-permute-start.3 = (bf16[128,1536]{1,0:T(8,128)(2,1)S(1)}, bf16[128,1536]{1,0:T(8,128)(2,1)S(1)}, u32[]{:S(2)}, u32[]{:S(2)}) collective-permute-start(bf16[128,1536]{1,0:T(8,128)(2,1)S(1)} %collective-permute-done.refs_0_), channel_id=1, source_target_pairs={{0,48},{1,49},{2,50},{3,51},{4,52},{5,53},{6,54},{7,55},{8,56},{9,... | collective-permute-start | bytes 1179656 | tf_op jit(solution)/shard_map/ppermute | solution.py:35
  22.2 10.0 %collective-permute-start.2 = (bf16[128,1536]{1,0:T(8,128)(2,1)S(1)}, bf16[128,1536]{1,0:T(8,128)(2,1)S(1)}, u32[]{:S(2)}, u32[]{:S(2)}) collective-permute-start(bf16[128,1536]{1,0:T(8,128)(2,1)S(1)} %collective-permute-done.refs_0_), channel_id=1, source_target_pairs={{0,16},{1,17},{2,18},{3,19},{4,20},{5,21},{6,22},{7,23},{8,24},{9,... | collective-permute-start | bytes 1179656 | tf_op jit(solution)/shard_map/ppermute | solution.py:35
  34.6 1.3 %collective-permute-start.7 = (f32[48,128]{1,0:T(8,128)S(1)}, f32[48,128]{1,0:T(8,128)S(1)}, u32[]{:S(2)}, u32[]{:S(2)}) collective-permute-start(f32[48,128]{1,0:T(8,128)S(1)} %get-tuple-element.67.mine), channel_id=1, source_target_pairs={{0,1},{1,0},{2,3},{3,2},{4,5},{5,4},{6,7},{7,6},{8,9},{9,8},{10,11... | collective-permute-start | bytes 73736 | tf_op jit(solution)/shard_map/ppermute | solution.py:35
  47.5 1.9 %copy-start = (bf16[2048,512]{1,0:T(8,128)(2,1)S(1)}, bf16[2048,512]{1,0:T(8,128)(2,1)}, u32[]{:S(2)}) copy-start(bf16[2048,512]{1,0:T(8,128)(2,1)} %param.6) | copy-start | bytes 6291460
  49.1 6.3 %collective-permute-start.8 = (bf16[8,512,128]{2,1,0:T(8,128)(2,1)S(1)}, bf16[8,512,128]{2,1,0:T(8,128)(2,1)S(1)}, u32[]{:S(2)}, u32[]{:S(2)}) collective-permute-start(bf16[8,512,128]{2,1,0:T(8,128)(2,1)S(1)} %get-tuple-element.80), channel_id=1, source_target_pairs={{0,1},{1,0},{2,3},{3,2},{4,5},{5,4},{6,7},{7,6},{8,9},{9,8},{10,11... | collective-permute-start | bytes 3145736 | tf_op jit(solution)/shard_map/ppermute | solution.py:35
  52.0 10.0 %collective-permute-start.11 = (bf16[256,512]{1,0:T(8,128)(2,1)S(1)}, bf16[256,512]{1,0:T(8,128)(2,1)S(1)}, u32[]{:S(2)}, u32[]{:S(2)}) collective-permute-start(bf16[256,512]{1,0:T(8,128)(2,1)S(1)} %get-tuple-element.89), channel_id=1, source_target_pairs={{0,16},{1,17},{2,18},{3,19},{4,20},{5,21},{6,22},{7,23},{8,24},{9,... | collective-permute-start | bytes 786440 | tf_op jit(solution)/shard_map/ppermute | solution.py:35
  53.5 8.5 %collective-permute-start.12 = (bf16[256,512]{1,0:T(8,128)(2,1)S(1)}, bf16[256,512]{1,0:T(8,128)(2,1)S(1)}, u32[]{:S(2)}, u32[]{:S(2)}) collective-permute-start(bf16[256,512]{1,0:T(8,128)(2,1)S(1)} %get-tuple-element.90), channel_id=1, source_target_pairs={{0,48},{1,49},{2,50},{3,51},{4,52},{5,53},{6,54},{7,55},{8,56},{9,... | collective-permute-start | bytes 786440 | tf_op jit(solution)/shard_map/ppermute | solution.py:35
  56.7 8.1 %collective-permute-start.13 = (bf16[512,128]{1,0:T(8,128)(2,1)S(1)}, bf16[512,128]{1,0:T(8,128)(2,1)S(1)}, u32[]{:S(2)}, u32[]{:S(2)}) collective-permute-start(bf16[512,128]{1,0:T(8,128)(2,1)S(1)} %get-tuple-element.93), channel_id=1, source_target_pairs={{0,8},{1,9},{2,10},{3,11},{4,12},{5,13},{6,14},{7,15},{8,0},{9,1},... | collective-permute-start | bytes 393224 | tf_op jit(solution)/shard_map/ppermute | solution.py:35
  57.3 9.1 %collective-permute-start.9 = (bf16[2,512,128]{2,1,0:T(8,128)(2,1)S(1)}, bf16[2,512,128]{2,1,0:T(8,128)(2,1)S(1)}, u32[]{:S(2)}, u32[]{:S(2)}) collective-permute-start(bf16[2,512,128]{2,1,0:T(8,128)(2,1)S(1)} %get-tuple-element.81), channel_id=1, source_target_pairs={{0,2},{1,3},{2,4},{3,5},{4,6},{5,7},{6,0},{7,1},{8,10},{9,11},{10,... | collective-permute-start | bytes 786440 | tf_op jit(solution)/shard_map/ppermute | solution.py:35
  58.2 8.2 %collective-permute-start.10 = (bf16[2,512,128]{2,1,0:T(8,128)(2,1)S(1)}, bf16[2,512,128]{2,1,0:T(8,128)(2,1)S(1)}, u32[]{:S(2)}, u32[]{:S(2)}) collective-permute-start(bf16[2,512,128]{2,1,0:T(8,128)(2,1)S(1)} %get-tuple-element.87), channel_id=1, source_target_pairs={{0,6},{1,7},{2,0},{3,1},{4,2},{5,3},{6,4},{7,5},{8,14},{9,15},{10,... | collective-permute-start | bytes 786440 | tf_op jit(solution)/shard_map/ppermute | solution.py:35
  62.1 6.7 %collective-permute-start.16 = (bf16[128,512]{1,0:T(8,128)(2,1)S(1)}, bf16[128,512]{1,0:T(8,128)(2,1)S(1)}, u32[]{:S(2)}, u32[]{:S(2)}) collective-permute-start(bf16[128,512]{1,0:T(8,128)(2,1)S(1)} %get-tuple-element.96), channel_id=1, source_target_pairs={{0,72},{1,73},{2,74},{3,75},{4,76},{5,77},{6,78},{7,79},{8,64},{9,... | collective-permute-start | bytes 393224 | tf_op jit(solution)/shard_map/ppermute | solution.py:35
  64.9 10.4 %collective-permute-start.14 = (bf16[512,128]{1,0:T(8,128)(2,1)S(1)}, bf16[512,128]{1,0:T(8,128)(2,1)S(1)}, u32[]{:S(2)}, u32[]{:S(2)}) collective-permute-start(bf16[512,128]{1,0:T(8,128)(2,1)S(1)} %add_convert_fusion.2), channel_id=1, source_target_pairs={{0,4},{1,5},{2,6},{3,7},{4,0},{5,1},{6,2},{7,3},{8,12},{9,13},{10,... | collective-permute-start | bytes 393224 | tf_op jit(solution)/shard_map/ppermute | solution.py:35
  66.5 8.8 %collective-permute-start.15 = (bf16[512,128]{1,0:T(8,128)(2,1)S(1)}, bf16[512,128]{1,0:T(8,128)(2,1)S(1)}, u32[]{:S(2)}, u32[]{:S(2)}) collective-permute-start(bf16[512,128]{1,0:T(8,128)(2,1)S(1)} %fusion.3), channel_id=1, source_target_pairs={{0,8},{1,9},{2,10},{3,11},{4,12},{5,13},{6,14},{7,15},{8,0},{9,1},... | collective-permute-start | bytes 393224 | tf_op jit(solution)/shard_map/ppermute | solution.py:35
  68.8 7.4 %collective-permute-start.17 = (bf16[128,512]{1,0:T(8,128)(2,1)S(1)}, bf16[128,512]{1,0:T(8,128)(2,1)S(1)}, u32[]{:S(2)}, u32[]{:S(2)}) collective-permute-start(bf16[128,512]{1,0:T(8,128)(2,1)S(1)} %add_convert_fusion.1), channel_id=1, source_target_pairs={{0,32},{1,33},{2,34},{3,35},{4,36},{5,37},{6,38},{7,39},{8,40},{9,... | collective-permute-start | bytes 393224 | tf_op jit(solution)/shard_map/ppermute | solution.py:35
  71.7 6.6 %collective-permute-start.18 = (bf16[128,512]{1,0:T(8,128)(2,1)S(1)}, bf16[128,512]{1,0:T(8,128)(2,1)S(1)}, u32[]{:S(2)}, u32[]{:S(2)}) collective-permute-start(bf16[128,512]{1,0:T(8,128)(2,1)S(1)} %slice.28), channel_id=1, source_target_pairs={{0,72},{1,73},{2,74},{3,75},{4,76},{5,77},{6,78},{7,79},{8,64},{9,... | collective-permute-start | bytes 393224 | tf_op jit(solution)/shard_map/ppermute | solution.py:35

commit v5 on v4

--- a/solution.py
+++ b/solution.py
@@ -60,8 +60,10 @@
     return pl.pallas_call(
         body,
         in_specs=specs,
-        out_specs=[pl.BlockSpec(memory_space=VMEM)] * len(out_shape),
-        out_shape=[VMEM(*s) for s in out_shape],
+        out_specs=[
+            pl.BlockSpec(memory_space=VMEM if isinstance(s, tuple) else pltpu.HBM) for s in out_shape
+        ],
+        out_shape=[VMEM(*s) if isinstance(s, tuple) else s for s in out_shape],
         compiler_params=pltpu.CompilerParams(vmem_limit_bytes=limit * MIB),
         cost_estimate=pl.CostEstimate(flops=flops, bytes_accessed=size, transcendentals=exps),
         **more,
@@ -341,7 +343,10 @@
     )
 
 
-def near_kernel(scale, logit_t, logit_s, lse, away, image_s, near, *texts):
+def near_kernel(scale, logit_t, logit_s, lse, away, image_s, loss, near, *refs):
+    texts, out_loss, sem = refs[:-2], refs[-2], refs[-1]
+    copy = pltpu.make_async_copy(loss, out_loss, sem)
+    copy.start()
     core = lax.rem(lax.axis_index("grp"), 2)
     blocks, _, block, width = image_s.shape
     rows = blocks * block
@@ -359,23 +364,26 @@
             jnp.dot(away[span, :], image_away, preferred_element_type=F32)
             + jnp.dot(near[span, :], image_near, preferred_element_type=F32)
         ).astype(out.dtype)
-
-
-def near_part(logit_t, logit_s, lse, away, image_s):
+    copy.wait()
+
+
+def near_part(logit_t, logit_s, lse, away, image_s, loss):
     count, rows = logit_t.shape
     width = image_s.shape[3]
     return call(
         functools.partial(near_kernel, 3.0 / math.sqrt(width)),
-        [(VMEM, v) for v in (logit_t, logit_s, lse, away, image_s)],
+        [(VMEM, v) for v in (logit_t, logit_s, lse, away, image_s, loss)],
         [(away.shape, BF16)]
         + [
             ((count // part, width), kind)
-            for part, kind in ((4, F32), (4, BF16), (4, BF16), (8, F32), (8, BF16))
-        ],
+            for part, kind in ((4, F32), (4, BF16), (4, BF16), (4, BF16))
+        ]
+        + [jax.ShapeDtypeStruct(loss.shape, F32)],
         10,
         flops=2 * count * rows * width,
         size=4 * count * rows,
         exps=count * rows,
+        scratch_shapes=[pltpu.SemaphoreType.DMA(())],
     )
 
 
@@ -451,24 +459,23 @@
         logit_t, logit_s, turned, received
     )
     from_core = permute(grad_other, other_core)
-    near, *texts = near_part(logit_t, logit_s, lse, away, image_s)
+    near, *texts, row_loss = near_part(logit_t, logit_s, lse, away, image_s, row_loss)
     image_kept, image_up, image_down, image_far, far_flip = image_part(turned, near, from_core)
     from_flip = permute(far_flip, along_y(0, 1))
     from_down, from_up = permute(image_up, along_y(1)), permute(image_down, along_y(3))
-    text_kept, text_left, text_right, text_far, far_cross = texts
-    far_cross, image_kept = lax.optimization_barrier((far_cross, image_kept))
-    from_cross = permute(far_cross, cross_z)
+    text_kept, text_left, text_right, text_far = texts
     from_right, from_left = permute(text_left, along_x(3)), permute(text_right, along_x(1))
     image_far = permute((image_far + from_flip.astype(F32)).astype(BF16), along_y(2))
-    text_far = permute((text_far + from_cross.astype(F32)).astype(BF16), along_x(2))
-    row_loss, from_down = lax.optimization_barrier((row_loss, from_down))
+    text_far, from_left, from_right, image_kept = lax.optimization_barrier(
+        (text_far, from_left, from_right, image_kept)
+    )
+    from_far = permute(text_far, along_x(2))
     image_sum = total([image_kept, from_down, from_up])
-    text_sum = total([text_kept, from_left, from_right])
-    image_sum, text_sum = lax.optimization_barrier((image_sum, text_sum))
     from_z = permute(image_sum[1].astype(BF16), along_y(0, 1))
+    text_sum = total([text_kept, from_left, from_right, from_far])
     from_across = permute(text_sum[n:].astype(BF16), cross_z)
     grad_image = total([image_sum[0], image_far, from_z]).T.astype(BF16)
-    grad_text = total([text_sum[:n], text_far, from_across]).astype(BF16)
+    grad_text = total([text_sum[:n], from_across]).astype(BF16)
     return row_loss.reshape(-1), grad_image, grad_text
 
 

time: 79.7 us -> 79 us (level)
  waiting for transfers between devices: 10.7 us -> 12.8 us
  starting transfers between devices: 33.7 us -> 31.8 us
    ppermute x19 -> x18, waiting for transfers between devices: 10.7 us -> 12.8 us  [permute(): lax.ppermute(v, AXES, [(i, index(*move(*place(i)))) for i in range(128)])]
    ppermute x19 -> x18, starting transfers between devices: 33.7 us -> 31.8 us  [permute(): lax.ppermute(v, AXES, [(i, index(*move(*place(i)))) for i in range(128)])]
  transfers between devices with their start and end apart: 19 -> 18, of which waited for: 9 -> 10; matrix products, arithmetic and copies ran while one was open for 2% -> 1% of each run, Pallas kernels for 19% -> 19%
where the time goes in v5:
time: 79 us; the launch traced here: 78.9 us
  starting transfers between devices  31.8 us (40%)
  Pallas kernels  20.1 us (25%)
  waiting for transfers between devices  12.8 us (16%)
  blocking collectives  11.6 us (15%)
  other arithmetic  0.96 us (1%)
  local copies, waits for them, and re-layouts  0.81 us (1%)
    ppermute x18, starting transfers between devices, permute(): lax.ppermute(v, AXES, [(i, index(*move(*place(i)))) for i in range(128)])  31.8 us
    pallas_call x9, Pallas kernels, call(): pl.pallas_call(body, in_specs=specs, out_specs=[pl.BlockSpec(memory_space...  20.1 us
    ppermute x18, waiting for transfers between devices, permute(): lax.ppermute(v, AXES, [(i, index(*move(*place(i)))) for i in range(128)])  12.8 us
    all_to_all x1, blocking collectives, shards(): lax.all_to_all(stats, 'grp', 0, 0, tiled=True, axis_index_groups=peers)  11.6 us
  transfers between devices with their start and end apart: 18, of which 10 were waited for; matrix products, arithmetic and copies ran while one was open for 1% of the time, Pallas kernels for 19%

profile of v5, /device:TPU:0, one launch (start us, length us, event | category | flops | bytes accessed | tf_op | source)
XLA Modules:
  0.0 78.9 jit_solution(13707914013198011559)
XLA Ops:
  0.6 1.0 %shard_map.67.own = bf16[128,1536]{1,0:T(8,128)(2,1)S(1)} custom-call(bf16[128,1024]{1,0:T(8,128)(2,1)} %text_t.1, bf16[128,512]{1,0:T(8,128)(2,1)} %text_s.1), custom_call_target="tpu_custom_call" | custom-call | tf_op jit(solution)/shard_map/pallas_call | solution.py:60
  1.6 3.2 %collective-permute-start.1 = (bf16[128,1536]{1,0:T(8,128)(2,1)S(1)}, bf16[128,1536]{1,0:T(8,128)(2,1)S(1)}, u32[]{:S(2)}, u32[]{:S(2)}) collective-permute-start(bf16[128,1536]{1,0:T(8,128)(2,1)S(1)} %shard_map.67.own), channel_id=1, source_target_pairs={{0,32},{1,33},{2,34},{3,35},{4,36},{5,37},{6,38},{7,39},{8,40},{9,... | collective-permute-start | bytes 1179656 | tf_op jit(solution)/shard_map/ppermute | solution.py:35
  4.8 4.0 %collective-permute-start = (bf16[128,1536]{1,0:T(8,128)(2,1)S(1)}, bf16[128,1536]{1,0:T(8,128)(2,1)S(1)}, u32[]{:S(2)}, u32[]{:S(2)}) collective-permute-start(bf16[128,1536]{1,0:T(8,128)(2,1)S(1)} %shard_map.67.own), channel_id=1, source_target_pairs={{0,72},{1,73},{2,74},{3,75},{4,76},{5,77},{6,78},{7,79},{8,64},{9,... | collective-permute-start | bytes 1179656 | tf_op jit(solution)/shard_map/ppermute | solution.py:35
  8.9 1.1 %collective-permute-start.6 = (bf16[128,1536]{1,0:T(8,128)(2,1)S(1)}, bf16[128,1536]{1,0:T(8,128)(2,1)S(1)}, u32[]{:S(2)}, u32[]{:S(2)}) collective-permute-start(bf16[128,1536]{1,0:T(8,128)(2,1)S(1)} %shard_map.67.own), channel_id=1, source_target_pairs={{0,48},{1,49},{2,50},{3,51},{4,52},{5,53},{6,54},{7,55},{8,56},{9,... | collective-permute-start | bytes 1179656 | tf_op jit(solution)/shard_map/ppermute | solution.py:35
  10.0 0.9 %collective-permute-start.5 = (bf16[128,1536]{1,0:T(8,128)(2,1)S(1)}, bf16[128,1536]{1,0:T(8,128)(2,1)S(1)}, u32[]{:S(2)}, u32[]{:S(2)}) collective-permute-start(bf16[128,1536]{1,0:T(8,128)(2,1)S(1)} %shard_map.67.own), channel_id=1, source_target_pairs={{0,16},{1,17},{2,18},{3,19},{4,20},{5,21},{6,22},{7,23},{8,24},{9,... | collective-permute-start | bytes 1179656 | tf_op jit(solution)/shard_map/ppermute | solution.py:35
  10.9 4.4 %shard_map.68 = (bf16[1024,2048]{1,0:T(8,128)(2,1)S(1)}, bf16[512,2048]{1,0:T(8,128)(2,1)S(1)}, f32[1024,2048]{1,0:T(8,128)S(1)}, f32[1024,2048]{1,0:T(8,128)S(1...) custom-call(bf16[128,1536]{1,0:T(8,128)(2,1)S(1)} %shard_map.67.own, bf16[8,2,128,1024]{3,2,1,0:T(8,128)(2,1)} %bitcast.19, ...), custom_call_target="tpu_custom_call" | custom-call | flops 805306368 | bytes 6291456 | tf_op jit(solution)/shard_map/pallas_call | solution.py:60
  15.3 2.4 %collective-permute-done.refs_0_ = bf16[128,1536]{1,0:T(8,128)(2,1)S(1)} collective-permute-done((bf16[128,1536]{1,0:T(8,128)(2,1)S(1)}, bf16[128,1536]{1,0:T(8,128)(2,1)S(1)}, u32[]{:S(2)}, u32[]{:S(2)}) %collective-permute-start) | collective-permute-done | bytes 393248 | tf_op jit(solution)/shard_map/ppermute | solution.py:35
  17.7 3.0 %collective-permute-start.4 = (bf16[128,1536]{1,0:T(8,128)(2,1)S(1)}, bf16[128,1536]{1,0:T(8,128)(2,1)S(1)}, u32[]{:S(2)}, u32[]{:S(2)}) collective-permute-start(bf16[128,1536]{1,0:T(8,128)(2,1)S(1)} %collective-permute-done.1.refs_1_), channel_id=1, source_target_pairs={{0,72},{1,73},{2,74},{3,75},{4,76},{5,77},{6,78},{7,79},{8,64},{9,... | collective-permute-start | bytes 1179656 | tf_op jit(solution)/shard_map/ppermute | solution.py:35
  20.6 1.5 %collective-permute-start.3 = (bf16[128,1536]{1,0:T(8,128)(2,1)S(1)}, bf16[128,1536]{1,0:T(8,128)(2,1)S(1)}, u32[]{:S(2)}, u32[]{:S(2)}) collective-permute-start(bf16[128,1536]{1,0:T(8,128)(2,1)S(1)} %collective-permute-done.refs_0_), channel_id=1, source_target_pairs={{0,48},{1,49},{2,50},{3,51},{4,52},{5,53},{6,54},{7,55},{8,56},{9,... | collective-permute-start | bytes 1179656 | tf_op jit(solution)/shard_map/ppermute | solution.py:35
  22.7 1.1 %collective-permute-done.6.refs_3_ = bf16[128,1536]{1,0:T(8,128)(2,1)S(1)} collective-permute-done((bf16[128,1536]{1,0:T(8,128)(2,1)S(1)}, bf16[128,1536]{1,0:T(8,128)(2,1)S(1)}, u32[]{:S(2)}, u32[]{:S(2)}) %collective-permute-start.6) | collective-permute-done | bytes 393248 | tf_op jit(solution)/shard_map/ppermute | solution.py:35
  23.8 5.0 %shard_map.69 = (f32[1024,2048]{1,0:T(8,128)S(1)}, f32[1024,2048]{1,0:T(8,128)S(1)}, bf16[512,1024]{1,0:T(8,128)(2,1)S(1)}, f32[8,2048]{1,0:T(8,128)S(1)}) custom-call(bf16[128,1536]{1,0:T(8,128)(2,1)S(1)} %collective-permute-done.refs_0_, ...), custom_call_target="tpu_custom_call", output_to_operand_aliasing={{0}: (6, {}), {1}: (7, {}), {2}: (8, {})} | custom-call | flops 3221225472 | bytes 2097152 | tf_op jit(solution)/shard_map/pallas_call | solution.py:60
  28.9 1.4 %shard_map.70 = (f32[1024,2048]{1,0:T(8,128)S(1)}, f32[1024,2048]{1,0:T(8,128)S(1)}, bf16[512,1024]{1,0:T(8,128)(2,1)S(1)}, f32[8,2048]{1,0:T(8,128)S(1)}) custom-call(bf16[128,1536]{1,0:T(8,128)(2,1)S(1)} %collective-permute-done.4.refs_0_, ...), custom_call_target="tpu_custom_call", output_to_operand_aliasing={{0}: (3, {}), {1}: (4, {}), {2}: (5, {})} | custom-call | flops 805306368 | bytes 524288 | tf_op jit(solution)/shard_map/pallas_call | solution.py:60
  30.3 0.9 %collective-permute-done.3.refs_1_ = bf16[128,1536]{1,0:T(8,128)(2,1)S(1)} collective-permute-done((bf16[128,1536]{1,0:T(8,128)(2,1)S(1)}, bf16[128,1536]{1,0:T(8,128)(2,1)S(1)}, u32[]{:S(2)}, u32[]{:S(2)}) %collective-permute-start.3) | collective-permute-done | bytes 393248 | tf_op jit(solution)/shard_map/ppermute | solution.py:35
  31.1 1.0 %collective-permute-done.2.refs_0_ = bf16[128,1536]{1,0:T(8,128)(2,1)S(1)} collective-permute-done((bf16[128,1536]{1,0:T(8,128)(2,1)S(1)}, bf16[128,1536]{1,0:T(8,128)(2,1)S(1)}, u32[]{:S(2)}, u32[]{:S(2)}) %collective-permute-start.2) | collective-permute-done | bytes 393248 | tf_op jit(solution)/shard_map/ppermute | solution.py:35
  32.1 2.5 %shard_map.71 = (f32[1024,2048]{1,0:T(8,128)S(1)}, f32[1024,2048]{1,0:T(8,128)S(1)}, bf16[512,1024]{1,0:T(8,128)(2,1)S(1)}, f32[48,128]{1,0:T(8,128)S(1)}) custom-call(bf16[128,1536]{1,0:T(8,128)(2,1)S(1)} %collective-permute-done.2.refs_0_, ...), custom_call_target="tpu_custom_call", output_to_operand_aliasing={{0}: (4, {}), {1}: (5, {}), {2}: (6, {})} | custom-call | flops 1610612736 | bytes 1048576 | tf_op jit(solution)/shard_map/pallas_call | solution.py:60
  34.7 1.2 %collective-permute-done.7.other = f32[48,128]{1,0:T(8,128)S(1)} collective-permute-done((f32[48,128]{1,0:T(8,128)S(1)}, f32[48,128]{1,0:T(8,128)S(1)}, u32[]{:S(2)}, u32[]{:S(2)}) %collective-permute-start.7) | collective-permute-done | bytes 24608 | tf_op jit(solution)/shard_map/ppermute | solution.py:35
  35.9 11.6 %all_to_all.5.received = f32[8,48,128]{2,1,0:T(8,128)S(1)} all-to-all(f32[8,48,128]{2,1,0:T(8,128)S(1)} %get-tuple-element.71), channel_id=1, replica_groups={{0,2,4,6,8,10,12,14},{1,3,5,7,9,11,13,15},{16,18,20,22,24,26,28,30},{17..., dimensions={0} | all-to-all | bytes 393216 | tf_op jit(solution)/shard_map/all_to_all | solution.py:457
  47.5 1.6 %shard_map.73 = (bf16[8,512,128]{2,1,0:T(8,128)(2,1)S(1)}, bf16[1024,1024]{1,0:T(8,128)(2,1)S(1)}, f32[32,128]{1,0:T(8,128)S(1)}, f32[16,128]{1,0:T(8,128)S(1)},...) custom-call(f32[1024,2048]{1,0:T(8,128)S(1)} %get-tuple-element.68.logit_t, ...), custom_call_target="tpu_custom_call", output_to_operand_aliasing={{4}: (0, {}), {5}: (1, {})} | custom-call | flops 1073741824 | bytes 8388608 | tf_op jit(solution)/shard_map/pallas_call | solution.py:60
  49.4 3.0 %shard_map.74 = (bf16[1024,1024]{1,0:T(8,128)(2,1)S(1)}, f32[256,512]{1,0:T(8,128)S(1)}, bf16[256,512]{1,0:T(8,128)(2,1)S(1)}, bf16[256,512]{1,0:T(8,128)(2,1)S(...) custom-call(f32[1024,2048]{1,0:T(8,128)S(1)} %get-tuple-element.72.logit_t, ...), custom_call_target="tpu_custom_call" | custom-call | flops 2147483648 | bytes 8388608 | tf_op jit(solution)/shard_map/pallas_call | solution.py:60
  52.4 1.5 %collective-permute-start.8 = (bf16[256,512]{1,0:T(8,128)(2,1)S(1)}, bf16[256,512]{1,0:T(8,128)(2,1)S(1)}, u32[]{:S(2)}, u32[]{:S(2)}) collective-permute-start(bf16[256,512]{1,0:T(8,128)(2,1)S(1)} %get-tuple-element.79), channel_id=1, source_target_pairs={{0,16},{1,17},{2,18},{3,19},{4,20},{5,21},{6,22},{7,23},{8,24},{9,... | collective-permute-start | bytes 786440 | tf_op jit(solution)/shard_map/ppermute | solution.py:35
  53.9 1.8 %collective-permute-start.9 = (bf16[256,512]{1,0:T(8,128)(2,1)S(1)}, bf16[256,512]{1,0:T(8,128)(2,1)S(1)}, u32[]{:S(2)}, u32[]{:S(2)}) collective-permute-start(bf16[256,512]{1,0:T(8,128)(2,1)S(1)} %get-tuple-element.80), channel_id=1, source_target_pairs={{0,48},{1,49},{2,50},{3,51},{4,52},{5,53},{6,54},{7,55},{8,56},{9,... | collective-permute-start | bytes 786440 | tf_op jit(solution)/shard_map/ppermute | solution.py:35
  55.7 1.4 %shard_map.75 = (f32[2,512,128]{2,1,0:T(8,128)S(1)}, bf16[2,512,128]{2,1,0:T(8,128)(2,1)S(1)}, bf16[2,512,128]{2,1,0:T(8,128)(2,1)S(1)}, f32[512,128]{1,0:T(8,128)S(1)}, bf16[512,128]{1,0:T(8,128)(2,1)S(1)}) custom-call(bf16[512,1024]{1,0:T(8,128)(2,1)S(1)} %get-tuple-element.70.turned, bf16[1024,1024]{1,0:T(8,128)(2,1)S(1)} %get-tuple-element.81.near, ...), custom_call_target="tpu_custom_call" | custom-call | flops 1073741824 | bytes 2097152 | tf_op jit(solution)/shard_map/pallas_call | solution.py:60
  57.7 0.9 %collective-permute-start.11 = (bf16[2,512,128]{2,1,0:T(8,128)(2,1)S(1)}, bf16[2,512,128]{2,1,0:T(8,128)(2,1)S(1)}, u32[]{:S(2)}, u32[]{:S(2)}) collective-permute-start(bf16[2,512,128]{2,1,0:T(8,128)(2,1)S(1)} %get-tuple-element.85), channel_id=1, source_target_pairs={{0,2},{1,3},{2,4},{3,5},{4,6},{5,7},{6,0},{7,1},{8,10},{9,11},{10,... | collective-permute-start | bytes 786440 | tf_op jit(solution)/shard_map/ppermute | solution.py:35
  58.5 2.4 %collective-permute-start.12 = (bf16[2,512,128]{2,1,0:T(8,128)(2,1)S(1)}, bf16[2,512,128]{2,1,0:T(8,128)(2,1)S(1)}, u32[]{:S(2)}, u32[]{:S(2)}) collective-permute-start(bf16[2,512,128]{2,1,0:T(8,128)(2,1)S(1)} %get-tuple-element.86), channel_id=1, source_target_pairs={{0,6},{1,7},{2,0},{3,1},{4,2},{5,3},{6,4},{7,5},{8,14},{9,15},{10,... | collective-permute-start | bytes 786440 | tf_op jit(solution)/shard_map/ppermute | solution.py:35
  60.9 1.4 %collective-permute-done.8 = bf16[256,512]{1,0:T(8,128)(2,1)S(1)} collective-permute-done((bf16[256,512]{1,0:T(8,128)(2,1)S(1)}, bf16[256,512]{1,0:T(8,128)(2,1)S(1)}, u32[]{:S(2)}, u32[]{:S(2)}) %collective-permute-start.8) | collective-permute-done | bytes 262176 | tf_op jit(solution)/shard_map/ppermute | solution.py:35
  62.3 2.6 %collective-permute-start.16 = (bf16[256,512]{1,0:T(8,128)(2,1)S(1)}, bf16[256,512]{1,0:T(8,128)(2,1)S(1)}, u32[]{:S(2)}, u32[]{:S(2)}) collective-permute-start(bf16[256,512]{1,0:T(8,128)(2,1)S(1)} %get-tuple-element.92), channel_id=1, source_target_pairs={{0,32},{1,33},{2,34},{3,35},{4,36},{5,37},{6,38},{7,39},{8,40},{9,... | collective-permute-start | bytes 786440 | tf_op jit(solution)/shard_map/ppermute | solution.py:35
  65.0 1.0 %collective-permute-start.14 = (bf16[512,128]{1,0:T(8,128)(2,1)S(1)}, bf16[512,128]{1,0:T(8,128)(2,1)S(1)}, u32[]{:S(2)}, u32[]{:S(2)}) collective-permute-start(bf16[512,128]{1,0:T(8,128)(2,1)S(1)} %add_convert_fusion), channel_id=1, source_target_pairs={{0,4},{1,5},{2,6},{3,7},{4,0},{5,1},{6,2},{7,3},{8,12},{9,13},{10,... | collective-permute-start | bytes 393224 | tf_op jit(solution)/shard_map/ppermute | solution.py:35
  66.9 3.6 %collective-permute-start.15 = (bf16[512,128]{1,0:T(8,128)(2,1)S(1)}, bf16[512,128]{1,0:T(8,128)(2,1)S(1)}, u32[]{:S(2)}, u32[]{:S(2)}) collective-permute-start(bf16[512,128]{1,0:T(8,128)(2,1)S(1)} %fusion.5), channel_id=1, source_target_pairs={{0,8},{1,9},{2,10},{3,11},{4,12},{5,13},{6,14},{7,15},{8,0},{9,1},... | collective-permute-start | bytes 393224 | tf_op jit(solution)/shard_map/ppermute | solution.py:35
  70.5 1.3 %collective-permute-done.16 = bf16[256,512]{1,0:T(8,128)(2,1)S(1)} collective-permute-done((bf16[256,512]{1,0:T(8,128)(2,1)S(1)}, bf16[256,512]{1,0:T(8,128)(2,1)S(1)}, u32[]{:S(2)}, u32[]{:S(2)}) %collective-permute-start.16) | collective-permute-done | bytes 262176 | tf_op jit(solution)/shard_map/ppermute | solution.py:35
  71.9 2.8 %collective-permute-start.17 = (bf16[128,512]{1,0:T(8,128)(2,1)S(1)}, bf16[128,512]{1,0:T(8,128)(2,1)S(1)}, u32[]{:S(2)}, u32[]{:S(2)}) collective-permute-start(bf16[128,512]{1,0:T(8,128)(2,1)S(1)} %slice.38), channel_id=1, source_target_pairs={{0,72},{1,73},{2,74},{3,75},{4,76},{5,77},{6,78},{7,79},{8,64},{9,... | collective-permute-start | bytes 393224 | tf_op jit(solution)/shard_map/ppermute | solution.py:35
  74.7 0.8 copy.20
  75.5 2.7 %collective-permute-done.17 = bf16[128,512]{1,0:T(8,128)(2,1)S(1)} collective-permute-done((bf16[128,512]{1,0:T(8,128)(2,1)S(1)}, bf16[128,512]{1,0:T(8,128)(2,1)S(1)}, u32[]{:S(2)}, u32[]{:S(2)}) %collective-permute-start.17) | collective-permute-done | bytes 131104 | tf_op jit(solution)/shard_map/ppermute | solution.py:35
  (24 shorter events, 3.5 us)
Async XLA Ops:
  1.6 13.6 %collective-permute-start.1 = (bf16[128,1536]{1,0:T(8,128)(2,1)S(1)}, bf16[128,1536]{1,0:T(8,128)(2,1)S(1)}, u32[]{:S(2)}, u32[]{:S(2)}) collective-permute-start(bf16[128,1536]{1,0:T(8,128)(2,1)S(1)} %shard_map.67.own), channel_id=1, source_target_pairs={{0,32},{1,33},{2,34},{3,35},{4,36},{5,37},{6,38},{7,39},{8,40},{9,... | collective-permute-start | bytes 1179656 | tf_op jit(solution)/shard_map/ppermute | solution.py:35
  4.8 12.9 %collective-permute-start = (bf16[128,1536]{1,0:T(8,128)(2,1)S(1)}, bf16[128,1536]{1,0:T(8,128)(2,1)S(1)}, u32[]{:S(2)}, u32[]{:S(2)}) collective-permute-start(bf16[128,1536]{1,0:T(8,128)(2,1)S(1)} %shard_map.67.own), channel_id=1, source_target_pairs={{0,72},{1,73},{2,74},{3,75},{4,76},{5,77},{6,78},{7,79},{8,64},{9,... | collective-permute-start | bytes 1179656 | tf_op jit(solution)/shard_map/ppermute | solution.py:35
  8.9 14.9 %collective-permute-start.6 = (bf16[128,1536]{1,0:T(8,128)(2,1)S(1)}, bf16[128,1536]{1,0:T(8,128)(2,1)S(1)}, u32[]{:S(2)}, u32[]{:S(2)}) collective-permute-start(bf16[128,1536]{1,0:T(8,128)(2,1)S(1)} %shard_map.67.own), channel_id=1, source_target_pairs={{0,48},{1,49},{2,50},{3,51},{4,52},{5,53},{6,54},{7,55},{8,56},{9,... | collective-permute-start | bytes 1179656 | tf_op jit(solution)/shard_map/ppermute | solution.py:35
  10.0 13.8 %collective-permute-start.5 = (bf16[128,1536]{1,0:T(8,128)(2,1)S(1)}, bf16[128,1536]{1,0:T(8,128)(2,1)S(1)}, u32[]{:S(2)}, u32[]{:S(2)}) collective-permute-start(bf16[128,1536]{1,0:T(8,128)(2,1)S(1)} %shard_map.67.own), channel_id=1, source_target_pairs={{0,16},{1,17},{2,18},{3,19},{4,20},{5,21},{6,22},{7,23},{8,24},{9,... | collective-permute-start | bytes 1179656 | tf_op jit(solution)/shard_map/ppermute | solution.py:35
  17.7 11.2 %collective-permute-start.4 = (bf16[128,1536]{1,0:T(8,128)(2,1)S(1)}, bf16[128,1536]{1,0:T(8,128)(2,1)S(1)}, u32[]{:S(2)}, u32[]{:S(2)}) collective-permute-start(bf16[128,1536]{1,0:T(8,128)(2,1)S(1)} %collective-permute-done.1.refs_1_), channel_id=1, source_target_pairs={{0,72},{1,73},{2,74},{3,75},{4,76},{5,77},{6,78},{7,79},{8,64},{9,... | collective-permute-start | bytes 1179656 | tf_op jit(solution)/shard_map/ppermute | solution.py:35
  20.6 10.5 %collective-permute-start.3 = (bf16[128,1536]{1,0:T(8,128)(2,1)S(1)}, bf16[128,1536]{1,0:T(8,128)(2,1)S(1)}, u32[]{:S(2)}, u32[]{:S(2)}) collective-permute-start(bf16[128,1536]{1,0:T(8,128)(2,1)S(1)} %collective-permute-done.refs_0_), channel_id=1, source_target_pairs={{0,48},{1,49},{2,50},{3,51},{4,52},{5,53},{6,54},{7,55},{8,56},{9,... | collective-permute-start | bytes 1179656 | tf_op jit(solution)/shard_map/ppermute | solution.py:35
  22.2 10.0 %collective-permute-start.2 = (bf16[128,1536]{1,0:T(8,128)(2,1)S(1)}, bf16[128,1536]{1,0:T(8,128)(2,1)S(1)}, u32[]{:S(2)}, u32[]{:S(2)}) collective-permute-start(bf16[128,1536]{1,0:T(8,128)(2,1)S(1)} %collective-permute-done.refs_0_), channel_id=1, source_target_pairs={{0,16},{1,17},{2,18},{3,19},{4,20},{5,21},{6,22},{7,23},{8,24},{9,... | collective-permute-start | bytes 1179656 | tf_op jit(solution)/shard_map/ppermute | solution.py:35
  34.6 1.3 %collective-permute-start.7 = (f32[48,128]{1,0:T(8,128)S(1)}, f32[48,128]{1,0:T(8,128)S(1)}, u32[]{:S(2)}, u32[]{:S(2)}) collective-permute-start(f32[48,128]{1,0:T(8,128)S(1)} %get-tuple-element.65.mine), channel_id=1, source_target_pairs={{0,1},{1,0},{2,3},{3,2},{4,5},{5,4},{6,7},{7,6},{8,9},{9,8},{10,11... | collective-permute-start | bytes 73736 | tf_op jit(solution)/shard_map/ppermute | solution.py:35
  47.5 1.9 %copy-start = (bf16[2048,512]{1,0:T(8,128)(2,1)S(1)}, bf16[2048,512]{1,0:T(8,128)(2,1)}, u32[]{:S(2)}) copy-start(bf16[2048,512]{1,0:T(8,128)(2,1)} %param.6) | copy-start | bytes 6291460
  49.1 6.6 %collective-permute-start.10 = (bf16[8,512,128]{2,1,0:T(8,128)(2,1)S(1)}, bf16[8,512,128]{2,1,0:T(8,128)(2,1)S(1)}, u32[]{:S(2)}, u32[]{:S(2)}) collective-permute-start(bf16[8,512,128]{2,1,0:T(8,128)(2,1)S(1)} %get-tuple-element.82), channel_id=1, source_target_pairs={{0,1},{1,0},{2,3},{3,2},{4,5},{5,4},{6,7},{7,6},{8,9},{9,8},{10,11... | collective-permute-start | bytes 3145736 | tf_op jit(solution)/shard_map/ppermute | solution.py:35
  52.4 10.0 %collective-permute-start.8 = (bf16[256,512]{1,0:T(8,128)(2,1)S(1)}, bf16[256,512]{1,0:T(8,128)(2,1)S(1)}, u32[]{:S(2)}, u32[]{:S(2)}) collective-permute-start(bf16[256,512]{1,0:T(8,128)(2,1)S(1)} %get-tuple-element.79), channel_id=1, source_target_pairs={{0,16},{1,17},{2,18},{3,19},{4,20},{5,21},{6,22},{7,23},{8,24},{9,... | collective-permute-start | bytes 786440 | tf_op jit(solution)/shard_map/ppermute | solution.py:35
  53.9 8.5 %collective-permute-start.9 = (bf16[256,512]{1,0:T(8,128)(2,1)S(1)}, bf16[256,512]{1,0:T(8,128)(2,1)S(1)}, u32[]{:S(2)}, u32[]{:S(2)}) collective-permute-start(bf16[256,512]{1,0:T(8,128)(2,1)S(1)} %get-tuple-element.80), channel_id=1, source_target_pairs={{0,48},{1,49},{2,50},{3,51},{4,52},{5,53},{6,54},{7,55},{8,56},{9,... | collective-permute-start | bytes 786440 | tf_op jit(solution)/shard_map/ppermute | solution.py:35
  57.0 7.9 %collective-permute-start.13 = (bf16[512,128]{1,0:T(8,128)(2,1)S(1)}, bf16[512,128]{1,0:T(8,128)(2,1)S(1)}, u32[]{:S(2)}, u32[]{:S(2)}) collective-permute-start(bf16[512,128]{1,0:T(8,128)(2,1)S(1)} %get-tuple-element.88), channel_id=1, source_target_pairs={{0,8},{1,9},{2,10},{3,11},{4,12},{5,13},{6,14},{7,15},{8,0},{9,1},... | collective-permute-start | bytes 393224 | tf_op jit(solution)/shard_map/ppermute | solution.py:35
  57.7 9.1 %collective-permute-start.11 = (bf16[2,512,128]{2,1,0:T(8,128)(2,1)S(1)}, bf16[2,512,128]{2,1,0:T(8,128)(2,1)S(1)}, u32[]{:S(2)}, u32[]{:S(2)}) collective-permute-start(bf16[2,512,128]{2,1,0:T(8,128)(2,1)S(1)} %get-tuple-element.85), channel_id=1, source_target_pairs={{0,2},{1,3},{2,4},{3,5},{4,6},{5,7},{6,0},{7,1},{8,10},{9,11},{10,... | collective-permute-start | bytes 786440 | tf_op jit(solution)/shard_map/ppermute | solution.py:35
  58.5 8.2 %collective-permute-start.12 = (bf16[2,512,128]{2,1,0:T(8,128)(2,1)S(1)}, bf16[2,512,128]{2,1,0:T(8,128)(2,1)S(1)}, u32[]{:S(2)}, u32[]{:S(2)}) collective-permute-start(bf16[2,512,128]{2,1,0:T(8,128)(2,1)S(1)} %get-tuple-element.86), channel_id=1, source_target_pairs={{0,6},{1,7},{2,0},{3,1},{4,2},{5,3},{6,4},{7,5},{8,14},{9,15},{10,... | collective-permute-start | bytes 786440 | tf_op jit(solution)/shard_map/ppermute | solution.py:35
  62.3 9.4 %collective-permute-start.16 = (bf16[256,512]{1,0:T(8,128)(2,1)S(1)}, bf16[256,512]{1,0:T(8,128)(2,1)S(1)}, u32[]{:S(2)}, u32[]{:S(2)}) collective-permute-start(bf16[256,512]{1,0:T(8,128)(2,1)S(1)} %get-tuple-element.92), channel_id=1, source_target_pairs={{0,32},{1,33},{2,34},{3,35},{4,36},{5,37},{6,38},{7,39},{8,40},{9,... | collective-permute-start | bytes 786440 | tf_op jit(solution)/shard_map/ppermute | solution.py:35
  65.0 9.7 %collective-permute-start.14 = (bf16[512,128]{1,0:T(8,128)(2,1)S(1)}, bf16[512,128]{1,0:T(8,128)(2,1)S(1)}, u32[]{:S(2)}, u32[]{:S(2)}) collective-permute-start(bf16[512,128]{1,0:T(8,128)(2,1)S(1)} %add_convert_fusion), channel_id=1, source_target_pairs={{0,4},{1,5},{2,6},{3,7},{4,0},{5,1},{6,2},{7,3},{8,12},{9,13},{10,... | collective-permute-start | bytes 393224 | tf_op jit(solution)/shard_map/ppermute | solution.py:35
  66.9 7.8 %collective-permute-start.15 = (bf16[512,128]{1,0:T(8,128)(2,1)S(1)}, bf16[512,128]{1,0:T(8,128)(2,1)S(1)}, u32[]{:S(2)}, u32[]{:S(2)}) collective-permute-start(bf16[512,128]{1,0:T(8,128)(2,1)S(1)} %fusion.5), channel_id=1, source_target_pairs={{0,8},{1,9},{2,10},{3,11},{4,12},{5,13},{6,14},{7,15},{8,0},{9,1},... | collective-permute-start | bytes 393224 | tf_op jit(solution)/shard_map/ppermute | solution.py:35
  71.9 6.3 %collective-permute-start.17 = (bf16[128,512]{1,0:T(8,128)(2,1)S(1)}, bf16[128,512]{1,0:T(8,128)(2,1)S(1)}, u32[]{:S(2)}, u32[]{:S(2)}) collective-permute-start(bf16[128,512]{1,0:T(8,128)(2,1)S(1)} %slice.38), channel_id=1, source_target_pairs={{0,72},{1,73},{2,74},{3,75},{4,76},{5,77},{6,78},{7,79},{8,64},{9,... | collective-permute-start | bytes 393224 | tf_op jit(solution)/shard_map/ppermute | solution.py:35

commit v6 on v5

--- a/solution.py
+++ b/solution.py
@@ -464,12 +464,12 @@
     from_flip = permute(far_flip, along_y(0, 1))
     from_down, from_up = permute(image_up, along_y(1)), permute(image_down, along_y(3))
     text_kept, text_left, text_right, text_far = texts
+    from_far = permute(text_far, along_x(2))
+    text_left, text_right, from_far, image_kept = lax.optimization_barrier(
+        (text_left, text_right, from_far, image_kept)
+    )
     from_right, from_left = permute(text_left, along_x(3)), permute(text_right, along_x(1))
     image_far = permute((image_far + from_flip.astype(F32)).astype(BF16), along_y(2))
-    text_far, from_left, from_right, image_kept = lax.optimization_barrier(
-        (text_far, from_left, from_right, image_kept)
-    )
-    from_far = permute(text_far, along_x(2))
     image_sum = total([image_kept, from_down, from_up])
     from_z = permute(image_sum[1].astype(BF16), along_y(0, 1))
     text_sum = total([text_kept, from_left, from_right, from_far])

time: 79 us -> 79.1 us (level)
  waiting for transfers between devices: 12.8 us -> 14.9 us
  starting transfers between devices: 31.8 us -> 29.8 us
    ppermute x18, waiting for transfers between devices: 12.8 us -> 14.9 us  [permute(): lax.ppermute(v, AXES, [(i, index(*move(*place(i)))) for i in range(128)])]
    ppermute x18, starting transfers between devices: 31.8 us -> 29.8 us  [permute(): lax.ppermute(v, AXES, [(i, index(*move(*place(i)))) for i in range(128)])]
  transfers between devices with their start and end apart: 18 -> 18, of which waited for: 10 -> 9; matrix products, arithmetic and copies ran while one was open for 1% -> 1% of each run, Pallas kernels for 19% -> 19%
where the time goes in v6:
time: 79.1 us; the launch traced here: 78.9 us
  starting transfers between devices  29.8 us (38%)
  Pallas kernels  20.1 us (25%)
  waiting for transfers between devices  14.9 us (19%)
  blocking collectives  11.6 us (15%)
  other arithmetic  0.96 us (1%)
  local copies, waits for them, and re-layouts  0.81 us (1%)
    ppermute x18, starting transfers between devices, permute(): lax.ppermute(v, AXES, [(i, index(*move(*place(i)))) for i in range(128)])  29.8 us
    pallas_call x9, Pallas kernels, call(): pl.pallas_call(body, in_specs=specs, out_specs=[pl.BlockSpec(memory_space...  20.1 us
    ppermute x18, waiting for transfers between devices, permute(): lax.ppermute(v, AXES, [(i, index(*move(*place(i)))) for i in range(128)])  14.9 us
    all_to_all x1, blocking collectives, shards(): lax.all_to_all(stats, 'grp', 0, 0, tiled=True, axis_index_groups=peers)  11.6 us
  transfers between devices with their start and end apart: 18, of which 9 were waited for; matrix products, arithmetic and copies ran while one was open for 1% of the time, Pallas kernels for 19%

profile of v6, /device:TPU:0, one launch (start us, length us, event | category | flops | bytes accessed | tf_op | source)
XLA Modules:
  0.0 78.9 jit_solution(1848208614004900342)
XLA Ops:
  0.6 1.0 %shard_map.67.own = bf16[128,1536]{1,0:T(8,128)(2,1)S(1)} custom-call(bf16[128,1024]{1,0:T(8,128)(2,1)} %text_t.1, bf16[128,512]{1,0:T(8,128)(2,1)} %text_s.1), custom_call_target="tpu_custom_call" | custom-call | tf_op jit(solution)/shard_map/pallas_call | solution.py:60
  1.6 3.2 %collective-permute-start.1 = (bf16[128,1536]{1,0:T(8,128)(2,1)S(1)}, bf16[128,1536]{1,0:T(8,128)(2,1)S(1)}, u32[]{:S(2)}, u32[]{:S(2)}) collective-permute-start(bf16[128,1536]{1,0:T(8,128)(2,1)S(1)} %shard_map.67.own), channel_id=1, source_target_pairs={{0,32},{1,33},{2,34},{3,35},{4,36},{5,37},{6,38},{7,39},{8,40},{9,... | collective-permute-start | bytes 1179656 | tf_op jit(solution)/shard_map/ppermute | solution.py:35
  4.8 4.0 %collective-permute-start = (bf16[128,1536]{1,0:T(8,128)(2,1)S(1)}, bf16[128,1536]{1,0:T(8,128)(2,1)S(1)}, u32[]{:S(2)}, u32[]{:S(2)}) collective-permute-start(bf16[128,1536]{1,0:T(8,128)(2,1)S(1)} %shard_map.67.own), channel_id=1, source_target_pairs={{0,72},{1,73},{2,74},{3,75},{4,76},{5,77},{6,78},{7,79},{8,64},{9,... | collective-permute-start | bytes 1179656 | tf_op jit(solution)/shard_map/ppermute | solution.py:35
  8.9 1.1 %collective-permute-start.6 = (bf16[128,1536]{1,0:T(8,128)(2,1)S(1)}, bf16[128,1536]{1,0:T(8,128)(2,1)S(1)}, u32[]{:S(2)}, u32[]{:S(2)}) collective-permute-start(bf16[128,1536]{1,0:T(8,128)(2,1)S(1)} %shard_map.67.own), channel_id=1, source_target_pairs={{0,48},{1,49},{2,50},{3,51},{4,52},{5,53},{6,54},{7,55},{8,56},{9,... | collective-permute-start | bytes 1179656 | tf_op jit(solution)/shard_map/ppermute | solution.py:35
  10.0 0.9 %collective-permute-start.5 = (bf16[128,1536]{1,0:T(8,128)(2,1)S(1)}, bf16[128,1536]{1,0:T(8,128)(2,1)S(1)}, u32[]{:S(2)}, u32[]{:S(2)}) collective-permute-start(bf16[128,1536]{1,0:T(8,128)(2,1)S(1)} %shard_map.67.own), channel_id=1, source_target_pairs={{0,16},{1,17},{2,18},{3,19},{4,20},{5,21},{6,22},{7,23},{8,24},{9,... | collective-permute-start | bytes 1179656 | tf_op jit(solution)/shard_map/ppermute | solution.py:35
  10.9 4.4 %shard_map.68 = (bf16[1024,2048]{1,0:T(8,128)(2,1)S(1)}, bf16[512,2048]{1,0:T(8,128)(2,1)S(1)}, f32[1024,2048]{1,0:T(8,128)S(1)}, f32[1024,2048]{1,0:T(8,128)S(1...) custom-call(bf16[128,1536]{1,0:T(8,128)(2,1)S(1)} %shard_map.67.own, bf16[8,2,128,1024]{3,2,1,0:T(8,128)(2,1)} %bitcast.19, ...), custom_call_target="tpu_custom_call" | custom-call | flops 805306368 | bytes 6291456 | tf_op jit(solution)/shard_map/pallas_call | solution.py:60
  15.3 2.4 %collective-permute-done.refs_0_ = bf16[128,1536]{1,0:T(8,128)(2,1)S(1)} collective-permute-done((bf16[128,1536]{1,0:T(8,128)(2,1)S(1)}, bf16[128,1536]{1,0:T(8,128)(2,1)S(1)}, u32[]{:S(2)}, u32[]{:S(2)}) %collective-permute-start) | collective-permute-done | bytes 393248 | tf_op jit(solution)/shard_map/ppermute | solution.py:35
  17.7 3.0 %collective-permute-start.4 = (bf16[128,1536]{1,0:T(8,128)(2,1)S(1)}, bf16[128,1536]{1,0:T(8,128)(2,1)S(1)}, u32[]{:S(2)}, u32[]{:S(2)}) collective-permute-start(bf16[128,1536]{1,0:T(8,128)(2,1)S(1)} %collective-permute-done.1.refs_1_), channel_id=1, source_target_pairs={{0,72},{1,73},{2,74},{3,75},{4,76},{5,77},{6,78},{7,79},{8,64},{9,... | collective-permute-start | bytes 1179656 | tf_op jit(solution)/shard_map/ppermute | solution.py:35
  20.6 1.5 %collective-permute-start.3 = (bf16[128,1536]{1,0:T(8,128)(2,1)S(1)}, bf16[128,1536]{1,0:T(8,128)(2,1)S(1)}, u32[]{:S(2)}, u32[]{:S(2)}) collective-permute-start(bf16[128,1536]{1,0:T(8,128)(2,1)S(1)} %collective-permute-done.refs_0_), channel_id=1, source_target_pairs={{0,48},{1,49},{2,50},{3,51},{4,52},{5,53},{6,54},{7,55},{8,56},{9,... | collective-permute-start | bytes 1179656 | tf_op jit(solution)/shard_map/ppermute | solution.py:35
  22.7 1.1 %collective-permute-done.6.refs_3_ = bf16[128,1536]{1,0:T(8,128)(2,1)S(1)} collective-permute-done((bf16[128,1536]{1,0:T(8,128)(2,1)S(1)}, bf16[128,1536]{1,0:T(8,128)(2,1)S(1)}, u32[]{:S(2)}, u32[]{:S(2)}) %collective-permute-start.6) | collective-permute-done | bytes 393248 | tf_op jit(solution)/shard_map/ppermute | solution.py:35
  23.8 5.0 %shard_map.69 = (f32[1024,2048]{1,0:T(8,128)S(1)}, f32[1024,2048]{1,0:T(8,128)S(1)}, bf16[512,1024]{1,0:T(8,128)(2,1)S(1)}, f32[8,2048]{1,0:T(8,128)S(1)}) custom-call(bf16[128,1536]{1,0:T(8,128)(2,1)S(1)} %collective-permute-done.refs_0_, ...), custom_call_target="tpu_custom_call", output_to_operand_aliasing={{0}: (6, {}), {1}: (7, {}), {2}: (8, {})} | custom-call | flops 3221225472 | bytes 2097152 | tf_op jit(solution)/shard_map/pallas_call | solution.py:60
  28.9 1.4 %shard_map.70 = (f32[1024,2048]{1,0:T(8,128)S(1)}, f32[1024,2048]{1,0:T(8,128)S(1)}, bf16[512,1024]{1,0:T(8,128)(2,1)S(1)}, f32[8,2048]{1,0:T(8,128)S(1)}) custom-call(bf16[128,1536]{1,0:T(8,128)(2,1)S(1)} %collective-permute-done.4.refs_0_, ...), custom_call_target="tpu_custom_call", output_to_operand_aliasing={{0}: (3, {}), {1}: (4, {}), {2}: (5, {})} | custom-call | flops 805306368 | bytes 524288 | tf_op jit(solution)/shard_map/pallas_call | solution.py:60
  30.3 0.9 %collective-permute-done.3.refs_1_ = bf16[128,1536]{1,0:T(8,128)(2,1)S(1)} collective-permute-done((bf16[128,1536]{1,0:T(8,128)(2,1)S(1)}, bf16[128,1536]{1,0:T(8,128)(2,1)S(1)}, u32[]{:S(2)}, u32[]{:S(2)}) %collective-permute-start.3) | collective-permute-done | bytes 393248 | tf_op jit(solution)/shard_map/ppermute | solution.py:35
  31.1 1.0 %collective-permute-done.2.refs_0_ = bf16[128,1536]{1,0:T(8,128)(2,1)S(1)} collective-permute-done((bf16[128,1536]{1,0:T(8,128)(2,1)S(1)}, bf16[128,1536]{1,0:T(8,128)(2,1)S(1)}, u32[]{:S(2)}, u32[]{:S(2)}) %collective-permute-start.2) | collective-permute-done | bytes 393248 | tf_op jit(solution)/shard_map/ppermute | solution.py:35
  32.1 2.5 %shard_map.71 = (f32[1024,2048]{1,0:T(8,128)S(1)}, f32[1024,2048]{1,0:T(8,128)S(1)}, bf16[512,1024]{1,0:T(8,128)(2,1)S(1)}, f32[48,128]{1,0:T(8,128)S(1)}) custom-call(bf16[128,1536]{1,0:T(8,128)(2,1)S(1)} %collective-permute-done.2.refs_0_, ...), custom_call_target="tpu_custom_call", output_to_operand_aliasing={{0}: (4, {}), {1}: (5, {}), {2}: (6, {})} | custom-call | flops 1610612736 | bytes 1048576 | tf_op jit(solution)/shard_map/pallas_call | solution.py:60
  34.7 1.2 %collective-permute-done.7.other = f32[48,128]{1,0:T(8,128)S(1)} collective-permute-done((f32[48,128]{1,0:T(8,128)S(1)}, f32[48,128]{1,0:T(8,128)S(1)}, u32[]{:S(2)}, u32[]{:S(2)}) %collective-permute-start.7) | collective-permute-done | bytes 24608 | tf_op jit(solution)/shard_map/ppermute | solution.py:35
  35.9 11.6 %all_to_all.5.received = f32[8,48,128]{2,1,0:T(8,128)S(1)} all-to-all(f32[8,48,128]{2,1,0:T(8,128)S(1)} %get-tuple-element.71), channel_id=1, replica_groups={{0,2,4,6,8,10,12,14},{1,3,5,7,9,11,13,15},{16,18,20,22,24,26,28,30},{17..., dimensions={0} | all-to-all | bytes 393216 | tf_op jit(solution)/shard_map/all_to_all | solution.py:457
  47.5 1.6 %shard_map.73 = (bf16[8,512,128]{2,1,0:T(8,128)(2,1)S(1)}, bf16[1024,1024]{1,0:T(8,128)(2,1)S(1)}, f32[32,128]{1,0:T(8,128)S(1)}, f32[16,128]{1,0:T(8,128)S(1)},...) custom-call(f32[1024,2048]{1,0:T(8,128)S(1)} %get-tuple-element.68.logit_t, ...), custom_call_target="tpu_custom_call", output_to_operand_aliasing={{4}: (0, {}), {5}: (1, {})} | custom-call | flops 1073741824 | bytes 8388608 | tf_op jit(solution)/shard_map/pallas_call | solution.py:60
  49.4 3.0 %shard_map.74 = (bf16[1024,1024]{1,0:T(8,128)(2,1)S(1)}, f32[256,512]{1,0:T(8,128)S(1)}, bf16[256,512]{1,0:T(8,128)(2,1)S(1)}, bf16[256,512]{1,0:T(8,128)(2,1)S(...) custom-call(f32[1024,2048]{1,0:T(8,128)S(1)} %get-tuple-element.72.logit_t, ...), custom_call_target="tpu_custom_call" | custom-call | flops 2147483648 | bytes 8388608 | tf_op jit(solution)/shard_map/pallas_call | solution.py:60
  52.4 3.0 %collective-permute-start.8 = (bf16[256,512]{1,0:T(8,128)(2,1)S(1)}, bf16[256,512]{1,0:T(8,128)(2,1)S(1)}, u32[]{:S(2)}, u32[]{:S(2)}) collective-permute-start(bf16[256,512]{1,0:T(8,128)(2,1)S(1)} %get-tuple-element.80), channel_id=1, source_target_pairs={{0,32},{1,33},{2,34},{3,35},{4,36},{5,37},{6,38},{7,39},{8,40},{9,... | collective-permute-start | bytes 786440 | tf_op jit(solution)/shard_map/ppermute | solution.py:35
  55.3 1.4 %shard_map.75 = (f32[2,512,128]{2,1,0:T(8,128)S(1)}, bf16[2,512,128]{2,1,0:T(8,128)(2,1)S(1)}, bf16[2,512,128]{2,1,0:T(8,128)(2,1)S(1)}, f32[512,128]{1,0:T(8,128)S(1)}, bf16[512,128]{1,0:T(8,128)(2,1)S(1)}) custom-call(bf16[512,1024]{1,0:T(8,128)(2,1)S(1)} %get-tuple-element.70.turned, bf16[1024,1024]{1,0:T(8,128)(2,1)S(1)} %get-tuple-element.81.near, ...), custom_call_target="tpu_custom_call" | custom-call | flops 1073741824 | bytes 2097152 | tf_op jit(solution)/shard_map/pallas_call | solution.py:60
  57.3 0.8 %collective-permute-start.10 = (bf16[2,512,128]{2,1,0:T(8,128)(2,1)S(1)}, bf16[2,512,128]{2,1,0:T(8,128)(2,1)S(1)}, u32[]{:S(2)}, u32[]{:S(2)}) collective-permute-start(bf16[2,512,128]{2,1,0:T(8,128)(2,1)S(1)} %get-tuple-element.85), channel_id=1, source_target_pairs={{0,2},{1,3},{2,4},{3,5},{4,6},{5,7},{6,0},{7,1},{8,10},{9,11},{10,... | collective-permute-start | bytes 786440 | tf_op jit(solution)/shard_map/ppermute | solution.py:35
  58.2 2.4 %collective-permute-start.11 = (bf16[2,512,128]{2,1,0:T(8,128)(2,1)S(1)}, bf16[2,512,128]{2,1,0:T(8,128)(2,1)S(1)}, u32[]{:S(2)}, u32[]{:S(2)}) collective-permute-start(bf16[2,512,128]{2,1,0:T(8,128)(2,1)S(1)} %get-tuple-element.86), channel_id=1, source_target_pairs={{0,6},{1,7},{2,0},{3,1},{4,2},{5,3},{6,4},{7,5},{8,14},{9,15},{10,... | collective-permute-start | bytes 786440 | tf_op jit(solution)/shard_map/ppermute | solution.py:35
  60.6 2.1 %collective-permute-done.8 = bf16[256,512]{1,0:T(8,128)(2,1)S(1)} collective-permute-done((bf16[256,512]{1,0:T(8,128)(2,1)S(1)}, bf16[256,512]{1,0:T(8,128)(2,1)S(1)}, u32[]{:S(2)}, u32[]{:S(2)}) %collective-permute-start.8) | collective-permute-done | bytes 262176 | tf_op jit(solution)/shard_map/ppermute | solution.py:35
  62.6 1.4 %collective-permute-start.15 = (bf16[256,512]{1,0:T(8,128)(2,1)S(1)}, bf16[256,512]{1,0:T(8,128)(2,1)S(1)}, u32[]{:S(2)}, u32[]{:S(2)}) collective-permute-start(bf16[256,512]{1,0:T(8,128)(2,1)S(1)} %get-tuple-element.90), channel_id=1, source_target_pairs={{0,16},{1,17},{2,18},{3,19},{4,20},{5,21},{6,22},{7,23},{8,24},{9,... | collective-permute-start | bytes 786440 | tf_op jit(solution)/shard_map/ppermute | solution.py:35
  64.1 1.8 %collective-permute-start.16 = (bf16[256,512]{1,0:T(8,128)(2,1)S(1)}, bf16[256,512]{1,0:T(8,128)(2,1)S(1)}, u32[]{:S(2)}, u32[]{:S(2)}) collective-permute-start(bf16[256,512]{1,0:T(8,128)(2,1)S(1)} %get-tuple-element.91), channel_id=1, source_target_pairs={{0,48},{1,49},{2,50},{3,51},{4,52},{5,53},{6,54},{7,55},{8,56},{9,... | collective-permute-start | bytes 786440 | tf_op jit(solution)/shard_map/ppermute | solution.py:35
  65.9 1.0 %collective-permute-start.13 = (bf16[512,128]{1,0:T(8,128)(2,1)S(1)}, bf16[512,128]{1,0:T(8,128)(2,1)S(1)}, u32[]{:S(2)}, u32[]{:S(2)}) collective-permute-start(bf16[512,128]{1,0:T(8,128)(2,1)S(1)} %add_convert_fusion), channel_id=1, source_target_pairs={{0,4},{1,5},{2,6},{3,7},{4,0},{5,1},{6,2},{7,3},{8,12},{9,13},{10,... | collective-permute-start | bytes 393224 | tf_op jit(solution)/shard_map/ppermute | solution.py:35
  67.0 1.3 %collective-permute-start.14 = (bf16[512,128]{1,0:T(8,128)(2,1)S(1)}, bf16[512,128]{1,0:T(8,128)(2,1)S(1)}, u32[]{:S(2)}, u32[]{:S(2)}) collective-permute-start(bf16[512,128]{1,0:T(8,128)(2,1)S(1)} %fusion.5), channel_id=1, source_target_pairs={{0,8},{1,9},{2,10},{3,11},{4,12},{5,13},{6,14},{7,15},{8,0},{9,1},... | collective-permute-start | bytes 393224 | tf_op jit(solution)/shard_map/ppermute | solution.py:35
  68.3 3.4 %collective-permute-done.15 = bf16[256,512]{1,0:T(8,128)(2,1)S(1)} collective-permute-done((bf16[256,512]{1,0:T(8,128)(2,1)S(1)}, bf16[256,512]{1,0:T(8,128)(2,1)S(1)}, u32[]{:S(2)}, u32[]{:S(2)}) %collective-permute-start.15) | collective-permute-done | bytes 262176 | tf_op jit(solution)/shard_map/ppermute | solution.py:35
  71.9 2.8 %collective-permute-start.17 = (bf16[128,512]{1,0:T(8,128)(2,1)S(1)}, bf16[128,512]{1,0:T(8,128)(2,1)S(1)}, u32[]{:S(2)}, u32[]{:S(2)}) collective-permute-start(bf16[128,512]{1,0:T(8,128)(2,1)S(1)} %slice.38), channel_id=1, source_target_pairs={{0,72},{1,73},{2,74},{3,75},{4,76},{5,77},{6,78},{7,79},{8,64},{9,... | collective-permute-start | bytes 393224 | tf_op jit(solution)/shard_map/ppermute | solution.py:35
  74.7 0.8 copy.20
  75.5 2.7 %collective-permute-done.17 = bf16[128,512]{1,0:T(8,128)(2,1)S(1)} collective-permute-done((bf16[128,512]{1,0:T(8,128)(2,1)S(1)}, bf16[128,512]{1,0:T(8,128)(2,1)S(1)}, u32[]{:S(2)}, u32[]{:S(2)}) %collective-permute-start.17) | collective-permute-done | bytes 131104 | tf_op jit(solution)/shard_map/ppermute | solution.py:35
  (24 shorter events, 2.8 us)
Async XLA Ops:
  1.6 13.6 %collective-permute-start.1 = (bf16[128,1536]{1,0:T(8,128)(2,1)S(1)}, bf16[128,1536]{1,0:T(8,128)(2,1)S(1)}, u32[]{:S(2)}, u32[]{:S(2)}) collective-permute-start(bf16[128,1536]{1,0:T(8,128)(2,1)S(1)} %shard_map.67.own), channel_id=1, source_target_pairs={{0,32},{1,33},{2,34},{3,35},{4,36},{5,37},{6,38},{7,39},{8,40},{9,... | collective-permute-start | bytes 1179656 | tf_op jit(solution)/shard_map/ppermute | solution.py:35
  4.8 12.9 %collective-permute-start = (bf16[128,1536]{1,0:T(8,128)(2,1)S(1)}, bf16[128,1536]{1,0:T(8,128)(2,1)S(1)}, u32[]{:S(2)}, u32[]{:S(2)}) collective-permute-start(bf16[128,1536]{1,0:T(8,128)(2,1)S(1)} %shard_map.67.own), channel_id=1, source_target_pairs={{0,72},{1,73},{2,74},{3,75},{4,76},{5,77},{6,78},{7,79},{8,64},{9,... | collective-permute-start | bytes 1179656 | tf_op jit(solution)/shard_map/ppermute | solution.py:35
  8.9 14.9 %collective-permute-start.6 = (bf16[128,1536]{1,0:T(8,128)(2,1)S(1)}, bf16[128,1536]{1,0:T(8,128)(2,1)S(1)}, u32[]{:S(2)}, u32[]{:S(2)}) collective-permute-start(bf16[128,1536]{1,0:T(8,128)(2,1)S(1)} %shard_map.67.own), channel_id=1, source_target_pairs={{0,48},{1,49},{2,50},{3,51},{4,52},{5,53},{6,54},{7,55},{8,56},{9,... | collective-permute-start | bytes 1179656 | tf_op jit(solution)/shard_map/ppermute | solution.py:35
  10.0 13.8 %collective-permute-start.5 = (bf16[128,1536]{1,0:T(8,128)(2,1)S(1)}, bf16[128,1536]{1,0:T(8,128)(2,1)S(1)}, u32[]{:S(2)}, u32[]{:S(2)}) collective-permute-start(bf16[128,1536]{1,0:T(8,128)(2,1)S(1)} %shard_map.67.own), channel_id=1, source_target_pairs={{0,16},{1,17},{2,18},{3,19},{4,20},{5,21},{6,22},{7,23},{8,24},{9,... | collective-permute-start | bytes 1179656 | tf_op jit(solution)/shard_map/ppermute | solution.py:35
  17.7 11.2 %collective-permute-start.4 = (bf16[128,1536]{1,0:T(8,128)(2,1)S(1)}, bf16[128,1536]{1,0:T(8,128)(2,1)S(1)}, u32[]{:S(2)}, u32[]{:S(2)}) collective-permute-start(bf16[128,1536]{1,0:T(8,128)(2,1)S(1)} %collective-permute-done.1.refs_1_), channel_id=1, source_target_pairs={{0,72},{1,73},{2,74},{3,75},{4,76},{5,77},{6,78},{7,79},{8,64},{9,... | collective-permute-start | bytes 1179656 | tf_op jit(solution)/shard_map/ppermute | solution.py:35
  20.6 10.5 %collective-permute-start.3 = (bf16[128,1536]{1,0:T(8,128)(2,1)S(1)}, bf16[128,1536]{1,0:T(8,128)(2,1)S(1)}, u32[]{:S(2)}, u32[]{:S(2)}) collective-permute-start(bf16[128,1536]{1,0:T(8,128)(2,1)S(1)} %collective-permute-done.refs_0_), channel_id=1, source_target_pairs={{0,48},{1,49},{2,50},{3,51},{4,52},{5,53},{6,54},{7,55},{8,56},{9,... | collective-permute-start | bytes 1179656 | tf_op jit(solution)/shard_map/ppermute | solution.py:35
  22.2 10.0 %collective-permute-start.2 = (bf16[128,1536]{1,0:T(8,128)(2,1)S(1)}, bf16[128,1536]{1,0:T(8,128)(2,1)S(1)}, u32[]{:S(2)}, u32[]{:S(2)}) collective-permute-start(bf16[128,1536]{1,0:T(8,128)(2,1)S(1)} %collective-permute-done.refs_0_), channel_id=1, source_target_pairs={{0,16},{1,17},{2,18},{3,19},{4,20},{5,21},{6,22},{7,23},{8,24},{9,... | collective-permute-start | bytes 1179656 | tf_op jit(solution)/shard_map/ppermute | solution.py:35
  34.6 1.3 %collective-permute-start.7 = (f32[48,128]{1,0:T(8,128)S(1)}, f32[48,128]{1,0:T(8,128)S(1)}, u32[]{:S(2)}, u32[]{:S(2)}) collective-permute-start(f32[48,128]{1,0:T(8,128)S(1)} %get-tuple-element.65.mine), channel_id=1, source_target_pairs={{0,1},{1,0},{2,3},{3,2},{4,5},{5,4},{6,7},{7,6},{8,9},{9,8},{10,11... | collective-permute-start | bytes 73736 | tf_op jit(solution)/shard_map/ppermute | solution.py:35
  47.5 1.9 %copy-start = (bf16[2048,512]{1,0:T(8,128)(2,1)S(1)}, bf16[2048,512]{1,0:T(8,128)(2,1)}, u32[]{:S(2)}) copy-start(bf16[2048,512]{1,0:T(8,128)(2,1)} %param.6) | copy-start | bytes 6291460
  49.1 6.3 %collective-permute-start.9 = (bf16[8,512,128]{2,1,0:T(8,128)(2,1)S(1)}, bf16[8,512,128]{2,1,0:T(8,128)(2,1)S(1)}, u32[]{:S(2)}, u32[]{:S(2)}) collective-permute-start(bf16[8,512,128]{2,1,0:T(8,128)(2,1)S(1)} %get-tuple-element.82), channel_id=1, source_target_pairs={{0,1},{1,0},{2,3},{3,2},{4,5},{5,4},{6,7},{7,6},{8,9},{9,8},{10,11... | collective-permute-start | bytes 3145736 | tf_op jit(solution)/shard_map/ppermute | solution.py:35
  52.4 10.3 %collective-permute-start.8 = (bf16[256,512]{1,0:T(8,128)(2,1)S(1)}, bf16[256,512]{1,0:T(8,128)(2,1)S(1)}, u32[]{:S(2)}, u32[]{:S(2)}) collective-permute-start(bf16[256,512]{1,0:T(8,128)(2,1)S(1)} %get-tuple-element.80), channel_id=1, source_target_pairs={{0,32},{1,33},{2,34},{3,35},{4,36},{5,37},{6,38},{7,39},{8,40},{9,... | collective-permute-start | bytes 786440 | tf_op jit(solution)/shard_map/ppermute | solution.py:35
  56.7 9.2 %collective-permute-start.12 = (bf16[512,128]{1,0:T(8,128)(2,1)S(1)}, bf16[512,128]{1,0:T(8,128)(2,1)S(1)}, u32[]{:S(2)}, u32[]{:S(2)}) collective-permute-start(bf16[512,128]{1,0:T(8,128)(2,1)S(1)} %get-tuple-element.88), channel_id=1, source_target_pairs={{0,8},{1,9},{2,10},{3,11},{4,12},{5,13},{6,14},{7,15},{8,0},{9,1},... | collective-permute-start | bytes 393224 | tf_op jit(solution)/shard_map/ppermute | solution.py:35
  57.3 9.6 %collective-permute-start.10 = (bf16[2,512,128]{2,1,0:T(8,128)(2,1)S(1)}, bf16[2,512,128]{2,1,0:T(8,128)(2,1)S(1)}, u32[]{:S(2)}, u32[]{:S(2)}) collective-permute-start(bf16[2,512,128]{2,1,0:T(8,128)(2,1)S(1)} %get-tuple-element.85), channel_id=1, source_target_pairs={{0,2},{1,3},{2,4},{3,5},{4,6},{5,7},{6,0},{7,1},{8,10},{9,11},{10,... | collective-permute-start | bytes 786440 | tf_op jit(solution)/shard_map/ppermute | solution.py:35
  58.2 8.7 %collective-permute-start.11 = (bf16[2,512,128]{2,1,0:T(8,128)(2,1)S(1)}, bf16[2,512,128]{2,1,0:T(8,128)(2,1)S(1)}, u32[]{:S(2)}, u32[]{:S(2)}) collective-permute-start(bf16[2,512,128]{2,1,0:T(8,128)(2,1)S(1)} %get-tuple-element.86), channel_id=1, source_target_pairs={{0,6},{1,7},{2,0},{3,1},{4,2},{5,3},{6,4},{7,5},{8,14},{9,15},{10,... | collective-permute-start | bytes 786440 | tf_op jit(solution)/shard_map/ppermute | solution.py:35
  62.6 9.1 %collective-permute-start.15 = (bf16[256,512]{1,0:T(8,128)(2,1)S(1)}, bf16[256,512]{1,0:T(8,128)(2,1)S(1)}, u32[]{:S(2)}, u32[]{:S(2)}) collective-permute-start(bf16[256,512]{1,0:T(8,128)(2,1)S(1)} %get-tuple-element.90), channel_id=1, source_target_pairs={{0,16},{1,17},{2,18},{3,19},{4,20},{5,21},{6,22},{7,23},{8,24},{9,... | collective-permute-start | bytes 786440 | tf_op jit(solution)/shard_map/ppermute | solution.py:35
  64.1 7.7 %collective-permute-start.16 = (bf16[256,512]{1,0:T(8,128)(2,1)S(1)}, bf16[256,512]{1,0:T(8,128)(2,1)S(1)}, u32[]{:S(2)}, u32[]{:S(2)}) collective-permute-start(bf16[256,512]{1,0:T(8,128)(2,1)S(1)} %get-tuple-element.91), channel_id=1, source_target_pairs={{0,48},{1,49},{2,50},{3,51},{4,52},{5,53},{6,54},{7,55},{8,56},{9,... | collective-permute-start | bytes 786440 | tf_op jit(solution)/shard_map/ppermute | solution.py:35
  65.9 8.8 %collective-permute-start.13 = (bf16[512,128]{1,0:T(8,128)(2,1)S(1)}, bf16[512,128]{1,0:T(8,128)(2,1)S(1)}, u32[]{:S(2)}, u32[]{:S(2)}) collective-permute-start(bf16[512,128]{1,0:T(8,128)(2,1)S(1)} %add_convert_fusion), channel_id=1, source_target_pairs={{0,4},{1,5},{2,6},{3,7},{4,0},{5,1},{6,2},{7,3},{8,12},{9,13},{10,... | collective-permute-start | bytes 393224 | tf_op jit(solution)/shard_map/ppermute | solution.py:35
  67.0 7.7 %collective-permute-start.14 = (bf16[512,128]{1,0:T(8,128)(2,1)S(1)}, bf16[512,128]{1,0:T(8,128)(2,1)S(1)}, u32[]{:S(2)}, u32[]{:S(2)}) collective-permute-start(bf16[512,128]{1,0:T(8,128)(2,1)S(1)} %fusion.5), channel_id=1, source_target_pairs={{0,8},{1,9},{2,10},{3,11},{4,12},{5,13},{6,14},{7,15},{8,0},{9,1},... | collective-permute-start | bytes 393224 | tf_op jit(solution)/shard_map/ppermute | solution.py:35
  71.9 6.3 %collective-permute-start.17 = (bf16[128,512]{1,0:T(8,128)(2,1)S(1)}, bf16[128,512]{1,0:T(8,128)(2,1)S(1)}, u32[]{:S(2)}, u32[]{:S(2)}) collective-permute-start(bf16[128,512]{1,0:T(8,128)(2,1)S(1)} %slice.38), channel_id=1, source_target_pairs={{0,72},{1,73},{2,74},{3,75},{4,76},{5,77},{6,78},{7,79},{8,64},{9,... | collective-permute-start | bytes 393224 | tf_op jit(solution)/shard_map/ppermute | solution.py:35

commit v7 on v6

--- a/solution.py
+++ b/solution.py
@@ -343,10 +343,7 @@
     )
 
 
-def near_kernel(scale, logit_t, logit_s, lse, away, image_s, loss, near, *refs):
-    texts, out_loss, sem = refs[:-2], refs[-2], refs[-1]
-    copy = pltpu.make_async_copy(loss, out_loss, sem)
-    copy.start()
+def near_kernel(scale, logit_t, logit_s, lse, away, image_s, near, *texts):
     core = lax.rem(lax.axis_index("grp"), 2)
     blocks, _, block, width = image_s.shape
     rows = blocks * block
@@ -364,30 +361,29 @@
             jnp.dot(away[span, :], image_away, preferred_element_type=F32)
             + jnp.dot(near[span, :], image_near, preferred_element_type=F32)
         ).astype(out.dtype)
-    copy.wait()
-
-
-def near_part(logit_t, logit_s, lse, away, image_s, loss):
+
+
+def near_part(logit_t, logit_s, lse, away, image_s):
     count, rows = logit_t.shape
     width = image_s.shape[3]
     return call(
         functools.partial(near_kernel, 3.0 / math.sqrt(width)),
-        [(VMEM, v) for v in (logit_t, logit_s, lse, away, image_s, loss)],
+        [(VMEM, v) for v in (logit_t, logit_s, lse, away, image_s)],
         [(away.shape, BF16)]
         + [
             ((count // part, width), kind)
             for part, kind in ((4, F32), (4, BF16), (4, BF16), (4, BF16))
-        ]
-        + [jax.ShapeDtypeStruct(loss.shape, F32)],
+        ],
         10,
         flops=2 * count * rows * width,
         size=4 * count * rows,
         exps=count * rows,
-        scratch_shapes=[pltpu.SemaphoreType.DMA(())],
-    )
-
-
-def image_kernel(turned, near, other, kept, up, down, far, far_flip):
+    )
+
+
+def image_kernel(turned, near, other, loss, kept, up, down, far, far_flip, out_loss, sem):
+    copy = pltpu.make_async_copy(loss, out_loss, sem)
+    copy.start()
     spot = lax.axis_index("grp")
     y, z = lax.rem(lax.div(spot, 2), 4), lax.div(spot, 8)
     outs = (
@@ -406,22 +402,25 @@
             out[...] = (
                 mine[:, flip * LANES : flip * LANES + LANES] + other[at].astype(F32)
             ).astype(out.dtype)
-
-
-def image_part(turned, near, other):
+    copy.wait()
+
+
+def image_part(turned, near, other, loss):
     count, rows = near.shape
     width = turned.shape[0]
     return call(
         image_kernel,
-        [(VMEM, turned), (VMEM, near), (VMEM, other)],
+        [(VMEM, turned), (VMEM, near), (VMEM, other), (VMEM, loss)],
         [
             ((2, width, LANES), F32),
             ((2, width, LANES), BF16),
             ((2, width, LANES), BF16),
             ((width, LANES), F32),
             ((width, LANES), BF16),
+            jax.ShapeDtypeStruct(loss.shape, F32),
         ],
         4,
+        scratch_shapes=[pltpu.SemaphoreType.DMA(())],
         flops=2 * count * rows * width,
         size=2 * count * rows,
     )
@@ -459,8 +458,10 @@
         logit_t, logit_s, turned, received
     )
     from_core = permute(grad_other, other_core)
-    near, *texts, row_loss = near_part(logit_t, logit_s, lse, away, image_s, row_loss)
-    image_kept, image_up, image_down, image_far, far_flip = image_part(turned, near, from_core)
+    near, *texts = near_part(logit_t, logit_s, lse, away, image_s)
+    image_kept, image_up, image_down, image_far, far_flip, row_loss = image_part(
+        turned, near, from_core, row_loss
+    )
     from_flip = permute(far_flip, along_y(0, 1))
     from_down, from_up = permute(image_up, along_y(1)), permute(image_down, along_y(3))
     text_kept, text_left, text_right, text_far = texts

time: 79.1 us -> 78.8 us (level)
  no operation moved by 1% of the time
where the time goes in v7:
time: 78.8 us; the launch traced here: 78.5 us
  starting transfers between devices  30 us (38%)
  Pallas kernels  20 us (25%)
  waiting for transfers between devices  14.4 us (18%)
  blocking collectives  11.6 us (15%)
  other arithmetic  0.96 us (1%)
  local copies, waits for them, and re-layouts  0.81 us (1%)
    ppermute x18, starting transfers between devices, permute(): lax.ppermute(v, AXES, [(i, index(*move(*place(i)))) for i in range(128)])  30 us
    pallas_call x9, Pallas kernels, call(): pl.pallas_call(body, in_specs=specs, out_specs=[pl.BlockSpec(memory_space...  20 us
    ppermute x18, waiting for transfers between devices, permute(): lax.ppermute(v, AXES, [(i, index(*move(*place(i)))) for i in range(128)])  14.4 us
    all_to_all x1, blocking collectives, shards(): lax.all_to_all(stats, 'grp', 0, 0, tiled=True, axis_index_groups=peers)  11.6 us
  transfers between devices with their start and end apart: 18, of which 9 were waited for; matrix products, arithmetic and copies ran while one was open for 1% of the time, Pallas kernels for 19%

profile of v7, /device:TPU:0, one launch (start us, length us, event | category | flops | bytes accessed | tf_op | source)
XLA Modules:
  0.0 78.5 jit_solution(7012594942267248143)
XLA Ops:
  0.6 1.0 %shard_map.67.own = bf16[128,1536]{1,0:T(8,128)(2,1)S(1)} custom-call(bf16[128,1024]{1,0:T(8,128)(2,1)} %text_t.1, bf16[128,512]{1,0:T(8,128)(2,1)} %text_s.1), custom_call_target="tpu_custom_call" | custom-call | tf_op jit(solution)/shard_map/pallas_call | solution.py:60
  1.6 3.2 %collective-permute-start.1 = (bf16[128,1536]{1,0:T(8,128)(2,1)S(1)}, bf16[128,1536]{1,0:T(8,128)(2,1)S(1)}, u32[]{:S(2)}, u32[]{:S(2)}) collective-permute-start(bf16[128,1536]{1,0:T(8,128)(2,1)S(1)} %shard_map.67.own), channel_id=1, source_target_pairs={{0,32},{1,33},{2,34},{3,35},{4,36},{5,37},{6,38},{7,39},{8,40},{9,... | collective-permute-start | bytes 1179656 | tf_op jit(solution)/shard_map/ppermute | solution.py:35
  4.8 4.0 %collective-permute-start = (bf16[128,1536]{1,0:T(8,128)(2,1)S(1)}, bf16[128,1536]{1,0:T(8,128)(2,1)S(1)}, u32[]{:S(2)}, u32[]{:S(2)}) collective-permute-start(bf16[128,1536]{1,0:T(8,128)(2,1)S(1)} %shard_map.67.own), channel_id=1, source_target_pairs={{0,72},{1,73},{2,74},{3,75},{4,76},{5,77},{6,78},{7,79},{8,64},{9,... | collective-permute-start | bytes 1179656 | tf_op jit(solution)/shard_map/ppermute | solution.py:35
  8.9 1.1 %collective-permute-start.6 = (bf16[128,1536]{1,0:T(8,128)(2,1)S(1)}, bf16[128,1536]{1,0:T(8,128)(2,1)S(1)}, u32[]{:S(2)}, u32[]{:S(2)}) collective-permute-start(bf16[128,1536]{1,0:T(8,128)(2,1)S(1)} %shard_map.67.own), channel_id=1, source_target_pairs={{0,48},{1,49},{2,50},{3,51},{4,52},{5,53},{6,54},{7,55},{8,56},{9,... | collective-permute-start | bytes 1179656 | tf_op jit(solution)/shard_map/ppermute | solution.py:35
  10.0 0.9 %collective-permute-start.5 = (bf16[128,1536]{1,0:T(8,128)(2,1)S(1)}, bf16[128,1536]{1,0:T(8,128)(2,1)S(1)}, u32[]{:S(2)}, u32[]{:S(2)}) collective-permute-start(bf16[128,1536]{1,0:T(8,128)(2,1)S(1)} %shard_map.67.own), channel_id=1, source_target_pairs={{0,16},{1,17},{2,18},{3,19},{4,20},{5,21},{6,22},{7,23},{8,24},{9,... | collective-permute-start | bytes 1179656 | tf_op jit(solution)/shard_map/ppermute | solution.py:35
  10.9 4.4 %shard_map.68 = (bf16[1024,2048]{1,0:T(8,128)(2,1)S(1)}, bf16[512,2048]{1,0:T(8,128)(2,1)S(1)}, f32[1024,2048]{1,0:T(8,128)S(1)}, f32[1024,2048]{1,0:T(8,128)S(1...) custom-call(bf16[128,1536]{1,0:T(8,128)(2,1)S(1)} %shard_map.67.own, bf16[8,2,128,1024]{3,2,1,0:T(8,128)(2,1)} %bitcast.19, ...), custom_call_target="tpu_custom_call" | custom-call | flops 805306368 | bytes 6291456 | tf_op jit(solution)/shard_map/pallas_call | solution.py:60
  15.3 2.4 %collective-permute-done.refs_0_ = bf16[128,1536]{1,0:T(8,128)(2,1)S(1)} collective-permute-done((bf16[128,1536]{1,0:T(8,128)(2,1)S(1)}, bf16[128,1536]{1,0:T(8,128)(2,1)S(1)}, u32[]{:S(2)}, u32[]{:S(2)}) %collective-permute-start) | collective-permute-done | bytes 393248 | tf_op jit(solution)/shard_map/ppermute | solution.py:35
  17.7 3.0 %collective-permute-start.4 = (bf16[128,1536]{1,0:T(8,128)(2,1)S(1)}, bf16[128,1536]{1,0:T(8,128)(2,1)S(1)}, u32[]{:S(2)}, u32[]{:S(2)}) collective-permute-start(bf16[128,1536]{1,0:T(8,128)(2,1)S(1)} %collective-permute-done.1.refs_1_), channel_id=1, source_target_pairs={{0,72},{1,73},{2,74},{3,75},{4,76},{5,77},{6,78},{7,79},{8,64},{9,... | collective-permute-start | bytes 1179656 | tf_op jit(solution)/shard_map/ppermute | solution.py:35
  20.6 1.5 %collective-permute-start.3 = (bf16[128,1536]{1,0:T(8,128)(2,1)S(1)}, bf16[128,1536]{1,0:T(8,128)(2,1)S(1)}, u32[]{:S(2)}, u32[]{:S(2)}) collective-permute-start(bf16[128,1536]{1,0:T(8,128)(2,1)S(1)} %collective-permute-done.refs_0_), channel_id=1, source_target_pairs={{0,48},{1,49},{2,50},{3,51},{4,52},{5,53},{6,54},{7,55},{8,56},{9,... | collective-permute-start | bytes 1179656 | tf_op jit(solution)/shard_map/ppermute | solution.py:35
  22.7 1.1 %collective-permute-done.6.refs_3_ = bf16[128,1536]{1,0:T(8,128)(2,1)S(1)} collective-permute-done((bf16[128,1536]{1,0:T(8,128)(2,1)S(1)}, bf16[128,1536]{1,0:T(8,128)(2,1)S(1)}, u32[]{:S(2)}, u32[]{:S(2)}) %collective-permute-start.6) | collective-permute-done | bytes 393248 | tf_op jit(solution)/shard_map/ppermute | solution.py:35
  23.8 5.0 %shard_map.69 = (f32[1024,2048]{1,0:T(8,128)S(1)}, f32[1024,2048]{1,0:T(8,128)S(1)}, bf16[512,1024]{1,0:T(8,128)(2,1)S(1)}, f32[8,2048]{1,0:T(8,128)S(1)}) custom-call(bf16[128,1536]{1,0:T(8,128)(2,1)S(1)} %collective-permute-done.refs_0_, ...), custom_call_target="tpu_custom_call", output_to_operand_aliasing={{0}: (6, {}), {1}: (7, {}), {2}: (8, {})} | custom-call | flops 3221225472 | bytes 2097152 | tf_op jit(solution)/shard_map/pallas_call | solution.py:60
  28.9 1.4 %shard_map.70 = (f32[1024,2048]{1,0:T(8,128)S(1)}, f32[1024,2048]{1,0:T(8,128)S(1)}, bf16[512,1024]{1,0:T(8,128)(2,1)S(1)}, f32[8,2048]{1,0:T(8,128)S(1)}) custom-call(bf16[128,1536]{1,0:T(8,128)(2,1)S(1)} %collective-permute-done.4.refs_0_, ...), custom_call_target="tpu_custom_call", output_to_operand_aliasing={{0}: (3, {}), {1}: (4, {}), {2}: (5, {})} | custom-call | flops 805306368 | bytes 524288 | tf_op jit(solution)/shard_map/pallas_call | solution.py:60
  30.3 0.9 %collective-permute-done.3.refs_1_ = bf16[128,1536]{1,0:T(8,128)(2,1)S(1)} collective-permute-done((bf16[128,1536]{1,0:T(8,128)(2,1)S(1)}, bf16[128,1536]{1,0:T(8,128)(2,1)S(1)}, u32[]{:S(2)}, u32[]{:S(2)}) %collective-permute-start.3) | collective-permute-done | bytes 393248 | tf_op jit(solution)/shard_map/ppermute | solution.py:35
  31.1 1.0 %collective-permute-done.2.refs_0_ = bf16[128,1536]{1,0:T(8,128)(2,1)S(1)} collective-permute-done((bf16[128,1536]{1,0:T(8,128)(2,1)S(1)}, bf16[128,1536]{1,0:T(8,128)(2,1)S(1)}, u32[]{:S(2)}, u32[]{:S(2)}) %collective-permute-start.2) | collective-permute-done | bytes 393248 | tf_op jit(solution)/shard_map/ppermute | solution.py:35
  32.1 2.5 %shard_map.71 = (f32[1024,2048]{1,0:T(8,128)S(1)}, f32[1024,2048]{1,0:T(8,128)S(1)}, bf16[512,1024]{1,0:T(8,128)(2,1)S(1)}, f32[48,128]{1,0:T(8,128)S(1)}) custom-call(bf16[128,1536]{1,0:T(8,128)(2,1)S(1)} %collective-permute-done.2.refs_0_, ...), custom_call_target="tpu_custom_call", output_to_operand_aliasing={{0}: (4, {}), {1}: (5, {}), {2}: (6, {})} | custom-call | flops 1610612736 | bytes 1048576 | tf_op jit(solution)/shard_map/pallas_call | solution.py:60
  34.7 1.2 %collective-permute-done.7.other = f32[48,128]{1,0:T(8,128)S(1)} collective-permute-done((f32[48,128]{1,0:T(8,128)S(1)}, f32[48,128]{1,0:T(8,128)S(1)}, u32[]{:S(2)}, u32[]{:S(2)}) %collective-permute-start.7) | collective-permute-done | bytes 24608 | tf_op jit(solution)/shard_map/ppermute | solution.py:35
  35.9 11.6 %all_to_all.5.received = f32[8,48,128]{2,1,0:T(8,128)S(1)} all-to-all(f32[8,48,128]{2,1,0:T(8,128)S(1)} %get-tuple-element.71), channel_id=1, replica_groups={{0,2,4,6,8,10,12,14},{1,3,5,7,9,11,13,15},{16,18,20,22,24,26,28,30},{17..., dimensions={0} | all-to-all | bytes 393216 | tf_op jit(solution)/shard_map/all_to_all | solution.py:456
  47.5 1.6 %shard_map.73 = (bf16[8,512,128]{2,1,0:T(8,128)(2,1)S(1)}, bf16[1024,1024]{1,0:T(8,128)(2,1)S(1)}, f32[32,128]{1,0:T(8,128)S(1)}, f32[16,128]{1,0:T(8,128)S(1)},...) custom-call(f32[1024,2048]{1,0:T(8,128)S(1)} %get-tuple-element.69.logit_t, ...), custom_call_target="tpu_custom_call", output_to_operand_aliasing={{4}: (0, {}), {5}: (1, {})} | custom-call | flops 1073741824 | bytes 8388608 | tf_op jit(solution)/shard_map/pallas_call | solution.py:60
  49.4 2.6 %shard_map.74 = (bf16[1024,1024]{1,0:T(8,128)(2,1)S(1)}, f32[256,512]{1,0:T(8,128)S(1)}, bf16[256,512]{1,0:T(8,128)(2,1)S(1)}, bf16[256,512]{1,0:T(8,128)(2,1)S(1)}, bf16[256,512]{1,0:T(8,128)(2,1)S(1)}) custom-call(f32[1024,2048]{1,0:T(8,128)S(1)} %get-tuple-element.72.logit_t, f32[1024,2048]{1,0:T(8,128)S(1)} %get-tuple-element.73.logit_s, ...), custom_call_target="tpu_custom_call" | custom-call | flops 2147483648 | bytes 8388608 | tf_op jit(solution)/shard_map/pallas_call | solution.py:60
  52.0 3.0 %collective-permute-start.9 = (bf16[256,512]{1,0:T(8,128)(2,1)S(1)}, bf16[256,512]{1,0:T(8,128)(2,1)S(1)}, u32[]{:S(2)}, u32[]{:S(2)}) collective-permute-start(bf16[256,512]{1,0:T(8,128)(2,1)S(1)} %get-tuple-element.82), channel_id=1, source_target_pairs={{0,32},{1,33},{2,34},{3,35},{4,36},{5,37},{6,38},{7,39},{8,40},{9,... | collective-permute-start | bytes 786440 | tf_op jit(solution)/shard_map/ppermute | solution.py:35
  55.0 1.6 %shard_map.75 = (f32[2,512,128]{2,1,0:T(8,128)S(1)}, bf16[2,512,128]{2,1,0:T(8,128)(2,1)S(1)}, bf16[2,512,128]{2,1,0:T(8,128)(2,1)S(1)}, f32[512,128]{1,0:T(8,12...) custom-call(bf16[512,1024]{1,0:T(8,128)(2,1)S(1)} %get-tuple-element.65.turned, ...), custom_call_target="tpu_custom_call" | custom-call | flops 1073741824 | bytes 2097152 | tf_op jit(solution)/shard_map/pallas_call | solution.py:60
  57.2 0.9 %collective-permute-start.10 = (bf16[2,512,128]{2,1,0:T(8,128)(2,1)S(1)}, bf16[2,512,128]{2,1,0:T(8,128)(2,1)S(1)}, u32[]{:S(2)}, u32[]{:S(2)}) collective-permute-start(bf16[2,512,128]{2,1,0:T(8,128)(2,1)S(1)} %get-tuple-element.85), channel_id=1, source_target_pairs={{0,2},{1,3},{2,4},{3,5},{4,6},{5,7},{6,0},{7,1},{8,10},{9,11},{10,... | collective-permute-start | bytes 786440 | tf_op jit(solution)/shard_map/ppermute | solution.py:35
  58.1 2.4 %collective-permute-start.11 = (bf16[2,512,128]{2,1,0:T(8,128)(2,1)S(1)}, bf16[2,512,128]{2,1,0:T(8,128)(2,1)S(1)}, u32[]{:S(2)}, u32[]{:S(2)}) collective-permute-start(bf16[2,512,128]{2,1,0:T(8,128)(2,1)S(1)} %get-tuple-element.86), channel_id=1, source_target_pairs={{0,6},{1,7},{2,0},{3,1},{4,2},{5,3},{6,4},{7,5},{8,14},{9,15},{10,... | collective-permute-start | bytes 786440 | tf_op jit(solution)/shard_map/ppermute | solution.py:35
  60.5 1.8 %collective-permute-done.9 = bf16[256,512]{1,0:T(8,128)(2,1)S(1)} collective-permute-done((bf16[256,512]{1,0:T(8,128)(2,1)S(1)}, bf16[256,512]{1,0:T(8,128)(2,1)S(1)}, u32[]{:S(2)}, u32[]{:S(2)}) %collective-permute-start.9) | collective-permute-done | bytes 262176 | tf_op jit(solution)/shard_map/ppermute | solution.py:35
  62.3 1.4 %collective-permute-start.15 = (bf16[256,512]{1,0:T(8,128)(2,1)S(1)}, bf16[256,512]{1,0:T(8,128)(2,1)S(1)}, u32[]{:S(2)}, u32[]{:S(2)}) collective-permute-start(bf16[256,512]{1,0:T(8,128)(2,1)S(1)} %get-tuple-element.90), channel_id=1, source_target_pairs={{0,16},{1,17},{2,18},{3,19},{4,20},{5,21},{6,22},{7,23},{8,24},{9,... | collective-permute-start | bytes 786440 | tf_op jit(solution)/shard_map/ppermute | solution.py:35
  63.7 1.8 %collective-permute-start.16 = (bf16[256,512]{1,0:T(8,128)(2,1)S(1)}, bf16[256,512]{1,0:T(8,128)(2,1)S(1)}, u32[]{:S(2)}, u32[]{:S(2)}) collective-permute-start(bf16[256,512]{1,0:T(8,128)(2,1)S(1)} %get-tuple-element.91), channel_id=1, source_target_pairs={{0,48},{1,49},{2,50},{3,51},{4,52},{5,53},{6,54},{7,55},{8,56},{9,... | collective-permute-start | bytes 786440 | tf_op jit(solution)/shard_map/ppermute | solution.py:35
  65.5 1.0 %collective-permute-start.13 = (bf16[512,128]{1,0:T(8,128)(2,1)S(1)}, bf16[512,128]{1,0:T(8,128)(2,1)S(1)}, u32[]{:S(2)}, u32[]{:S(2)}) collective-permute-start(bf16[512,128]{1,0:T(8,128)(2,1)S(1)} %add_convert_fusion), channel_id=1, source_target_pairs={{0,4},{1,5},{2,6},{3,7},{4,0},{5,1},{6,2},{7,3},{8,12},{9,13},{10,... | collective-permute-start | bytes 393224 | tf_op jit(solution)/shard_map/ppermute | solution.py:35
  66.7 1.5 %collective-permute-start.14 = (bf16[512,128]{1,0:T(8,128)(2,1)S(1)}, bf16[512,128]{1,0:T(8,128)(2,1)S(1)}, u32[]{:S(2)}, u32[]{:S(2)}) collective-permute-start(bf16[512,128]{1,0:T(8,128)(2,1)S(1)} %fusion.5), channel_id=1, source_target_pairs={{0,8},{1,9},{2,10},{3,11},{4,12},{5,13},{6,14},{7,15},{8,0},{9,1},... | collective-permute-start | bytes 393224 | tf_op jit(solution)/shard_map/ppermute | solution.py:35
  68.2 3.2 %collective-permute-done.15 = bf16[256,512]{1,0:T(8,128)(2,1)S(1)} collective-permute-done((bf16[256,512]{1,0:T(8,128)(2,1)S(1)}, bf16[256,512]{1,0:T(8,128)(2,1)S(1)}, u32[]{:S(2)}, u32[]{:S(2)}) %collective-permute-start.15) | collective-permute-done | bytes 262176 | tf_op jit(solution)/shard_map/ppermute | solution.py:35
  71.6 2.7 %collective-permute-start.17 = (bf16[128,512]{1,0:T(8,128)(2,1)S(1)}, bf16[128,512]{1,0:T(8,128)(2,1)S(1)}, u32[]{:S(2)}, u32[]{:S(2)}) collective-permute-start(bf16[128,512]{1,0:T(8,128)(2,1)S(1)} %slice.38), channel_id=1, source_target_pairs={{0,72},{1,73},{2,74},{3,75},{4,76},{5,77},{6,78},{7,79},{8,64},{9,... | collective-permute-start | bytes 393224 | tf_op jit(solution)/shard_map/ppermute | solution.py:35
  74.4 0.8 copy.20
  75.1 2.7 %collective-permute-done.17 = bf16[128,512]{1,0:T(8,128)(2,1)S(1)} collective-permute-done((bf16[128,512]{1,0:T(8,128)(2,1)S(1)}, bf16[128,512]{1,0:T(8,128)(2,1)S(1)}, u32[]{:S(2)}, u32[]{:S(2)}) %collective-permute-start.17) | collective-permute-done | bytes 131104 | tf_op jit(solution)/shard_map/ppermute | solution.py:35
  (24 shorter events, 2.8 us)
Async XLA Ops:
  1.6 13.6 %collective-permute-start.1 = (bf16[128,1536]{1,0:T(8,128)(2,1)S(1)}, bf16[128,1536]{1,0:T(8,128)(2,1)S(1)}, u32[]{:S(2)}, u32[]{:S(2)}) collective-permute-start(bf16[128,1536]{1,0:T(8,128)(2,1)S(1)} %shard_map.67.own), channel_id=1, source_target_pairs={{0,32},{1,33},{2,34},{3,35},{4,36},{5,37},{6,38},{7,39},{8,40},{9,... | collective-permute-start | bytes 1179656 | tf_op jit(solution)/shard_map/ppermute | solution.py:35
  4.8 12.9 %collective-permute-start = (bf16[128,1536]{1,0:T(8,128)(2,1)S(1)}, bf16[128,1536]{1,0:T(8,128)(2,1)S(1)}, u32[]{:S(2)}, u32[]{:S(2)}) collective-permute-start(bf16[128,1536]{1,0:T(8,128)(2,1)S(1)} %shard_map.67.own), channel_id=1, source_target_pairs={{0,72},{1,73},{2,74},{3,75},{4,76},{5,77},{6,78},{7,79},{8,64},{9,... | collective-permute-start | bytes 1179656 | tf_op jit(solution)/shard_map/ppermute | solution.py:35
  8.9 14.9 %collective-permute-start.6 = (bf16[128,1536]{1,0:T(8,128)(2,1)S(1)}, bf16[128,1536]{1,0:T(8,128)(2,1)S(1)}, u32[]{:S(2)}, u32[]{:S(2)}) collective-permute-start(bf16[128,1536]{1,0:T(8,128)(2,1)S(1)} %shard_map.67.own), channel_id=1, source_target_pairs={{0,48},{1,49},{2,50},{3,51},{4,52},{5,53},{6,54},{7,55},{8,56},{9,... | collective-permute-start | bytes 1179656 | tf_op jit(solution)/shard_map/ppermute | solution.py:35
  10.0 13.8 %collective-permute-start.5 = (bf16[128,1536]{1,0:T(8,128)(2,1)S(1)}, bf16[128,1536]{1,0:T(8,128)(2,1)S(1)}, u32[]{:S(2)}, u32[]{:S(2)}) collective-permute-start(bf16[128,1536]{1,0:T(8,128)(2,1)S(1)} %shard_map.67.own), channel_id=1, source_target_pairs={{0,16},{1,17},{2,18},{3,19},{4,20},{5,21},{6,22},{7,23},{8,24},{9,... | collective-permute-start | bytes 1179656 | tf_op jit(solution)/shard_map/ppermute | solution.py:35
  17.7 11.2 %collective-permute-start.4 = (bf16[128,1536]{1,0:T(8,128)(2,1)S(1)}, bf16[128,1536]{1,0:T(8,128)(2,1)S(1)}, u32[]{:S(2)}, u32[]{:S(2)}) collective-permute-start(bf16[128,1536]{1,0:T(8,128)(2,1)S(1)} %collective-permute-done.1.refs_1_), channel_id=1, source_target_pairs={{0,72},{1,73},{2,74},{3,75},{4,76},{5,77},{6,78},{7,79},{8,64},{9,... | collective-permute-start | bytes 1179656 | tf_op jit(solution)/shard_map/ppermute | solution.py:35
  20.6 10.5 %collective-permute-start.3 = (bf16[128,1536]{1,0:T(8,128)(2,1)S(1)}, bf16[128,1536]{1,0:T(8,128)(2,1)S(1)}, u32[]{:S(2)}, u32[]{:S(2)}) collective-permute-start(bf16[128,1536]{1,0:T(8,128)(2,1)S(1)} %collective-permute-done.refs_0_), channel_id=1, source_target_pairs={{0,48},{1,49},{2,50},{3,51},{4,52},{5,53},{6,54},{7,55},{8,56},{9,... | collective-permute-start | bytes 1179656 | tf_op jit(solution)/shard_map/ppermute | solution.py:35
  22.2 10.0 %collective-permute-start.2 = (bf16[128,1536]{1,0:T(8,128)(2,1)S(1)}, bf16[128,1536]{1,0:T(8,128)(2,1)S(1)}, u32[]{:S(2)}, u32[]{:S(2)}) collective-permute-start(bf16[128,1536]{1,0:T(8,128)(2,1)S(1)} %collective-permute-done.refs_0_), channel_id=1, source_target_pairs={{0,16},{1,17},{2,18},{3,19},{4,20},{5,21},{6,22},{7,23},{8,24},{9,... | collective-permute-start | bytes 1179656 | tf_op jit(solution)/shard_map/ppermute | solution.py:35
  34.6 1.3 %collective-permute-start.7 = (f32[48,128]{1,0:T(8,128)S(1)}, f32[48,128]{1,0:T(8,128)S(1)}, u32[]{:S(2)}, u32[]{:S(2)}) collective-permute-start(f32[48,128]{1,0:T(8,128)S(1)} %get-tuple-element.66.mine), channel_id=1, source_target_pairs={{0,1},{1,0},{2,3},{3,2},{4,5},{5,4},{6,7},{7,6},{8,9},{9,8},{10,11... | collective-permute-start | bytes 73736 | tf_op jit(solution)/shard_map/ppermute | solution.py:35
  47.5 1.9 %copy-start = (bf16[2048,512]{1,0:T(8,128)(2,1)S(1)}, bf16[2048,512]{1,0:T(8,128)(2,1)}, u32[]{:S(2)}) copy-start(bf16[2048,512]{1,0:T(8,128)(2,1)} %param.6) | copy-start | bytes 6291460
  49.1 5.9 %collective-permute-start.8 = (bf16[8,512,128]{2,1,0:T(8,128)(2,1)S(1)}, bf16[8,512,128]{2,1,0:T(8,128)(2,1)S(1)}, u32[]{:S(2)}, u32[]{:S(2)}) collective-permute-start(bf16[8,512,128]{2,1,0:T(8,128)(2,1)S(1)} %get-tuple-element.77), channel_id=1, source_target_pairs={{0,1},{1,0},{2,3},{3,2},{4,5},{5,4},{6,7},{7,6},{8,9},{9,8},{10,11... | collective-permute-start | bytes 3145736 | tf_op jit(solution)/shard_map/ppermute | solution.py:35
  52.0 10.3 %collective-permute-start.9 = (bf16[256,512]{1,0:T(8,128)(2,1)S(1)}, bf16[256,512]{1,0:T(8,128)(2,1)S(1)}, u32[]{:S(2)}, u32[]{:S(2)}) collective-permute-start(bf16[256,512]{1,0:T(8,128)(2,1)S(1)} %get-tuple-element.82), channel_id=1, source_target_pairs={{0,32},{1,33},{2,34},{3,35},{4,36},{5,37},{6,38},{7,39},{8,40},{9,... | collective-permute-start | bytes 786440 | tf_op jit(solution)/shard_map/ppermute | solution.py:35
  56.6 8.9 %collective-permute-start.12 = (bf16[512,128]{1,0:T(8,128)(2,1)S(1)}, bf16[512,128]{1,0:T(8,128)(2,1)S(1)}, u32[]{:S(2)}, u32[]{:S(2)}) collective-permute-start(bf16[512,128]{1,0:T(8,128)(2,1)S(1)} %get-tuple-element.88), channel_id=1, source_target_pairs={{0,8},{1,9},{2,10},{3,11},{4,12},{5,13},{6,14},{7,15},{8,0},{9,1},... | collective-permute-start | bytes 393224 | tf_op jit(solution)/shard_map/ppermute | solution.py:35
  57.2 9.3 %collective-permute-start.10 = (bf16[2,512,128]{2,1,0:T(8,128)(2,1)S(1)}, bf16[2,512,128]{2,1,0:T(8,128)(2,1)S(1)}, u32[]{:S(2)}, u32[]{:S(2)}) collective-permute-start(bf16[2,512,128]{2,1,0:T(8,128)(2,1)S(1)} %get-tuple-element.85), channel_id=1, source_target_pairs={{0,2},{1,3},{2,4},{3,5},{4,6},{5,7},{6,0},{7,1},{8,10},{9,11},{10,... | collective-permute-start | bytes 786440 | tf_op jit(solution)/shard_map/ppermute | solution.py:35
  58.1 8.5 %collective-permute-start.11 = (bf16[2,512,128]{2,1,0:T(8,128)(2,1)S(1)}, bf16[2,512,128]{2,1,0:T(8,128)(2,1)S(1)}, u32[]{:S(2)}, u32[]{:S(2)}) collective-permute-start(bf16[2,512,128]{2,1,0:T(8,128)(2,1)S(1)} %get-tuple-element.86), channel_id=1, source_target_pairs={{0,6},{1,7},{2,0},{3,1},{4,2},{5,3},{6,4},{7,5},{8,14},{9,15},{10,... | collective-permute-start | bytes 786440 | tf_op jit(solution)/shard_map/ppermute | solution.py:35
  62.3 9.1 %collective-permute-start.15 = (bf16[256,512]{1,0:T(8,128)(2,1)S(1)}, bf16[256,512]{1,0:T(8,128)(2,1)S(1)}, u32[]{:S(2)}, u32[]{:S(2)}) collective-permute-start(bf16[256,512]{1,0:T(8,128)(2,1)S(1)} %get-tuple-element.90), channel_id=1, source_target_pairs={{0,16},{1,17},{2,18},{3,19},{4,20},{5,21},{6,22},{7,23},{8,24},{9,... | collective-permute-start | bytes 786440 | tf_op jit(solution)/shard_map/ppermute | solution.py:35
  63.7 7.7 %collective-permute-start.16 = (bf16[256,512]{1,0:T(8,128)(2,1)S(1)}, bf16[256,512]{1,0:T(8,128)(2,1)S(1)}, u32[]{:S(2)}, u32[]{:S(2)}) collective-permute-start(bf16[256,512]{1,0:T(8,128)(2,1)S(1)} %get-tuple-element.91), channel_id=1, source_target_pairs={{0,48},{1,49},{2,50},{3,51},{4,52},{5,53},{6,54},{7,55},{8,56},{9,... | collective-permute-start | bytes 786440 | tf_op jit(solution)/shard_map/ppermute | solution.py:35
  65.5 8.8 %collective-permute-start.13 = (bf16[512,128]{1,0:T(8,128)(2,1)S(1)}, bf16[512,128]{1,0:T(8,128)(2,1)S(1)}, u32[]{:S(2)}, u32[]{:S(2)}) collective-permute-start(bf16[512,128]{1,0:T(8,128)(2,1)S(1)} %add_convert_fusion), channel_id=1, source_target_pairs={{0,4},{1,5},{2,6},{3,7},{4,0},{5,1},{6,2},{7,3},{8,12},{9,13},{10,... | collective-permute-start | bytes 393224 | tf_op jit(solution)/shard_map/ppermute | solution.py:35
  66.7 7.6 %collective-permute-start.14 = (bf16[512,128]{1,0:T(8,128)(2,1)S(1)}, bf16[512,128]{1,0:T(8,128)(2,1)S(1)}, u32[]{:S(2)}, u32[]{:S(2)}) collective-permute-start(bf16[512,128]{1,0:T(8,128)(2,1)S(1)} %fusion.5), channel_id=1, source_target_pairs={{0,8},{1,9},{2,10},{3,11},{4,12},{5,13},{6,14},{7,15},{8,0},{9,1},... | collective-permute-start | bytes 393224 | tf_op jit(solution)/shard_map/ppermute | solution.py:35
  71.6 6.3 %collective-permute-start.17 = (bf16[128,512]{1,0:T(8,128)(2,1)S(1)}, bf16[128,512]{1,0:T(8,128)(2,1)S(1)}, u32[]{:S(2)}, u32[]{:S(2)}) collective-permute-start(bf16[128,512]{1,0:T(8,128)(2,1)S(1)} %slice.38), channel_id=1, source_target_pairs={{0,72},{1,73},{2,74},{3,75},{4,76},{5,77},{6,78},{7,79},{8,64},{9,... | collective-permute-start | bytes 393224 | tf_op jit(solution)/shard_map/ppermute | solution.py:35
